TPU v7x, 512 devices: a whole 4x4x16 slice. The times are simulated.
512 devices in a mesh: blk: 128 (over x, z, y_lo), lane: 4 (over y_hi, core).
Axes of the slice: x: 4, y: 4 (y_hi: 2, y_lo: 2; y = y_hi * 2 + y_lo), z: 16, core: 2. Of those that a mesh axis runs over, the one named last changes fastest.
Arguments:
- left_factor: bfloat16 [65536, 512], P('blk'), may hold values from -6 to 6
- right_factor: bfloat16 [4, 65536, 512], P('lane', 'blk'), may hold values from -6 to 6
- observed: bfloat16 [4, 4, 512, 65536], P('lane', None, None, 'blk'), may hold values from -6 to 6
- row_codes: int32 [65536], P('blk'), may hold values from 0 to 1073741823
- shift_codes: int32 [4, 4, 65536], P('lane', None, 'blk'), may hold values from 0 to 29
Outputs:
- left_out: bfloat16 [65536, 512], P('blk')
- right_out: bfloat16 [4, 65536, 512], P('lane', 'blk')
Inputs may be any that keep to these rules, and one draw needn't show every extreme that they name: `row_codes`: each row's word carries thirty independent sampling bits. `shift_codes`: A bit number for each lane, cycle step and visited tile entry column.
All inputs are finite; a program needn't handle non-finite values.
Results may differ from a plain program's by a relative error of at most 0.013.
Values may be sent and summed in bfloat16 or wider, within the bound.
No kernel may reach another device: no remote copies, remote signals or barrier semaphores. Data moves between devices by JAX's collectives and lax.ppermute only.
A program may use at most 64 MiB of HBM per device.

v0:
```python
import math

import jax
import jax.numpy as jnp
from jax import lax
from jax.sharding import PartitionSpec as P

step_right = 0.25
step_left = 0.1


def passed_along(value, axis, steps):
    count = lax.axis_size(axis)
    pairs = [(source, (source + steps) % count) for source in range(count)]
    return lax.ppermute(value, axis, pairs)


def cut_along(x, dim, devices):
    before, after = (x.shape[:dim], x.shape[dim + 1 :])
    return jnp.moveaxis(x.reshape(*before, devices, -1, *after), dim, 0)


def summed_on_arrival(x, axis, dim):
    devices = lax.axis_size(axis)
    pieces = lax.all_to_all(cut_along(x, dim, devices), axis, 0, 0, tiled=True)
    return jnp.sum(pieces.astype(jnp.float32), axis=0)


def in_order(pieces, dim):
    shape = list(pieces.shape[1:])
    shape[dim] *= pieces.shape[0]
    return jnp.moveaxis(pieces, 0, dim).reshape(shape)


def copy_for_each(x, axis):
    devices = lax.axis_size(axis)
    return lax.all_to_all(jnp.broadcast_to(x[None], (devices, *x.shape)), axis, 0, 0, tiled=True)


def collect(x, axis, dim):
    return in_order(copy_for_each(x, axis), dim)


def visit_tile(right_part, left_factor, target, row_codes, shifts, root_scale):
    predicted = (
        lax.dot_general(
            right_part, left_factor, (((1,), (1,)), ((), ())), preferred_element_type=jnp.float32
        )
        * root_scale
    )
    sample_bits = jnp.right_shift(row_codes[None, :], shifts[:, None]) & 1
    error_tile = jnp.where(sample_bits == 1, predicted - target.astype(jnp.float32), 0.0).astype(
        jnp.bfloat16
    )
    grad_right = jnp.dot(error_tile, left_factor, preferred_element_type=jnp.float32)
    grad_left = lax.dot_general(
        error_tile, right_part, (((0,), (0,)), ((), ())), preferred_element_type=jnp.float32
    )
    updated = (right_part.astype(jnp.float32) - step_right * root_scale * grad_right).astype(
        jnp.bfloat16
    )
    return (updated, grad_left)


def local(left_factor, right_factor, observed, row_codes, shift_codes):
    rank_size = left_factor.shape[1]
    root_scale = 1.0 / math.sqrt(rank_size)
    cycle_steps = observed.shape[1]
    column_count = observed.shape[2]
    right_now = right_factor[0]
    grad_sum = jnp.zeros(left_factor.shape, jnp.float32)
    for cycle_step in range(cycle_steps):
        target = observed[0, cycle_step]
        shifts = shift_codes[0, cycle_step]
        last_step = cycle_step + 1 == cycle_steps
        half_cols = column_count // 2
        pieces = []
        for portion in range(2):
            first_col = portion * half_cols
            updated, grad_left = visit_tile(
                right_now[first_col : first_col + half_cols],
                left_factor,
                target[first_col : first_col + half_cols],
                row_codes,
                shifts[first_col : first_col + half_cols],
                root_scale,
            )
            grad_sum = grad_sum + grad_left
            pieces.append(updated if last_step else passed_along(updated, "blk", 1))
        right_now = jnp.concatenate(pieces, axis=0)
    share_part = summed_on_arrival(grad_sum.astype(jnp.bfloat16), "lane", 0)
    share_rows = share_part.shape[0]
    first_row = lax.axis_index("lane") * share_rows
    own_rows = lax.dynamic_slice_in_dim(left_factor, first_row, share_rows, 0)
    renewed = (own_rows.astype(jnp.float32) - step_left * root_scale * share_part).astype(
        jnp.bfloat16
    )
    left_out = collect(renewed, "lane", 0)
    return (left_out, right_now[None])


def solution(mesh):
    in_specs = (
        P("blk", None),
        P("lane", "blk", None),
        P("lane", None, None, "blk"),
        P("blk"),
        P("lane", None, "blk"),
    )
    out_specs = (P("blk", None), P("lane", "blk", None))
    return jax.shard_map(local, mesh=mesh, in_specs=in_specs, out_specs=out_specs, check_vma=False)
```

profile of v0, /device:TPU:1, one launch (start us, length us, event | category | flops | bytes accessed | tf_op | source)
XLA Modules:
  0.0 90.4 jit_solution(3024270642785368908)
XLA Ops:
  0.7 0.9 %fusion.43 = (s32[1,1,256]{2,1,0:T(1,128)S(1)}, s32[1,1,256]{2,1,0:T(1,128)S(1)}, s32[1,1,256]{2,1,0:T(1,128)S(1)}, s32[1,1,256]{2,1,0:T(1,128)S(1)}, s32[1,1,25...) fusion(s32[1,4,512]{2,1,0:T(4,128)} %param.9), kind=kLoop, calls=%fused_computation.78 | loop fusion | bytes 16384 | tf_op jit(solution)/shard_map/slice | solution.py:85
  1.6 1.6 %fusion.26 = bf16[256,512]{1,0:T(8,128)(2,1)S(1)} fusion(bf16[512,512]{1,0:T(8,128)(2,1)} %param.5, bf16[1,4,512,512]{3,2,1,0:T(8,128)(2,1)} %param.7, s32[256]{0:T(256)S(1)} %bitcast.100, s32[512]{0:T(512)} %param.8, bf16[1,512,512]{2,1,0:T(8,128)(2,1)} %param.6), kind=kOutput, calls=%fused_computation.44 | convolution fusion | flops 135266304 | bytes 1313792 | tf_op jit(solution)/shard_map/dot_general | solution.py:46
  3.6 4.0 %collective-permute-start = (bf16[256,512]{1,0:T(8,128)(2,1)S(1)}, bf16[256,512]{1,0:T(8,128)(2,1)S(1)}, u32[]{:S(2)}, u32[]{:S(2)}) collective-permute-start(bf16[256,512]{1,0:T(8,128)(2,1)S(1)} %fusion.24), channel_id=1, source_target_pairs={{0,4},{4,8},{8,12},{12,16},{16,20},{20,24},{24,28},{28,32},{32,36}... | collective-permute-start | bytes 786440 | tf_op jit(solution)/shard_map/ppermute | solution.py:15
  7.6 0.4 fusion.27
  8.3 3.4 %collective-permute-start.1 = (bf16[256,512]{1,0:T(8,128)(2,1)S(1)}, bf16[256,512]{1,0:T(8,128)(2,1)S(1)}, u32[]{:S(2)}, u32[]{:S(2)}) collective-permute-start(bf16[256,512]{1,0:T(8,128)(2,1)S(1)} %fusion.25), channel_id=1, source_target_pairs={{0,4},{4,8},{8,12},{12,16},{16,20},{20,24},{24,28},{28,32},{32,36}... | collective-permute-start | bytes 786440 | tf_op jit(solution)/shard_map/ppermute | solution.py:15
  12.4 12.3 %collective-permute-done = bf16[256,512]{1,0:T(8,128)(2,1)S(1)} collective-permute-done((bf16[256,512]{1,0:T(8,128)(2,1)S(1)}, bf16[256,512]{1,0:T(8,128)(2,1)S(1)}, u32[]{:S(2)}, u32[]{:S(2)}) %collective-permute-start) | collective-permute-done | bytes 262176 | tf_op jit(solution)/shard_map/ppermute | solution.py:15
  24.7 0.4 fusion.28
  25.4 1.9 %collective-permute-start.2 = (bf16[256,512]{1,0:T(8,128)(2,1)S(1)}, bf16[256,512]{1,0:T(8,128)(2,1)S(1)}, u32[]{:S(2)}, u32[]{:S(2)}) collective-permute-start(bf16[256,512]{1,0:T(8,128)(2,1)S(1)} %subtract_convert_fusion.5), channel_id=1, source_target_pairs={{0,4},{4,8},{8,12},{12,16},{16,20},{20,24},{24,28},{28,32},{32,36}... | collective-permute-start | bytes 786440 | tf_op jit(solution)/shard_map/ppermute | solution.py:15
  27.4 3.0 %collective-permute-done.1 = bf16[256,512]{1,0:T(8,128)(2,1)S(1)} collective-permute-done((bf16[256,512]{1,0:T(8,128)(2,1)S(1)}, bf16[256,512]{1,0:T(8,128)(2,1)S(1)}, u32[]{:S(2)}, u32[]{:S(2)}) %collective-permute-start.1) | collective-permute-done | bytes 262176 | tf_op jit(solution)/shard_map/ppermute | solution.py:15
  30.4 0.4 fusion.29
  31.1 1.9 %collective-permute-start.3 = (bf16[256,512]{1,0:T(8,128)(2,1)S(1)}, bf16[256,512]{1,0:T(8,128)(2,1)S(1)}, u32[]{:S(2)}, u32[]{:S(2)}) collective-permute-start(bf16[256,512]{1,0:T(8,128)(2,1)S(1)} %subtract_convert_fusion.4), channel_id=1, source_target_pairs={{0,4},{4,8},{8,12},{12,16},{16,20},{20,24},{24,28},{28,32},{32,36}... | collective-permute-start | bytes 786440 | tf_op jit(solution)/shard_map/ppermute | solution.py:15
  33.0 0.3 fusion.44
  33.3 4.0 %collective-permute-done.2 = bf16[256,512]{1,0:T(8,128)(2,1)S(1)} collective-permute-done((bf16[256,512]{1,0:T(8,128)(2,1)S(1)}, bf16[256,512]{1,0:T(8,128)(2,1)S(1)}, u32[]{:S(2)}, u32[]{:S(2)}) %collective-permute-start.2) | collective-permute-done | bytes 262176 | tf_op jit(solution)/shard_map/ppermute | solution.py:15
  37.3 0.4 fusion.30
  38.0 1.9 %collective-permute-start.4 = (bf16[256,512]{1,0:T(8,128)(2,1)S(1)}, bf16[256,512]{1,0:T(8,128)(2,1)S(1)}, u32[]{:S(2)}, u32[]{:S(2)}) collective-permute-start(bf16[256,512]{1,0:T(8,128)(2,1)S(1)} %subtract_convert_fusion.3), channel_id=1, source_target_pairs={{0,4},{4,8},{8,12},{12,16},{16,20},{20,24},{24,28},{28,32},{32,36}... | collective-permute-start | bytes 786440 | tf_op jit(solution)/shard_map/ppermute | solution.py:15
  39.9 3.8 %collective-permute-done.3 = bf16[256,512]{1,0:T(8,128)(2,1)S(1)} collective-permute-done((bf16[256,512]{1,0:T(8,128)(2,1)S(1)}, bf16[256,512]{1,0:T(8,128)(2,1)S(1)}, u32[]{:S(2)}, u32[]{:S(2)}) %collective-permute-start.3) | collective-permute-done | bytes 262176 | tf_op jit(solution)/shard_map/ppermute | solution.py:15
  43.7 0.4 fusion.31
  44.4 1.9 %collective-permute-start.5 = (bf16[256,512]{1,0:T(8,128)(2,1)S(1)}, bf16[256,512]{1,0:T(8,128)(2,1)S(1)}, u32[]{:S(2)}, u32[]{:S(2)}) collective-permute-start(bf16[256,512]{1,0:T(8,128)(2,1)S(1)} %subtract_convert_fusion.2), channel_id=1, source_target_pairs={{0,4},{4,8},{8,12},{12,16},{16,20},{20,24},{24,28},{28,32},{32,36}... | collective-permute-start | bytes 786440 | tf_op jit(solution)/shard_map/ppermute | solution.py:15
  46.4 0.3 fusion.45
  46.7 0.3 fusion.46
  47.0 2.3 %collective-permute-done.4 = bf16[256,512]{1,0:T(8,128)(2,1)S(1)} collective-permute-done((bf16[256,512]{1,0:T(8,128)(2,1)S(1)}, bf16[256,512]{1,0:T(8,128)(2,1)S(1)}, u32[]{:S(2)}, u32[]{:S(2)}) %collective-permute-start.4) | collective-permute-done | bytes 262176 | tf_op jit(solution)/shard_map/ppermute | solution.py:15
  49.3 0.4 fusion.32
  50.0 6.2 %collective-permute-done.5 = bf16[256,512]{1,0:T(8,128)(2,1)S(1)} collective-permute-done((bf16[256,512]{1,0:T(8,128)(2,1)S(1)}, bf16[256,512]{1,0:T(8,128)(2,1)S(1)}, u32[]{:S(2)}, u32[]{:S(2)}) %collective-permute-start.5) | collective-permute-done | bytes 262176 | tf_op jit(solution)/shard_map/ppermute | solution.py:15
  56.2 0.4 fusion.33
  56.9 1.3 %fusion.5 = bf16[512,512]{1,0:T(8,128)(2,1)} fusion(f32[512,512]{1,0:T(8,128)S(1)} %fusion.48, f32[512,512]{1,0:T(8,128)S(1)} %fusion.47, f32[512,512]{1,0:T(8,128)S(1)} %fusion.46, f32[512,512]{1,0:T(8,128)S(1)} %fusion.45, f32[512,512]{1,0:T(8,128)S(1)} %fusion.44, f32[512,512]{1,0:T(8,128)S(1)} %convolution_add_fusion.1, ...), kind=kOutput, calls=%fused_computation.7 | convolution fusion | flops 136052736 | bytes 7340032 | tf_op jit(solution)/shard_map/dot_general | solution.py:56
  58.2 7.2 %all-to-all-start = ((bf16[4,128,512]{2,1,0:T(8,128)(2,1)}), bf16[4,128,512]{2,1,0:T(8,128)(2,1)S(1)}, u32[]{:S(2)}, u32[]{:S(2)}) async-start(bf16[4,128,512]{2,1,0:T(8,128)(2,1)} %bitcast.18), calls=%async_computation | async-start | bytes 1048576 | tf_op jit(solution)/shard_map/all_to_all | solution.py:25
  65.4 9.5 %all-to-all-done = bf16[4,128,512]{2,1,0:T(8,128)(2,1)S(1)} async-done(((bf16[4,128,512]{2,1,0:T(8,128)(2,1)}), bf16[4,128,512]{2,1,0:T(8,128)(2,1)S(1)}, u32[]{:S(2)}, u32[]{:S(2)}) %all-to-all-start) | async-done | bytes 524320 | tf_op jit(solution)/shard_map/all_to_all | solution.py:25
  75.0 0.8 broadcast_in_dim.16
  75.9 4.3 %all-to-all-start.1 = ((bf16[4,128,512]{2,1,0:T(8,128)(2,1)}), bf16[4,128,512]{2,1,0:T(8,128)(2,1)S(1)}, u32[]{:S(2)}, u32[]{:S(2)}) async-start(bf16[4,128,512]{2,1,0:T(8,128)(2,1)} %broadcast_in_dim.16), calls=%async_computation.1 | async-start | bytes 1048576 | tf_op jit(solution)/shard_map/all_to_all | solution.py:37
  80.8 0.8 maximum_bitcast_fusion
  81.6 8.0 %all-to-all-done.1 = bf16[4,128,512]{2,1,0:T(8,128)(2,1)S(1)} async-done(((bf16[4,128,512]{2,1,0:T(8,128)(2,1)}), bf16[4,128,512]{2,1,0:T(8,128)(2,1)S(1)}, u32[]{:S(2)}, u32[]{:S(2)}) %all-to-all-start.1) | async-done | bytes 524320 | tf_op jit(solution)/shard_map/all_to_all | solution.py:37
  89.6 0.8 copy.8
  (22 shorter events, 3.9 us)
Async XLA Ops:
  0.6 2.6 %copy-start = (bf16[512,512]{1,0:T(8,128)(2,1)S(1)}, bf16[512,512]{1,0:T(8,128)(2,1)}, u32[]{:S(2)}) copy-start(bf16[512,512]{1,0:T(8,128)(2,1)} %param.5) | copy-start | bytes 1572868
  0.6 2.6 %copy-start.1 = (bf16[1,512,512]{2,1,0:T(8,128)(2,1)S(1)}, bf16[1,512,512]{2,1,0:T(8,128)(2,1)}, u32[]{:S(2)}) copy-start(bf16[1,512,512]{2,1,0:T(8,128)(2,1)} %param.6) | copy-start | bytes 1572868
  0.7 7.0 %copy-start.2 = (bf16[1,4,512,512]{3,2,1,0:T(8,128)(2,1)S(1)}, bf16[1,4,512,512]{3,2,1,0:T(8,128)(2,1)}, u32[]{:S(2)}) copy-start(bf16[1,4,512,512]{3,2,1,0:T(8,128)(2,1)} %param.7) | copy-start | bytes 6291460
  0.7 7.0 %copy-start.3 = (s32[512]{0:T(512)S(1)}, s32[512]{0:T(512)}, u32[]{:S(2)}) copy-start(s32[512]{0:T(512)} %param.8) | copy-start | bytes 6148
  3.6 21.2 %collective-permute-start = (bf16[256,512]{1,0:T(8,128)(2,1)S(1)}, bf16[256,512]{1,0:T(8,128)(2,1)S(1)}, u32[]{:S(2)}, u32[]{:S(2)}) collective-permute-start(bf16[256,512]{1,0:T(8,128)(2,1)S(1)} %fusion.24), channel_id=1, source_target_pairs={{0,4},{4,8},{8,12},{12,16},{16,20},{20,24},{24,28},{28,32},{32,36}... | collective-permute-start | bytes 786440 | tf_op jit(solution)/shard_map/ppermute | solution.py:15
  8.3 22.0 %collective-permute-start.1 = (bf16[256,512]{1,0:T(8,128)(2,1)S(1)}, bf16[256,512]{1,0:T(8,128)(2,1)S(1)}, u32[]{:S(2)}, u32[]{:S(2)}) collective-permute-start(bf16[256,512]{1,0:T(8,128)(2,1)S(1)} %fusion.25), channel_id=1, source_target_pairs={{0,4},{4,8},{8,12},{12,16},{16,20},{20,24},{24,28},{28,32},{32,36}... | collective-permute-start | bytes 786440 | tf_op jit(solution)/shard_map/ppermute | solution.py:15
  25.4 11.9 %collective-permute-start.2 = (bf16[256,512]{1,0:T(8,128)(2,1)S(1)}, bf16[256,512]{1,0:T(8,128)(2,1)S(1)}, u32[]{:S(2)}, u32[]{:S(2)}) collective-permute-start(bf16[256,512]{1,0:T(8,128)(2,1)S(1)} %subtract_convert_fusion.5), channel_id=1, source_target_pairs={{0,4},{4,8},{8,12},{12,16},{16,20},{20,24},{24,28},{28,32},{32,36}... | collective-permute-start | bytes 786440 | tf_op jit(solution)/shard_map/ppermute | solution.py:15
  31.1 12.7 %collective-permute-start.3 = (bf16[256,512]{1,0:T(8,128)(2,1)S(1)}, bf16[256,512]{1,0:T(8,128)(2,1)S(1)}, u32[]{:S(2)}, u32[]{:S(2)}) collective-permute-start(bf16[256,512]{1,0:T(8,128)(2,1)S(1)} %subtract_convert_fusion.4), channel_id=1, source_target_pairs={{0,4},{4,8},{8,12},{12,16},{16,20},{20,24},{24,28},{28,32},{32,36}... | collective-permute-start | bytes 786440 | tf_op jit(solution)/shard_map/ppermute | solution.py:15
  38.0 11.3 %collective-permute-start.4 = (bf16[256,512]{1,0:T(8,128)(2,1)S(1)}, bf16[256,512]{1,0:T(8,128)(2,1)S(1)}, u32[]{:S(2)}, u32[]{:S(2)}) collective-permute-start(bf16[256,512]{1,0:T(8,128)(2,1)S(1)} %subtract_convert_fusion.3), channel_id=1, source_target_pairs={{0,4},{4,8},{8,12},{12,16},{16,20},{20,24},{24,28},{28,32},{32,36}... | collective-permute-start | bytes 786440 | tf_op jit(solution)/shard_map/ppermute | solution.py:15
  44.4 11.8 %collective-permute-start.5 = (bf16[256,512]{1,0:T(8,128)(2,1)S(1)}, bf16[256,512]{1,0:T(8,128)(2,1)S(1)}, u32[]{:S(2)}, u32[]{:S(2)}) collective-permute-start(bf16[256,512]{1,0:T(8,128)(2,1)S(1)} %subtract_convert_fusion.2), channel_id=1, source_target_pairs={{0,4},{4,8},{8,12},{12,16},{16,20},{20,24},{24,28},{28,32},{32,36}... | collective-permute-start | bytes 786440 | tf_op jit(solution)/shard_map/ppermute | solution.py:15
  58.2 16.7 %all-to-all-start = ((bf16[4,128,512]{2,1,0:T(8,128)(2,1)}), bf16[4,128,512]{2,1,0:T(8,128)(2,1)S(1)}, u32[]{:S(2)}, u32[]{:S(2)}) async-start(bf16[4,128,512]{2,1,0:T(8,128)(2,1)} %bitcast.18), calls=%async_computation | async-start | bytes 1048576 | tf_op jit(solution)/shard_map/all_to_all | solution.py:25
  75.9 13.8 %all-to-all-start.1 = ((bf16[4,128,512]{2,1,0:T(8,128)(2,1)}), bf16[4,128,512]{2,1,0:T(8,128)(2,1)S(1)}, u32[]{:S(2)}, u32[]{:S(2)}) async-start(bf16[4,128,512]{2,1,0:T(8,128)(2,1)} %broadcast_in_dim.16), calls=%async_computation.1 | async-start | bytes 1048576 | tf_op jit(solution)/shard_map/all_to_all | solution.py:37
where the time goes:
time: 90.8 us; the launch traced here: 90.4 us
  waiting for transfers between devices  49.1 us (54%)
  starting transfers between devices  26.7 us (29%)
  matrix products  10.2 us (11%)
  local copies, waits for them, and re-layouts  2.57 us (3%)
  other arithmetic  0.94 us (1%)
    ppermute x6, waiting for transfers between devices, passed_along(): return lax.ppermute(value, axis, pairs)  31.6 us
    ppermute x6, starting transfers between devices, passed_along(): return lax.ppermute(value, axis, pairs)  15.1 us
    all_to_all x1, waiting for transfers between devices, summed_on_arrival(): pieces = lax.all_to_all(cut_along(x, dim, devices), axis, 0, 0, tiled=True)  9.48 us
    all_to_all x1, waiting for transfers between devices, copy_for_each(): lax.all_to_all(jnp.broadcast_to(x[None], (devices, *x.shape)), axis, 0, 0...  8.04 us
    all_to_all x1, starting transfers between devices, summed_on_arrival(): pieces = lax.all_to_all(cut_along(x, dim, devices), axis, 0, 0, tiled=True)  7.23 us
    all_to_all x1, starting transfers between devices, copy_for_each(): lax.all_to_all(jnp.broadcast_to(x[None], (devices, *x.shape)), axis, 0, 0...  4.31 us
    dot_general x8, matrix products, visit_tile(): lax.dot_general(right_part, left_factor, (((1,), (1,)), ((), ())), prefer...  4.2 us
    dot_general x8, matrix products, visit_tile(): lax.dot_general(error_tile, right_part, (((0,), (0,)), ((), ())), preferr...  3.58 us
  transfers between devices with their start and end apart: 8, of which 8 were waited for; matrix products, arithmetic and copies ran while one was open for 8% of the time, Pallas kernels for 0%

commit v1 on v0

v1 whole, which is shorter than its diff:
```python
import math

import jax
import jax.numpy as jnp
from jax import lax
from jax.sharding import PartitionSpec as P

step_right = 0.25
step_left = 0.1
chunk_rows = (128, 128, 128, 128)


def passed_along(value):
    count = lax.axis_size("blk")
    return lax.ppermute(value, "blk", [(i, (i + 1) % count) for i in range(count)])


def swapped(value, bit):
    count = lax.axis_size("lane")
    return lax.ppermute(value, "lane", [(i, i ^ bit) for i in range(count)])


def visit(right_part, left_factor, target, row_codes, shifts, root_scale):
    predicted = (
        lax.dot_general(
            right_part, left_factor, (((1,), (1,)), ((), ())), preferred_element_type=jnp.float32
        )
        * root_scale
    )
    sample_bits = jnp.right_shift(row_codes[None, :], shifts[:, None]) & 1
    error_tile = jnp.where(sample_bits == 1, predicted - target.astype(jnp.float32), 0.0).astype(
        jnp.bfloat16
    )
    grad_right = jnp.dot(error_tile, left_factor, preferred_element_type=jnp.float32)
    updated = (right_part.astype(jnp.float32) - step_right * root_scale * grad_right).astype(
        jnp.bfloat16
    )
    return updated, error_tile


def local(left_factor, right_factor, observed, row_codes, shift_codes):
    rank_size = left_factor.shape[1]
    root_scale = 1.0 / math.sqrt(rank_size)
    cycle_steps = observed.shape[1]
    firsts = [sum(chunk_rows[:i]) for i in range(len(chunk_rows))]
    parts = [right_factor[0, a : a + n] for a, n in zip(firsts, chunk_rows)]
    grad_sum = jnp.zeros(left_factor.shape, jnp.float32)
    for s in range(cycle_steps):
        for i, (a, n) in enumerate(zip(firsts, chunk_rows)):
            updated, error_tile = visit(
                parts[i],
                left_factor,
                observed[0, s, a : a + n],
                row_codes,
                shift_codes[0, s, a : a + n],
                root_scale,
            )
            grad_sum = grad_sum + lax.dot_general(
                error_tile, parts[i], (((0,), (0,)), ((), ())), preferred_element_type=jnp.float32
            )
            parts[i] = updated if s + 1 == cycle_steps else passed_along(updated)
    right_out = jnp.concatenate(parts, axis=0)[None]

    half = left_factor.shape[0] // 2
    core = lax.axis_index("lane") % 2
    theirs = lax.dynamic_slice_in_dim(grad_sum, (1 - core) * half, half, 0)
    mine = lax.dynamic_slice_in_dim(grad_sum, core * half, half, 0)
    own_rows = lax.dynamic_slice_in_dim(left_factor, core * half, half, 0)
    chip_sum = (mine + swapped(theirs.astype(jnp.bfloat16), 1).astype(jnp.float32)).astype(
        jnp.bfloat16
    )
    total = chip_sum.astype(jnp.float32) + swapped(chip_sum, 2).astype(jnp.float32)
    renewed = (own_rows.astype(jnp.float32) - step_left * root_scale * total).astype(jnp.bfloat16)
    other = swapped(renewed, 1)
    left_out = jnp.concatenate(
        [jnp.where(core == 0, renewed, other), jnp.where(core == 0, other, renewed)], axis=0
    )
    return left_out, right_out


def solution(mesh):
    in_specs = (
        P("blk", None),
        P("lane", "blk", None),
        P("lane", None, None, "blk"),
        P("blk"),
        P("lane", None, "blk"),
    )
    out_specs = (P("blk", None), P("lane", "blk", None))
    return jax.shard_map(local, mesh=mesh, in_specs=in_specs, out_specs=out_specs, check_vma=False)
```

time: 90.8 us -> 95.5 us (1.052)
  waiting for transfers between devices: 49.1 us -> 12.8 us
  starting transfers between devices: 26.7 us -> 54.7 us
  matrix products: 10.2 us -> 22.2 us
    ppermute x6 -> x15, starting transfers between devices: 15.1 us -> 54.7 us  [the longest x12 41.9 us: passed_along(): lax.ppermute(value, 'blk', [(i, (i + 1) % count) for i in range(count)])]
    ppermute x6 -> x15, waiting for transfers between devices: 31.6 us -> 12.8 us  [the longest x12 6.79 us: passed_along(): lax.ppermute(value, 'blk', [(i, (i + 1) % count) for i in range(count)])]
    all_to_all x2 -> x0, waiting for transfers between devices: 17.5 us -> none  [the longest x1 9.48 us: summed_on_arrival(): pieces = lax.all_to_all(cut_along(x, dim, devices), axis, 0, 0, tiled=True)]
    dot_general x24 -> x48, matrix products: 10.2 us -> 22.2 us  [the longest x16 10.9 us: visit(): lax.dot_general(right_part, left_factor, (((1,), (1,)), ((), ())), prefer...]
    all_to_all x2 -> x0, starting transfers between devices: 11.5 us -> none  [the longest x1 7.23 us: summed_on_arrival(): pieces = lax.all_to_all(cut_along(x, dim, devices), axis, 0, 0, tiled=True)]
  transfers between devices with their start and end apart: 8 -> 15, of which waited for: 8 -> 3; matrix products, arithmetic and copies ran while one was open for 8% -> 20% of each run, Pallas kernels for 0% -> 0%
where the time goes in v1:
time: 95.5 us; the launch traced here: 94.8 us
  starting transfers between devices  54.7 us (57%)
  matrix products  22.2 us (23%)
  waiting for transfers between devices  12.8 us (13%)
  local copies, waits for them, and re-layouts  1.93 us (2%)
  other arithmetic  1.89 us (2%)
  between operations  1.3 us (1%)
    ppermute x12, starting transfers between devices, passed_along(): lax.ppermute(value, 'blk', [(i, (i + 1) % count) for i in range(count)])  41.9 us
    ppermute x3, starting transfers between devices, swapped(): return lax.ppermute(value, 'lane', [(i, i ^ bit) for i in range(count)])  12.9 us
    dot_general x16, matrix products, visit(): lax.dot_general(right_part, left_factor, (((1,), (1,)), ((), ())), prefer...  10.9 us
    ppermute x12, waiting for transfers between devices, passed_along(): lax.ppermute(value, 'blk', [(i, (i + 1) % count) for i in range(count)])  6.79 us
    ppermute x3, waiting for transfers between devices, swapped(): return lax.ppermute(value, 'lane', [(i, i ^ bit) for i in range(count)])  5.99 us
    dot_general x16, matrix products, visit(): jnp.dot(error_tile, left_factor, preferred_element_type=jnp.float32)  5.74 us
    dot_general x16, matrix products, local(): lax.dot_general(error_tile, parts[i], (((0,), (0,)), ((), ())), preferred...  5.56 us
  transfers between devices with their start and end apart: 15, of which 3 were waited for; matrix products, arithmetic and copies ran while one was open for 20% of the time, Pallas kernels for 0%

profile of v1, /device:TPU:1, one launch (start us, length us, event | category | flops | bytes accessed | tf_op | source)
XLA Modules:
  0.0 94.8 jit_solution(8489965455068101834)
XLA Ops:
  0.7 0.9 slice_bitcast_fusion.3
  1.6 1.4 %fusion.54 = bf16[128,512]{1,0:T(8,128)(2,1)S(1)} fusion(bf16[512,512]{1,0:T(8,128)(2,1)} %param.5, bf16[1,4,512,512]{3,2,1,0:T(8,128)(2,1)} %param.7, s32[128]{0:T(128)S(1)} %get-tuple-element.14, s32[512]{0:T(512)} %param.8, bf16[1,512,512]{2,1,0:T(8,128)(2,1)} %param.6), kind=kOutput, calls=%fused_computation.90 | convolution fusion | flops 67633152 | bytes 920064 | tf_op jit(solution)/shard_map/dot_general | solution.py:25
  3.0 1.3 %fusion.47 = bf16[128,512]{1,0:T(8,128)(2,1)S(1)} fusion(bf16[128,512]{1,0:T(8,128)(2,1)S(1)} %fusion.54, bf16[512,512]{1,0:T(8,128)(2,1)} %param.5, bf16[1,512,512]{2,1,0:T(8,128)(2,1)} %param.6), kind=kOutput, calls=%fused_computation.83 | convolution fusion | flops 67371008 | bytes 917504 | tf_op jit(solution)/shard_map/dot_general | solution.py:34
  4.3 4.0 %collective-permute-start.3 = (bf16[128,512]{1,0:T(8,128)(2,1)S(1)}, bf16[128,512]{1,0:T(8,128)(2,1)S(1)}, u32[]{:S(2)}, u32[]{:S(2)}) collective-permute-start(bf16[128,512]{1,0:T(8,128)(2,1)S(1)} %fusion.47), channel_id=1, source_target_pairs={{0,4},{4,8},{8,12},{12,16},{16,20},{20,24},{24,28},{28,32},{32,36}... | collective-permute-start | bytes 393224 | tf_op jit(solution)/shard_map/ppermute | solution.py:15
  8.4 1.2 %fusion.53 = bf16[128,512]{1,0:T(8,128)(2,1)S(1)} fusion(bf16[512,512]{1,0:T(8,128)(2,1)S(1)} %copy-done, bf16[1,4,512,512]{3,2,1,0:T(8,128)(2,1)} %param.7, s32[128]{0:T(128)S(1)} %get-tuple-element.15, s32[512]{0:T(512)S(1)} %copy-done.6, bf16[1,512,512]{2,1,0:T(8,128)(2,1)S(1)} %copy-done.1), kind=kOutput, calls=%fused_computation.89 | convolution fusion | flops 67633152 | bytes 920064 | tf_op jit(solution)/shard_map/dot_general | solution.py:25
  9.8 3.4 %collective-permute-start.2 = (bf16[128,512]{1,0:T(8,128)(2,1)S(1)}, bf16[128,512]{1,0:T(8,128)(2,1)S(1)}, u32[]{:S(2)}, u32[]{:S(2)}) collective-permute-start(bf16[128,512]{1,0:T(8,128)(2,1)S(1)} %fusion.48), channel_id=1, source_target_pairs={{0,4},{4,8},{8,12},{12,16},{16,20},{20,24},{24,28},{28,32},{32,36}... | collective-permute-start | bytes 393224 | tf_op jit(solution)/shard_map/ppermute | solution.py:15
  13.3 1.2 %fusion.52 = bf16[128,512]{1,0:T(8,128)(2,1)S(1)} fusion(bf16[512,512]{1,0:T(8,128)(2,1)S(1)} %copy-done, bf16[1,4,512,512]{3,2,1,0:T(8,128)(2,1)} %param.7, s32[128]{0:T(128)S(1)} %get-tuple-element.16, s32[512]{0:T(512)S(1)} %copy-done.6, bf16[1,512,512]{2,1,0:T(8,128)(2,1)S(1)} %copy-done.1), kind=kOutput, calls=%fused_computation.88 | convolution fusion | flops 67633152 | bytes 920064 | tf_op jit(solution)/shard_map/dot_general | solution.py:25
  14.8 3.2 %collective-permute-start.1 = (bf16[128,512]{1,0:T(8,128)(2,1)S(1)}, bf16[128,512]{1,0:T(8,128)(2,1)S(1)}, u32[]{:S(2)}, u32[]{:S(2)}) collective-permute-start(bf16[128,512]{1,0:T(8,128)(2,1)S(1)} %fusion.49), channel_id=1, source_target_pairs={{0,4},{4,8},{8,12},{12,16},{16,20},{20,24},{24,28},{28,32},{32,36}... | collective-permute-start | bytes 393224 | tf_op jit(solution)/shard_map/ppermute | solution.py:15
  18.0 1.2 %fusion.51 = bf16[128,512]{1,0:T(8,128)(2,1)S(1)} fusion(bf16[512,512]{1,0:T(8,128)(2,1)S(1)} %copy-done, bf16[1,4,512,512]{3,2,1,0:T(8,128)(2,1)} %param.7, s32[128]{0:T(128)S(1)} %get-tuple-element.17, s32[512]{0:T(512)S(1)} %copy-done.6, bf16[1,512,512]{2,1,0:T(8,128)(2,1)S(1)} %copy-done.1), kind=kOutput, calls=%fused_computation.87 | convolution fusion | flops 67633152 | bytes 920064 | tf_op jit(solution)/shard_map/dot_general | solution.py:25
  19.4 3.4 %collective-permute-start = (bf16[128,512]{1,0:T(8,128)(2,1)S(1)}, bf16[128,512]{1,0:T(8,128)(2,1)S(1)}, u32[]{:S(2)}, u32[]{:S(2)}) collective-permute-start(bf16[128,512]{1,0:T(8,128)(2,1)S(1)} %fusion.50), channel_id=1, source_target_pairs={{0,4},{4,8},{8,12},{12,16},{16,20},{20,24},{24,28},{28,32},{32,36}... | collective-permute-start | bytes 393224 | tf_op jit(solution)/shard_map/ppermute | solution.py:15
  24.2 1.4 %fusion.58 = bf16[128,512]{1,0:T(8,128)(2,1)S(1)} fusion(bf16[128,512]{1,0:T(8,128)(2,1)S(1)} %collective-permute-done.3, bf16[512,512]{1,0:T(8,128)(2,1)S(1)} %copy-done, bf16[1,4,512,512]{3,2,1,0:T(8,128)(2,1)} %param.7, s32[128]{0:T(128)S(1)} %get-tuple-element.10, s32[512]{0:T(512)S(1)} %copy-done.6), kind=kOutput, calls=%fused_computation.94 | convolution fusion | flops 67633152 | bytes 920064 | tf_op jit(solution)/shard_map/dot_general | solution.py:25
  25.8 3.2 %collective-permute-start.7 = (bf16[128,512]{1,0:T(8,128)(2,1)S(1)}, bf16[128,512]{1,0:T(8,128)(2,1)S(1)}, u32[]{:S(2)}, u32[]{:S(2)}) collective-permute-start(bf16[128,512]{1,0:T(8,128)(2,1)S(1)} %subtract_convert_fusion.9), channel_id=1, source_target_pairs={{0,4},{4,8},{8,12},{12,16},{16,20},{20,24},{24,28},{28,32},{32,36}... | collective-permute-start | bytes 393224 | tf_op jit(solution)/shard_map/ppermute | solution.py:15
  29.1 1.2 %fusion.57 = bf16[128,512]{1,0:T(8,128)(2,1)S(1)} fusion(bf16[128,512]{1,0:T(8,128)(2,1)S(1)} %collective-permute-done.2, bf16[512,512]{1,0:T(8,128)(2,1)S(1)} %copy-done, bf16[1,4,512,512]{3,2,1,0:T(8,128)(2,1)} %param.7, s32[128]{0:T(128)S(1)} %get-tuple-element.11, s32[512]{0:T(512)S(1)} %copy-done.6), kind=kOutput, calls=%fused_computation.93 | convolution fusion | flops 67633152 | bytes 920064 | tf_op jit(solution)/shard_map/dot_general | solution.py:25
  30.5 3.4 %collective-permute-start.6 = (bf16[128,512]{1,0:T(8,128)(2,1)S(1)}, bf16[128,512]{1,0:T(8,128)(2,1)S(1)}, u32[]{:S(2)}, u32[]{:S(2)}) collective-permute-start(bf16[128,512]{1,0:T(8,128)(2,1)S(1)} %subtract_convert_fusion.10), channel_id=1, source_target_pairs={{0,4},{4,8},{8,12},{12,16},{16,20},{20,24},{24,28},{28,32},{32,36}... | collective-permute-start | bytes 393224 | tf_op jit(solution)/shard_map/ppermute | solution.py:15
  34.6 3.2 %collective-permute-start.5 = (bf16[128,512]{1,0:T(8,128)(2,1)S(1)}, bf16[128,512]{1,0:T(8,128)(2,1)S(1)}, u32[]{:S(2)}, u32[]{:S(2)}) collective-permute-start(bf16[128,512]{1,0:T(8,128)(2,1)S(1)} %subtract_convert_fusion.11), channel_id=1, source_target_pairs={{0,4},{4,8},{8,12},{12,16},{16,20},{20,24},{24,28},{28,32},{32,36}... | collective-permute-start | bytes 393224 | tf_op jit(solution)/shard_map/ppermute | solution.py:15
  38.4 4.6 %collective-permute-start.4 = (bf16[128,512]{1,0:T(8,128)(2,1)S(1)}, bf16[128,512]{1,0:T(8,128)(2,1)S(1)}, u32[]{:S(2)}, u32[]{:S(2)}) collective-permute-start(bf16[128,512]{1,0:T(8,128)(2,1)S(1)} %subtract_convert_fusion.12), channel_id=1, source_target_pairs={{0,4},{4,8},{8,12},{12,16},{16,20},{20,24},{24,28},{28,32},{32,36}... | collective-permute-start | bytes 393224 | tf_op jit(solution)/shard_map/ppermute | solution.py:15
  44.5 3.2 %collective-permute-start.11 = (bf16[128,512]{1,0:T(8,128)(2,1)S(1)}, bf16[128,512]{1,0:T(8,128)(2,1)S(1)}, u32[]{:S(2)}, u32[]{:S(2)}) collective-permute-start(bf16[128,512]{1,0:T(8,128)(2,1)S(1)} %subtract_convert_fusion.5), channel_id=1, source_target_pairs={{0,4},{4,8},{8,12},{12,16},{16,20},{20,24},{24,28},{28,32},{32,36}... | collective-permute-start | bytes 393224 | tf_op jit(solution)/shard_map/ppermute | solution.py:15
  48.3 3.5 %collective-permute-start.10 = (bf16[128,512]{1,0:T(8,128)(2,1)S(1)}, bf16[128,512]{1,0:T(8,128)(2,1)S(1)}, u32[]{:S(2)}, u32[]{:S(2)}) collective-permute-start(bf16[128,512]{1,0:T(8,128)(2,1)S(1)} %subtract_convert_fusion.6), channel_id=1, source_target_pairs={{0,4},{4,8},{8,12},{12,16},{16,20},{20,24},{24,28},{28,32},{32,36}... | collective-permute-start | bytes 393224 | tf_op jit(solution)/shard_map/ppermute | solution.py:15
  51.8 0.3 fusion.60
  52.4 3.2 %collective-permute-start.9 = (bf16[128,512]{1,0:T(8,128)(2,1)S(1)}, bf16[128,512]{1,0:T(8,128)(2,1)S(1)}, u32[]{:S(2)}, u32[]{:S(2)}) collective-permute-start(bf16[128,512]{1,0:T(8,128)(2,1)S(1)} %subtract_convert_fusion.7), channel_id=1, source_target_pairs={{0,4},{4,8},{8,12},{12,16},{16,20},{20,24},{24,28},{28,32},{32,36}... | collective-permute-start | bytes 393224 | tf_op jit(solution)/shard_map/ppermute | solution.py:15
  55.6 0.3 fusion.59
  56.2 3.4 %collective-permute-start.8 = (bf16[128,512]{1,0:T(8,128)(2,1)S(1)}, bf16[128,512]{1,0:T(8,128)(2,1)S(1)}, u32[]{:S(2)}, u32[]{:S(2)}) collective-permute-start(bf16[128,512]{1,0:T(8,128)(2,1)S(1)} %subtract_convert_fusion.8), channel_id=1, source_target_pairs={{0,4},{4,8},{8,12},{12,16},{16,20},{20,24},{24,28},{28,32},{32,36}... | collective-permute-start | bytes 393224 | tf_op jit(solution)/shard_map/ppermute | solution.py:15
  60.9 6.8 %collective-permute-done.8 = bf16[128,512]{1,0:T(8,128)(2,1)S(1)} collective-permute-done((bf16[128,512]{1,0:T(8,128)(2,1)S(1)}, bf16[128,512]{1,0:T(8,128)(2,1)S(1)}, u32[]{:S(2)}, u32[]{:S(2)}) %collective-permute-start.8) | collective-permute-done | bytes 131104 | tf_op jit(solution)/shard_map/ppermute | solution.py:15
  70.3 0.6 copy-done.4
  71.2 0.8 fusion.10
  72.1 5.3 %collective-permute-start.12 = (bf16[256,512]{1,0:T(8,128)(2,1)S(1)}, bf16[256,512]{1,0:T(8,128)(2,1)S(1)}, u32[]{:S(2)}, u32[]{:S(2)}) collective-permute-start(bf16[256,512]{1,0:T(8,128)(2,1)S(1)} %dynamic-slice_convert_fusion), channel_id=1, source_target_pairs={{0,1},{1,0},{2,3},{3,2},{4,5},{5,4},{6,7},{7,6},{8,9},{9,8},{10,11... | collective-permute-start | bytes 786440 | tf_op jit(solution)/shard_map/ppermute | solution.py:20
  77.4 1.1 %subtract_convert_fusion.1 = bf16[128,512]{1,0:T(8,128)(2,1)S(1)} fusion(bf16[128,512]{1,0:T(8,128)(2,1)S(1)} %collective-permute-done.11, bf16[128,512]{1,0:T(8,128)(2,1)} %copy-done.4, bf16[512,512]{1,0:T(8,128)(2,1)S(1)} %copy-done), kind=kOutput, calls=%fused_computation.108 | convolution fusion | flops 67371008 | bytes 917504 | tf_op jit(solution)/shard_map/dot_general | solution.py:34
  78.6 4.5 %collective-permute-start.13 = (bf16[256,512]{1,0:T(8,128)(2,1)S(1)}, bf16[256,512]{1,0:T(8,128)(2,1)S(1)}, u32[]{:S(2)}, u32[]{:S(2)}) collective-permute-start(bf16[256,512]{1,0:T(8,128)(2,1)S(1)} %add_convert_fusion), channel_id=1, source_target_pairs={{0,2},{1,3},{2,0},{3,1},{4,6},{5,7},{6,4},{7,5},{8,10},{9,11},{10,... | collective-permute-start | bytes 786440 | tf_op jit(solution)/shard_map/ppermute | solution.py:20
  83.7 5.9 %collective-permute-done.13 = bf16[256,512]{1,0:T(8,128)(2,1)S(1)} collective-permute-done((bf16[256,512]{1,0:T(8,128)(2,1)S(1)}, bf16[256,512]{1,0:T(8,128)(2,1)S(1)}, u32[]{:S(2)}, u32[]{:S(2)}) %collective-permute-start.13) | collective-permute-done | bytes 262176 | tf_op jit(solution)/shard_map/ppermute | solution.py:20
  89.7 3.1 %collective-permute-start.14 = (bf16[256,512]{1,0:T(8,128)(2,1)S(1)}, bf16[256,512]{1,0:T(8,128)(2,1)S(1)}, u32[]{:S(2)}, u32[]{:S(2)}) collective-permute-start(bf16[256,512]{1,0:T(8,128)(2,1)S(1)} %subtract_convert_fusion), channel_id=1, source_target_pairs={{0,1},{1,0},{2,3},{3,2},{4,5},{5,4},{6,7},{7,6},{8,9},{9,8},{10,11... | collective-permute-start | bytes 786440 | tf_op jit(solution)/shard_map/ppermute | solution.py:20
  93.0 0.8 maximum_bitcast_fusion
  94.0 0.8 pad_maximum_fusion
  (67 shorter events, 11.3 us)
Async XLA Ops:
  0.6 7.7 %copy-start = (bf16[512,512]{1,0:T(8,128)(2,1)S(1)}, bf16[512,512]{1,0:T(8,128)(2,1)}, u32[]{:S(2)}) copy-start(bf16[512,512]{1,0:T(8,128)(2,1)} %param.5) | copy-start | bytes 1572868
  0.6 7.7 %copy-start.6 = (s32[512]{0:T(512)S(1)}, s32[512]{0:T(512)}, u32[]{:S(2)}) copy-start(s32[512]{0:T(512)} %param.8) | copy-start | bytes 6148
  0.7 7.7 %copy-start.1 = (bf16[1,512,512]{2,1,0:T(8,128)(2,1)S(1)}, bf16[1,512,512]{2,1,0:T(8,128)(2,1)}, u32[]{:S(2)}) copy-start(bf16[1,512,512]{2,1,0:T(8,128)(2,1)} %param.6) | copy-start | bytes 1572868
  4.3 19.9 %collective-permute-start.3 = (bf16[128,512]{1,0:T(8,128)(2,1)S(1)}, bf16[128,512]{1,0:T(8,128)(2,1)S(1)}, u32[]{:S(2)}, u32[]{:S(2)}) collective-permute-start(bf16[128,512]{1,0:T(8,128)(2,1)S(1)} %fusion.47), channel_id=1, source_target_pairs={{0,4},{4,8},{8,12},{12,16},{16,20},{20,24},{24,28},{28,32},{32,36}... | collective-permute-start | bytes 393224 | tf_op jit(solution)/shard_map/ppermute | solution.py:15
  9.8 19.2 %collective-permute-start.2 = (bf16[128,512]{1,0:T(8,128)(2,1)S(1)}, bf16[128,512]{1,0:T(8,128)(2,1)S(1)}, u32[]{:S(2)}, u32[]{:S(2)}) collective-permute-start(bf16[128,512]{1,0:T(8,128)(2,1)S(1)} %fusion.48), channel_id=1, source_target_pairs={{0,4},{4,8},{8,12},{12,16},{16,20},{20,24},{24,28},{28,32},{32,36}... | collective-permute-start | bytes 393224 | tf_op jit(solution)/shard_map/ppermute | solution.py:15
  14.8 19.2 %collective-permute-start.1 = (bf16[128,512]{1,0:T(8,128)(2,1)S(1)}, bf16[128,512]{1,0:T(8,128)(2,1)S(1)}, u32[]{:S(2)}, u32[]{:S(2)}) collective-permute-start(bf16[128,512]{1,0:T(8,128)(2,1)S(1)} %fusion.49), channel_id=1, source_target_pairs={{0,4},{4,8},{8,12},{12,16},{16,20},{20,24},{24,28},{28,32},{32,36}... | collective-permute-start | bytes 393224 | tf_op jit(solution)/shard_map/ppermute | solution.py:15
  19.4 18.3 %collective-permute-start = (bf16[128,512]{1,0:T(8,128)(2,1)S(1)}, bf16[128,512]{1,0:T(8,128)(2,1)S(1)}, u32[]{:S(2)}, u32[]{:S(2)}) collective-permute-start(bf16[128,512]{1,0:T(8,128)(2,1)S(1)} %fusion.50), channel_id=1, source_target_pairs={{0,4},{4,8},{8,12},{12,16},{16,20},{20,24},{24,28},{28,32},{32,36}... | collective-permute-start | bytes 393224 | tf_op jit(solution)/shard_map/ppermute | solution.py:15
  24.2 9.8 %copy-start.5 = (bf16[1,4,512,512]{3,2,1,0:T(8,128)(2,1)S(1)}, bf16[1,4,512,512]{3,2,1,0:T(8,128)(2,1)}, u32[]{:S(2)}) copy-start(bf16[1,4,512,512]{3,2,1,0:T(8,128)(2,1)} %param.7) | copy-start | bytes 6291460
  25.8 18.1 %collective-permute-start.7 = (bf16[128,512]{1,0:T(8,128)(2,1)S(1)}, bf16[128,512]{1,0:T(8,128)(2,1)S(1)}, u32[]{:S(2)}, u32[]{:S(2)}) collective-permute-start(bf16[128,512]{1,0:T(8,128)(2,1)S(1)} %subtract_convert_fusion.9), channel_id=1, source_target_pairs={{0,4},{4,8},{8,12},{12,16},{16,20},{20,24},{24,28},{28,32},{32,36}... | collective-permute-start | bytes 393224 | tf_op jit(solution)/shard_map/ppermute | solution.py:15
  30.5 17.2 %collective-permute-start.6 = (bf16[128,512]{1,0:T(8,128)(2,1)S(1)}, bf16[128,512]{1,0:T(8,128)(2,1)S(1)}, u32[]{:S(2)}, u32[]{:S(2)}) collective-permute-start(bf16[128,512]{1,0:T(8,128)(2,1)S(1)} %subtract_convert_fusion.10), channel_id=1, source_target_pairs={{0,4},{4,8},{8,12},{12,16},{16,20},{20,24},{24,28},{28,32},{32,36}... | collective-permute-start | bytes 393224 | tf_op jit(solution)/shard_map/ppermute | solution.py:15
  34.6 17.2 %collective-permute-start.5 = (bf16[128,512]{1,0:T(8,128)(2,1)S(1)}, bf16[128,512]{1,0:T(8,128)(2,1)S(1)}, u32[]{:S(2)}, u32[]{:S(2)}) collective-permute-start(bf16[128,512]{1,0:T(8,128)(2,1)S(1)} %subtract_convert_fusion.11), channel_id=1, source_target_pairs={{0,4},{4,8},{8,12},{12,16},{16,20},{20,24},{24,28},{28,32},{32,36}... | collective-permute-start | bytes 393224 | tf_op jit(solution)/shard_map/ppermute | solution.py:15
  38.4 17.2 %collective-permute-start.4 = (bf16[128,512]{1,0:T(8,128)(2,1)S(1)}, bf16[128,512]{1,0:T(8,128)(2,1)S(1)}, u32[]{:S(2)}, u32[]{:S(2)}) collective-permute-start(bf16[128,512]{1,0:T(8,128)(2,1)S(1)} %subtract_convert_fusion.12), channel_id=1, source_target_pairs={{0,4},{4,8},{8,12},{12,16},{16,20},{20,24},{24,28},{28,32},{32,36}... | collective-permute-start | bytes 393224 | tf_op jit(solution)/shard_map/ppermute | solution.py:15
  44.5 25.1 %collective-permute-start.11 = (bf16[128,512]{1,0:T(8,128)(2,1)S(1)}, bf16[128,512]{1,0:T(8,128)(2,1)S(1)}, u32[]{:S(2)}, u32[]{:S(2)}) collective-permute-start(bf16[128,512]{1,0:T(8,128)(2,1)S(1)} %subtract_convert_fusion.5), channel_id=1, source_target_pairs={{0,4},{4,8},{8,12},{12,16},{16,20},{20,24},{24,28},{28,32},{32,36}... | collective-permute-start | bytes 393224 | tf_op jit(solution)/shard_map/ppermute | solution.py:15
  48.3 20.6 %collective-permute-start.10 = (bf16[128,512]{1,0:T(8,128)(2,1)S(1)}, bf16[128,512]{1,0:T(8,128)(2,1)S(1)}, u32[]{:S(2)}, u32[]{:S(2)}) collective-permute-start(bf16[128,512]{1,0:T(8,128)(2,1)S(1)} %subtract_convert_fusion.6), channel_id=1, source_target_pairs={{0,4},{4,8},{8,12},{12,16},{16,20},{20,24},{24,28},{28,32},{32,36}... | collective-permute-start | bytes 393224 | tf_op jit(solution)/shard_map/ppermute | solution.py:15
  52.4 15.9 %collective-permute-start.9 = (bf16[128,512]{1,0:T(8,128)(2,1)S(1)}, bf16[128,512]{1,0:T(8,128)(2,1)S(1)}, u32[]{:S(2)}, u32[]{:S(2)}) collective-permute-start(bf16[128,512]{1,0:T(8,128)(2,1)S(1)} %subtract_convert_fusion.7), channel_id=1, source_target_pairs={{0,4},{4,8},{8,12},{12,16},{16,20},{20,24},{24,28},{28,32},{32,36}... | collective-permute-start | bytes 393224 | tf_op jit(solution)/shard_map/ppermute | solution.py:15
  56.2 11.5 %collective-permute-start.8 = (bf16[128,512]{1,0:T(8,128)(2,1)S(1)}, bf16[128,512]{1,0:T(8,128)(2,1)S(1)}, u32[]{:S(2)}, u32[]{:S(2)}) collective-permute-start(bf16[128,512]{1,0:T(8,128)(2,1)S(1)} %subtract_convert_fusion.8), channel_id=1, source_target_pairs={{0,4},{4,8},{8,12},{12,16},{16,20},{20,24},{24,28},{28,32},{32,36}... | collective-permute-start | bytes 393224 | tf_op jit(solution)/shard_map/ppermute | solution.py:15
  69.3 0.7 copy-start.2
  70.3 0.7 copy-start.4
  72.1 11.1 %copy-start.3 = (bf16[128,512]{1,0:T(8,128)(2,1)S(1)}, bf16[128,512]{1,0:T(8,128)(2,1)}, u32[]{:S(2)}) copy-start(bf16[128,512]{1,0:T(8,128)(2,1)} %copy-done.2) | copy-start | bytes 393220
  72.1 6.4 %collective-permute-start.12 = (bf16[256,512]{1,0:T(8,128)(2,1)S(1)}, bf16[256,512]{1,0:T(8,128)(2,1)S(1)}, u32[]{:S(2)}, u32[]{:S(2)}) collective-permute-start(bf16[256,512]{1,0:T(8,128)(2,1)S(1)} %dynamic-slice_convert_fusion), channel_id=1, source_target_pairs={{0,1},{1,0},{2,3},{3,2},{4,5},{5,4},{6,7},{7,6},{8,9},{9,8},{10,11... | collective-permute-start | bytes 786440 | tf_op jit(solution)/shard_map/ppermute | solution.py:20
  78.6 11.0 %collective-permute-start.13 = (bf16[256,512]{1,0:T(8,128)(2,1)S(1)}, bf16[256,512]{1,0:T(8,128)(2,1)S(1)}, u32[]{:S(2)}, u32[]{:S(2)}) collective-permute-start(bf16[256,512]{1,0:T(8,128)(2,1)S(1)} %add_convert_fusion), channel_id=1, source_target_pairs={{0,2},{1,3},{2,0},{3,1},{4,6},{5,7},{6,4},{7,5},{8,10},{9,11},{10,... | collective-permute-start | bytes 786440 | tf_op jit(solution)/shard_map/ppermute | solution.py:20
  89.7 4.2 %collective-permute-start.14 = (bf16[256,512]{1,0:T(8,128)(2,1)S(1)}, bf16[256,512]{1,0:T(8,128)(2,1)S(1)}, u32[]{:S(2)}, u32[]{:S(2)}) collective-permute-start(bf16[256,512]{1,0:T(8,128)(2,1)S(1)} %subtract_convert_fusion), channel_id=1, source_target_pairs={{0,1},{1,0},{2,3},{3,2},{4,5},{5,4},{6,7},{7,6},{8,9},{9,8},{10,11... | collective-permute-start | bytes 786440 | tf_op jit(solution)/shard_map/ppermute | solution.py:20

commit v2 on v1

v2 whole, which is shorter than its diff:
```python
import functools
import math

import jax
import jax.numpy as jnp
from jax import lax
from jax.experimental import pallas as pl
from jax.experimental.pallas import tpu as pltpu
from jax.sharding import PartitionSpec as P

step_right = 0.25
step_left = 0.1
f32 = jnp.float32
bf16 = jnp.bfloat16
vmem_bytes = 12 << 20
in_vmem = pl.BlockSpec(memory_space=pltpu.VMEM)
in_hbm = pl.BlockSpec(memory_space=pltpu.HBM)
params = pltpu.CompilerParams(vmem_limit_bytes=vmem_bytes)


def passed_along(value):
    count = lax.axis_size("blk")
    return lax.ppermute(value, "blk", [(i, (i + 1) % count) for i in range(count)])


def both(value, bit):
    groups = [[i, i ^ bit] for i in range(lax.axis_size("lane")) if i < i ^ bit]
    return lax.all_gather(value, "lane", axis=0, axis_index_groups=groups, tiled=False)


def keep_hbm(*arrays):
    return [pltpu.with_memory_space_constraint(x, pltpu.HBM) for x in arrays]


def keep_vmem(*arrays):
    return [pltpu.with_memory_space_constraint(x, pltpu.VMEM) for x in arrays]


def cost(n, w, products):
    return pl.CostEstimate(flops=2 * products * n * w * w, bytes_accessed=8 * n * w, transcendentals=0)


def times_transposed(a, left):
    return lax.dot_general(a, left, (((1,), (1,)), ((), ())), preferred_element_type=f32)


def errors(predicted, target, codes, shifts, scale):
    rows, columns = predicted.shape
    by_row = jnp.broadcast_to(shifts, (128, rows)).T
    by_row = jnp.concatenate([by_row] * (columns // 128), axis=1)
    bits = jnp.right_shift(jnp.broadcast_to(codes, (rows, columns)), by_row) & 1
    return jnp.where(bits == 1, predicted * scale - target.astype(f32), 0.0).astype(bf16)


def stepped(right, error, left, scale):
    grad = jnp.dot(error, left, preferred_element_type=f32)
    return (right.astype(f32) - step_right * scale * grad).astype(bf16)


def first_kernel(n, scale, right_hbm, left_hbm, observed_hbm, codes_hbm, shifts_hbm,
                 out, error, right, left, codes, shifts, target, sems):
    pairs = [
        (right_hbm.at[0, pl.ds(0, n)], right),
        (left_hbm, left),
        (codes_hbm, codes),
        (shifts_hbm, shifts),
        (observed_hbm.at[0, 0, pl.ds(0, n)], target),
    ]
    copies = [pltpu.make_async_copy(a, b, sems.at[i]) for i, (a, b) in enumerate(pairs)]
    for c in copies:
        c.start()
    for c in copies[:2]:
        c.wait()
    predicted = times_transposed(right[...], left[...])
    for c in copies[2:]:
        c.wait()
    err = errors(predicted, target[...], codes[...], shifts[0:1, 0, 0:n], scale)
    error[...] = err
    out[...] = stepped(right[...], err, left[...], scale)


def second_kernel(n, scale, right_hbm, observed_hbm, left, codes, shifts,
                  out, error, right, following, target, sems):
    pairs = [
        (right_hbm.at[0, pl.ds(n, n)], right),
        (observed_hbm.at[0, 0, pl.ds(n, n)], target),
        (observed_hbm.at[0, 1, pl.ds(0, n)], following),
    ]
    copies = [pltpu.make_async_copy(a, b, sems.at[i]) for i, (a, b) in enumerate(pairs)]
    for c in copies:
        c.start()
    copies[0].wait()
    predicted = times_transposed(right[...], left[...])
    copies[1].wait()
    err = errors(predicted, target[...], codes[...], shifts[0:1, 0, n : 2 * n], scale)
    error[...] = err
    out[...] = stepped(right[...], err, left[...], scale)
    copies[2].wait()


def visit_kernel(s, a, n, scale, observed_hbm, right, left, target, codes, shifts, prior, out, error, following, sem):
    s_next, a_next = (s + 1, 0) if a else (s, n)
    copy = pltpu.make_async_copy(observed_hbm.at[0, s_next, pl.ds(a_next, n)], following, sem)
    copy.start()
    predicted = times_transposed(right[...], left[...])
    err = errors(predicted, target[...], codes[...], shifts[0:1, s, a : a + n], scale)
    error[...] = err
    out[...] = stepped(right[...], err, left[...], scale)
    copy.wait()


def last_kernel(s, a, n, scale, right, left, target, codes, shifts, prior, grad_sum, out, theirs, mine, total):
    half = left.shape[0] // 2
    core = lax.rem(lax.axis_index("lane"), 2)
    predicted = times_transposed(right[...], left[...])
    err = errors(predicted, target[...], codes[...], shifts[0:1, s, a : a + n], scale)
    total[...] = grad_sum[...] + lax.dot_general(
        err, right[...], (((0,), (0,)), ((), ())), preferred_element_type=f32
    )
    theirs[...] = total[pl.ds(pl.multiple_of((1 - core) * half, half), half), :].astype(bf16)
    mine[...] = total[pl.ds(pl.multiple_of(core * half, half), half), :]
    out[...] = stepped(right[...], err, left[...], scale)


def store_kernel(left, first, second, left_hbm, right_hbm, sems):
    n = first.shape[0]
    pairs = [(left, left_hbm), (first, right_hbm.at[0, pl.ds(0, n)]), (second, right_hbm.at[0, pl.ds(n, n)])]
    copies = [pltpu.make_async_copy(a, b, sems.at[i]) for i, (a, b) in enumerate(pairs)]
    for c in copies:
        c.start()
    for c in copies:
        c.wait()


def local(left_factor, right_factor, observed, row_codes, shift_codes):
    rows, w = left_factor.shape
    scale = 1.0 / math.sqrt(w)
    steps = observed.shape[1]
    n = right_factor.shape[1] // 2
    part, tile = pltpu.VMEM((n, w), bf16), pltpu.VMEM((n, rows), bf16)
    right_hbm, left_hbm, observed_hbm, codes_hbm, shifts_hbm = keep_hbm(
        right_factor, left_factor, observed, row_codes[None, :], shift_codes
    )
    after_a, error_a, right_a, plain_left, codes, shifts = pl.pallas_call(
        functools.partial(first_kernel, n, scale),
        out_shape=[part, tile, part, pltpu.VMEM((rows, w), bf16), pltpu.VMEM((1, rows), jnp.int32),
                   pltpu.VMEM(shift_codes.shape, jnp.int32)],
        in_specs=[in_hbm] * 5,
        out_specs=[in_vmem] * 6,
        scratch_shapes=[pltpu.VMEM((n, rows), bf16), pltpu.SemaphoreType.DMA((5,))],
        compiler_params=params,
        cost_estimate=cost(n, w, 2),
        name="first_visit",
    )(right_hbm, left_hbm, observed_hbm, codes_hbm, shifts_hbm)
    moving = [passed_along(after_a), None]
    left, codes, shifts = keep_vmem(plain_left, codes, shifts)
    after_b, error_b, right_b, following = pl.pallas_call(
        functools.partial(second_kernel, n, scale),
        out_shape=[part, tile, part, tile],
        in_specs=[in_hbm] * 2 + [in_vmem] * 3,
        out_specs=[in_vmem] * 4,
        scratch_shapes=[pltpu.VMEM((n, rows), bf16), pltpu.SemaphoreType.DMA((3,))],
        compiler_params=params,
        cost_estimate=cost(n, w, 2),
        name="second_visit",
    )(right_hbm, observed_hbm, left, codes, shifts)
    moving[1] = passed_along(after_b)

    def left_gradient(error, right):
        return lax.dot_general(error, right, (((0,), (0,)), ((), ())), preferred_element_type=f32)

    grad_sum = left_gradient(error_a, right_a) + left_gradient(error_b, right_b)
    parts, error = [None, None], error_b
    for s in range(1, steps):
        for i in range(2):
            right, = keep_vmem(moving[i])
            if s + 1 == steps and i == 1:
                grad_in, = keep_vmem(grad_sum)
                parts[i], theirs, mine = pl.pallas_call(
                    functools.partial(last_kernel, s, i * n, n, scale),
                    out_shape=[part, pltpu.VMEM((rows // 2, w), bf16), pltpu.VMEM((rows // 2, w), f32)],
                    in_specs=[in_vmem] * 7,
                    out_specs=[in_vmem] * 3,
                    scratch_shapes=[pltpu.VMEM((rows, w), f32)],
                    compiler_params=params,
                    cost_estimate=cost(n, w, 3),
                    name="last_visit",
                )(right, left, *keep_vmem(following), codes, shifts, *keep_vmem(error), grad_in)
                continue
            parts[i], error, following = pl.pallas_call(
                functools.partial(visit_kernel, s, i * n, n, scale),
                out_shape=[part, tile, tile],
                in_specs=[in_hbm] + [in_vmem] * 6,
                out_specs=[in_vmem] * 3,
                scratch_shapes=[pltpu.SemaphoreType.DMA],
                compiler_params=params,
                cost_estimate=cost(n, w, 2),
                name="visit",
            )(observed_hbm, right, left, *keep_vmem(following), codes, shifts, *keep_vmem(error))
            grad_sum = grad_sum + left_gradient(error, moving[i])
            if s + 1 < steps:
                moving[i] = passed_along(parts[i])

    half = rows // 2
    core = lax.axis_index("lane") % 2
    own_rows = lax.dynamic_slice_in_dim(plain_left, core * half, half, 0)
    sent = both(theirs, 1)
    chip_sum = mine + jnp.where(core == 0, sent[1], sent[0]).astype(f32)
    sums = both(chip_sum.astype(bf16), 2).astype(f32)
    renewed = own_rows.astype(f32) - step_left * scale * (sums[0] + sums[1])
    new_left = both(renewed.astype(bf16), 1).reshape(rows, w)
    return tuple(
        pl.pallas_call(
            store_kernel,
            out_shape=[jax.ShapeDtypeStruct((rows, w), bf16), jax.ShapeDtypeStruct(right_factor.shape, bf16)],
            in_specs=[in_vmem] * 3,
            out_specs=[in_hbm] * 2,
            scratch_shapes=[pltpu.SemaphoreType.DMA((3,))],
            compiler_params=params,
            name="store",
        )(*keep_vmem(new_left, *parts))
    )


def solution(mesh):
    in_specs = (
        P("blk", None),
        P("lane", "blk", None),
        P("lane", None, None, "blk"),
        P("blk"),
        P("lane", None, "blk"),
    )
    out_specs = (P("blk", None), P("lane", "blk", None))
    return jax.shard_map(local, mesh=mesh, in_specs=in_specs, out_specs=out_specs, check_vma=False)
```

time: 95.5 us -> 76.2 us (0.80)
  starting transfers between devices: 54.7 us -> 15.1 us
  matrix products: 22.2 us -> 2.47 us
  blocking collectives: 0 us -> 17.6 us
  waiting for transfers between devices: 12.8 us -> 29 us
  Pallas kernels: 0 us -> 10.3 us
  local copies, waits for them, and re-layouts: 1.93 us -> 0 us
  other arithmetic: 1.89 us -> 0.38 us
    ppermute x12 -> x6, starting transfers between devices: 41.9 us -> 15.1 us  [passed_along(): lax.ppermute(value, 'blk', [(i, (i + 1) % count) for i in range(count)])]
    ppermute x12 -> x6, waiting for transfers between devices: 6.79 us -> 29 us  [passed_along(): lax.ppermute(value, 'blk', [(i, (i + 1) % count) for i in range(count)])]
    dot_general x48 -> x7, matrix products: 22.2 us -> 2.47 us  [left_gradient(): lax.dot_general(error, right, (((0,), (0,)), ((), ())), preferred_element...]
    all_gather x0 -> x3, blocking collectives: none -> 17.6 us  [both(): lax.all_gather(value, 'lane', axis=0, axis_index_groups=groups, tiled=False)]
    ppermute x3 -> x0, starting transfers between devices: 12.9 us -> none  [swapped(): return lax.ppermute(value, 'lane', [(i, i ^ bit) for i in range(count)])]
    pallas_call x0 -> x9, Pallas kernels: none -> 10.3 us  [the longest x5 4.79 us: local(): pl.pallas_call(functools.partial(visit_kernel, s, i * n, n, scale), out_s...]
    ppermute x3 -> x0, waiting for transfers between devices: 5.99 us -> none  [swapped(): return lax.ppermute(value, 'lane', [(i, i ^ bit) for i in range(count)])]
    unnamed x14 -> x0, local copies, waits for them, and re-layouts: 1 us -> none
  transfers between devices with their start and end apart: 15 -> 6, of which waited for: 3 -> 6; matrix products, arithmetic and copies ran while one was open for 20% -> 3% of each run, Pallas kernels for 0% -> 9%
where the time goes in v2:
time: 76.2 us; the launch traced here: 75.7 us
  waiting for transfers between devices  29 us (38%)
  blocking collectives  17.6 us (23%)
  starting transfers between devices  15.1 us (20%)
  Pallas kernels  10.3 us (14%)
  matrix products  2.47 us (3%)
  between operations  0.8 us (1%)
    ppermute x6, waiting for transfers between devices, passed_along(): lax.ppermute(value, 'blk', [(i, (i + 1) % count) for i in range(count)])  29 us
    all_gather x3, blocking collectives, both(): lax.all_gather(value, 'lane', axis=0, axis_index_groups=groups, tiled=False)  17.6 us
    ppermute x6, starting transfers between devices, passed_along(): lax.ppermute(value, 'blk', [(i, (i + 1) % count) for i in range(count)])  15.1 us
    pallas_call x5, Pallas kernels, local(): pl.pallas_call(functools.partial(visit_kernel, s, i * n, n, scale), out_s...  4.79 us
    dot_general x7, matrix products, left_gradient(): lax.dot_general(error, right, (((0,), (0,)), ((), ())), preferred_element...  2.47 us
    pallas_call x1, Pallas kernels, local(): pl.pallas_call(functools.partial(first_kernel, n, scale), out_shape=[part...  1.87 us
    pallas_call x1, Pallas kernels, local(): pl.pallas_call(functools.partial(second_kernel, n, scale), out_shape=[par...  1.68 us
  transfers between devices with their start and end apart: 6, of which 6 were waited for; matrix products, arithmetic and copies ran while one was open for 3% of the time, Pallas kernels for 9%

profile of v2, /device:TPU:1, one launch (start us, length us, event | category | flops | bytes accessed | tf_op | source)
XLA Modules:
  0.0 75.7 jit_solution(845983000296105909)
XLA Ops:
  0.6 1.9 %first_visit.1 = (bf16[256,512]{1,0:T(8,128)(2,1)S(1)}, bf16[256,512]{1,0:T(8,128)(2,1)S(1)}, bf16[256,512]{1,0:T(8,128)(2,1)S(1)}, bf16[512,512]{1,0:T(8,128)(2...) custom-call(bf16[1,512,512]{2,1,0:T(8,128)(2,1)} %right_hbm.3, bf16[512,512]{1,0:T(8,128)(2,1)} %left_hbm.1, ...), custom_call_target="tpu_custom_call" | custom-call | flops 268435456 | bytes 1048576 | tf_op jit(solution)/shard_map/first_visit/pallas_call | solution.py:144
  2.5 4.0 %collective-permute-start.1 = (bf16[256,512]{1,0:T(8,128)(2,1)S(1)}, bf16[256,512]{1,0:T(8,128)(2,1)S(1)}, u32[]{:S(2)}, u32[]{:S(2)}) collective-permute-start(bf16[256,512]{1,0:T(8,128)(2,1)S(1)} %get-tuple-element.34), channel_id=1, source_target_pairs={{0,4},{4,8},{8,12},{12,16},{16,20},{20,24},{24,28},{28,32},{32,36}... | collective-permute-start | bytes 786440 | tf_op jit(solution)/shard_map/ppermute | solution.py:23
  6.5 1.7 %second_visit.1 = (bf16[256,512]{1,0:T(8,128)(2,1)S(1)}, bf16[256,512]{1,0:T(8,128)(2,1)S(1)}, bf16[256,512]{1,0:T(8,128)(2,1)S(1)}, bf16[256,512]{1,0:T(8,128)(2,1)S(1)}) custom-call(bf16[1,512,512]{2,1,0:T(8,128)(2,1)} %right_hbm.3, bf16[1,4,512,512]{3,2,1,0:T(8,128)(2,1)} %observed_hbm.13, bf16[512,512]{1,0:T(8,128)(2,1)S(1)} %get-tuple-element.30.left, ...), custom_call_target="tpu_custom_call" | custom-call | flops 268435456 | bytes 1048576 | tf_op jit(solution)/shard_map/second_visit/pallas_call | solution.py:157
  8.2 3.4 %collective-permute-start = (bf16[256,512]{1,0:T(8,128)(2,1)S(1)}, bf16[256,512]{1,0:T(8,128)(2,1)S(1)}, u32[]{:S(2)}, u32[]{:S(2)}) collective-permute-start(bf16[256,512]{1,0:T(8,128)(2,1)S(1)} %get-tuple-element.33), channel_id=1, source_target_pairs={{0,4},{4,8},{8,12},{12,16},{16,20},{20,24},{24,28},{28,32},{32,36}... | collective-permute-start | bytes 786440 | tf_op jit(solution)/shard_map/ppermute | solution.py:23
  11.7 0.3 fusion.8
  12.0 0.3 convolution_add_fusion.1
  12.3 11.3 %collective-permute-done.1.right = bf16[256,512]{1,0:T(8,128)(2,1)S(1)} collective-permute-done((bf16[256,512]{1,0:T(8,128)(2,1)S(1)}, bf16[256,512]{1,0:T(8,128)(2,1)S(1)}, u32[]{:S(2)}, u32[]{:S(2)}) %collective-permute-start.1) | collective-permute-done | bytes 262176 | tf_op jit(solution)/shard_map/ppermute | solution.py:23
  23.7 1.0 %visit.5 = (bf16[256,512]{1,0:T(8,128)(2,1)S(1)}, bf16[256,512]{1,0:T(8,128)(2,1)S(1)}, bf16[256,512]{1,0:T(8,128)(2,1)S(1)}) custom-call(bf16[1,4,512,512]{3,2,1,0:T(8,128)(2,1)} %observed_hbm.13, bf16[256,512]{1,0:T(8,128)(2,1)S(1)} %collective-permute-done.1.right, bf16[512,512]{1,0:T(8,128)(2,1)S(1)} %get-tuple-element.30.left, ...), custom_call_target="tpu_custom_call" | custom-call | flops 268435456 | bytes 1048576 | tf_op jit(solution)/shard_map/visit/pallas_call | solution.py:190
  24.7 1.9 %collective-permute-start.3 = (bf16[256,512]{1,0:T(8,128)(2,1)S(1)}, bf16[256,512]{1,0:T(8,128)(2,1)S(1)}, u32[]{:S(2)}, u32[]{:S(2)}) collective-permute-start(bf16[256,512]{1,0:T(8,128)(2,1)S(1)} %get-tuple-element.40), channel_id=1, source_target_pairs={{0,4},{4,8},{8,12},{12,16},{16,20},{20,24},{24,28},{28,32},{32,36}... | collective-permute-start | bytes 786440 | tf_op jit(solution)/shard_map/ppermute | solution.py:23
  26.6 2.7 %collective-permute-done.right = bf16[256,512]{1,0:T(8,128)(2,1)S(1)} collective-permute-done((bf16[256,512]{1,0:T(8,128)(2,1)S(1)}, bf16[256,512]{1,0:T(8,128)(2,1)S(1)}, u32[]{:S(2)}, u32[]{:S(2)}) %collective-permute-start) | collective-permute-done | bytes 262176 | tf_op jit(solution)/shard_map/ppermute | solution.py:23
  29.3 1.0 %visit.6 = (bf16[256,512]{1,0:T(8,128)(2,1)S(1)}, bf16[256,512]{1,0:T(8,128)(2,1)S(1)}, bf16[256,512]{1,0:T(8,128)(2,1)S(1)}) custom-call(bf16[1,4,512,512]{3,2,1,0:T(8,128)(2,1)} %observed_hbm.13, bf16[256,512]{1,0:T(8,128)(2,1)S(1)} %collective-permute-done.right, bf16[512,512]{1,0:T(8,128)(2,1)S(1)} %get-tuple-element.30.left, ...), custom_call_target="tpu_custom_call" | custom-call | flops 268435456 | bytes 1048576 | tf_op jit(solution)/shard_map/visit/pallas_call | solution.py:190
  30.3 1.9 %collective-permute-start.2 = (bf16[256,512]{1,0:T(8,128)(2,1)S(1)}, bf16[256,512]{1,0:T(8,128)(2,1)S(1)}, u32[]{:S(2)}, u32[]{:S(2)}) collective-permute-start(bf16[256,512]{1,0:T(8,128)(2,1)S(1)} %get-tuple-element.39), channel_id=1, source_target_pairs={{0,4},{4,8},{8,12},{12,16},{16,20},{20,24},{24,28},{28,32},{32,36}... | collective-permute-start | bytes 786440 | tf_op jit(solution)/shard_map/ppermute | solution.py:23
  32.2 0.3 fusion.9
  32.5 4.0 %collective-permute-done.3.right = bf16[256,512]{1,0:T(8,128)(2,1)S(1)} collective-permute-done((bf16[256,512]{1,0:T(8,128)(2,1)S(1)}, bf16[256,512]{1,0:T(8,128)(2,1)S(1)}, u32[]{:S(2)}, u32[]{:S(2)}) %collective-permute-start.3) | collective-permute-done | bytes 262176 | tf_op jit(solution)/shard_map/ppermute | solution.py:23
  36.5 1.0 %visit.7 = (bf16[256,512]{1,0:T(8,128)(2,1)S(1)}, bf16[256,512]{1,0:T(8,128)(2,1)S(1)}, bf16[256,512]{1,0:T(8,128)(2,1)S(1)}) custom-call(bf16[1,4,512,512]{3,2,1,0:T(8,128)(2,1)} %observed_hbm.13, bf16[256,512]{1,0:T(8,128)(2,1)S(1)} %collective-permute-done.3.right, bf16[512,512]{1,0:T(8,128)(2,1)S(1)} %get-tuple-element.30.left, ...), custom_call_target="tpu_custom_call" | custom-call | flops 268435456 | bytes 1048576 | tf_op jit(solution)/shard_map/visit/pallas_call | solution.py:190
  37.5 1.9 %collective-permute-start.5 = (bf16[256,512]{1,0:T(8,128)(2,1)S(1)}, bf16[256,512]{1,0:T(8,128)(2,1)S(1)}, u32[]{:S(2)}, u32[]{:S(2)}) collective-permute-start(bf16[256,512]{1,0:T(8,128)(2,1)S(1)} %get-tuple-element.46), channel_id=1, source_target_pairs={{0,4},{4,8},{8,12},{12,16},{16,20},{20,24},{24,28},{28,32},{32,36}... | collective-permute-start | bytes 786440 | tf_op jit(solution)/shard_map/ppermute | solution.py:23
  39.4 3.6 %collective-permute-done.2.right = bf16[256,512]{1,0:T(8,128)(2,1)S(1)} collective-permute-done((bf16[256,512]{1,0:T(8,128)(2,1)S(1)}, bf16[256,512]{1,0:T(8,128)(2,1)S(1)}, u32[]{:S(2)}, u32[]{:S(2)}) %collective-permute-start.2) | collective-permute-done | bytes 262176 | tf_op jit(solution)/shard_map/ppermute | solution.py:23
  43.0 1.0 %visit.8 = (bf16[256,512]{1,0:T(8,128)(2,1)S(1)}, bf16[256,512]{1,0:T(8,128)(2,1)S(1)}, bf16[256,512]{1,0:T(8,128)(2,1)S(1)}) custom-call(bf16[1,4,512,512]{3,2,1,0:T(8,128)(2,1)} %observed_hbm.13, bf16[256,512]{1,0:T(8,128)(2,1)S(1)} %collective-permute-done.2.right, bf16[512,512]{1,0:T(8,128)(2,1)S(1)} %get-tuple-element.30.left, ...), custom_call_target="tpu_custom_call" | custom-call | flops 268435456 | bytes 1048576 | tf_op jit(solution)/shard_map/visit/pallas_call | solution.py:190
  43.9 1.9 %collective-permute-start.4 = (bf16[256,512]{1,0:T(8,128)(2,1)S(1)}, bf16[256,512]{1,0:T(8,128)(2,1)S(1)}, u32[]{:S(2)}, u32[]{:S(2)}) collective-permute-start(bf16[256,512]{1,0:T(8,128)(2,1)S(1)} %get-tuple-element.45), channel_id=1, source_target_pairs={{0,4},{4,8},{8,12},{12,16},{16,20},{20,24},{24,28},{28,32},{32,36}... | collective-permute-start | bytes 786440 | tf_op jit(solution)/shard_map/ppermute | solution.py:23
  45.9 0.3 fusion.10
  46.2 0.3 fusion.11
  46.5 2.3 %collective-permute-done.5.right = bf16[256,512]{1,0:T(8,128)(2,1)S(1)} collective-permute-done((bf16[256,512]{1,0:T(8,128)(2,1)S(1)}, bf16[256,512]{1,0:T(8,128)(2,1)S(1)}, u32[]{:S(2)}, u32[]{:S(2)}) %collective-permute-start.5) | collective-permute-done | bytes 262176 | tf_op jit(solution)/shard_map/ppermute | solution.py:23
  48.8 1.0 %visit.9 = (bf16[256,512]{1,0:T(8,128)(2,1)S(1)}, bf16[256,512]{1,0:T(8,128)(2,1)S(1)}, bf16[256,512]{1,0:T(8,128)(2,1)S(1)}) custom-call(bf16[1,4,512,512]{3,2,1,0:T(8,128)(2,1)} %observed_hbm.13, bf16[256,512]{1,0:T(8,128)(2,1)S(1)} %collective-permute-done.5.right, bf16[512,512]{1,0:T(8,128)(2,1)S(1)} %get-tuple-element.30.left, ...), custom_call_target="tpu_custom_call" | custom-call | flops 268435456 | bytes 1048576 | tf_op jit(solution)/shard_map/visit/pallas_call | solution.py:190
  49.8 0.3 fusion.12
  50.1 0.5 fusion.3.grad_sum
  50.6 5.1 %collective-permute-done.4.right = bf16[256,512]{1,0:T(8,128)(2,1)S(1)} collective-permute-done((bf16[256,512]{1,0:T(8,128)(2,1)S(1)}, bf16[256,512]{1,0:T(8,128)(2,1)S(1)}, u32[]{:S(2)}, u32[]{:S(2)}) %collective-permute-start.4) | collective-permute-done | bytes 262176 | tf_op jit(solution)/shard_map/ppermute | solution.py:23
  55.7 1.0 %last_visit.1 = (bf16[256,512]{1,0:T(8,128)(2,1)S(1)}, bf16[256,512]{1,0:T(8,128)(2,1)S(1)}, f32[256,512]{1,0:T(8,128)S(1)}) custom-call(bf16[256,512]{1,0:T(8,128)(2,1)S(1)} %collective-permute-done.4.right, bf16[512,512]{1,0:T(8,128)(2,1)S(1)} %get-tuple-element.30.left, bf16[256,512]{1,0:T(8,128)(2,1)S(1)} %get-tuple-element.49.target, ...), custom_call_target="tpu_custom_call" | custom-call | flops 402653184 | bytes 1048576 | tf_op jit(solution)/shard_map/last_visit/pallas_call | solution.py:179
  56.7 4.9 %all-gather = bf16[512,512]{1,0:T(8,128)(2,1)S(1)} all-gather(bf16[256,512]{1,0:T(8,128)(2,1)S(1)} %get-tuple-element.55), channel_id=2, replica_groups={{0,1},{2,3},{4,5},{6,7},{8,9},{10,11},{12,13},{14,15},{16,17},{18,19},{..., dimensions={0}, use_global_device_ids=true | all-gather | bytes 786432 | tf_op jit(solution)/shard_map/all_gather | solution.py:28
  61.7 9.7 %all-gather.1 = bf16[512,512]{1,0:T(8,128)(2,1)S(1)} all-gather(bf16[256,512]{1,0:T(8,128)(2,1)S(1)} %fusion.7), channel_id=3, replica_groups={{0,2},{1,3},{4,6},{5,7},{8,10},{9,11},{12,14},{13,15},{16,18},{17,19},{..., dimensions={0}, use_global_device_ids=true | all-gather | bytes 786432 | tf_op jit(solution)/shard_map/all_gather | solution.py:28
  71.5 0.1 fusion.6
  71.7 3.0 %all-gather.2.left = bf16[512,512]{1,0:T(8,128)(2,1)S(1)} all-gather(bf16[256,512]{1,0:T(8,128)(2,1)S(1)} %fusion.6), channel_id=4, replica_groups={{0,1},{2,3},{4,5},{6,7},{8,9},{10,11},{12,13},{14,15},{16,17},{18,19},{..., dimensions={0}, use_global_device_ids=true | all-gather | bytes 786432 | tf_op jit(solution)/shard_map/all_gather | solution.py:28
  74.7 1.0 %store.1 = (bf16[512,512]{1,0:T(8,128)(2,1)}, bf16[1,512,512]{2,1,0:T(8,128)(2,1)}) custom-call(bf16[512,512]{1,0:T(8,128)(2,1)S(1)} %all-gather.2.left, bf16[256,512]{1,0:T(8,128)(2,1)S(1)} %get-tuple-element.56.first, bf16[256,512]{1,0:T(8,128)(2,1)S(1)} %get-tuple-element.57.second), custom_call_target="tpu_custom_call" | custom-call | tf_op jit(solution)/shard_map/store/pallas_call | solution.py:213
  (2 shorter events, 0.2 us)
Async XLA Ops:
  2.5 21.2 %collective-permute-start.1 = (bf16[256,512]{1,0:T(8,128)(2,1)S(1)}, bf16[256,512]{1,0:T(8,128)(2,1)S(1)}, u32[]{:S(2)}, u32[]{:S(2)}) collective-permute-start(bf16[256,512]{1,0:T(8,128)(2,1)S(1)} %get-tuple-element.34), channel_id=1, source_target_pairs={{0,4},{4,8},{8,12},{12,16},{16,20},{20,24},{24,28},{28,32},{32,36}... | collective-permute-start | bytes 786440 | tf_op jit(solution)/shard_map/ppermute | solution.py:23
  8.2 21.1 %collective-permute-start = (bf16[256,512]{1,0:T(8,128)(2,1)S(1)}, bf16[256,512]{1,0:T(8,128)(2,1)S(1)}, u32[]{:S(2)}, u32[]{:S(2)}) collective-permute-start(bf16[256,512]{1,0:T(8,128)(2,1)S(1)} %get-tuple-element.33), channel_id=1, source_target_pairs={{0,4},{4,8},{8,12},{12,16},{16,20},{20,24},{24,28},{28,32},{32,36}... | collective-permute-start | bytes 786440 | tf_op jit(solution)/shard_map/ppermute | solution.py:23
  24.7 11.9 %collective-permute-start.3 = (bf16[256,512]{1,0:T(8,128)(2,1)S(1)}, bf16[256,512]{1,0:T(8,128)(2,1)S(1)}, u32[]{:S(2)}, u32[]{:S(2)}) collective-permute-start(bf16[256,512]{1,0:T(8,128)(2,1)S(1)} %get-tuple-element.40), channel_id=1, source_target_pairs={{0,4},{4,8},{8,12},{12,16},{16,20},{20,24},{24,28},{28,32},{32,36}... | collective-permute-start | bytes 786440 | tf_op jit(solution)/shard_map/ppermute | solution.py:23
  30.3 12.7 %collective-permute-start.2 = (bf16[256,512]{1,0:T(8,128)(2,1)S(1)}, bf16[256,512]{1,0:T(8,128)(2,1)S(1)}, u32[]{:S(2)}, u32[]{:S(2)}) collective-permute-start(bf16[256,512]{1,0:T(8,128)(2,1)S(1)} %get-tuple-element.39), channel_id=1, source_target_pairs={{0,4},{4,8},{8,12},{12,16},{16,20},{20,24},{24,28},{28,32},{32,36}... | collective-permute-start | bytes 786440 | tf_op jit(solution)/shard_map/ppermute | solution.py:23
  37.5 11.3 %collective-permute-start.5 = (bf16[256,512]{1,0:T(8,128)(2,1)S(1)}, bf16[256,512]{1,0:T(8,128)(2,1)S(1)}, u32[]{:S(2)}, u32[]{:S(2)}) collective-permute-start(bf16[256,512]{1,0:T(8,128)(2,1)S(1)} %get-tuple-element.46), channel_id=1, source_target_pairs={{0,4},{4,8},{8,12},{12,16},{16,20},{20,24},{24,28},{28,32},{32,36}... | collective-permute-start | bytes 786440 | tf_op jit(solution)/shard_map/ppermute | solution.py:23
  43.9 11.8 %collective-permute-start.4 = (bf16[256,512]{1,0:T(8,128)(2,1)S(1)}, bf16[256,512]{1,0:T(8,128)(2,1)S(1)}, u32[]{:S(2)}, u32[]{:S(2)}) collective-permute-start(bf16[256,512]{1,0:T(8,128)(2,1)S(1)} %get-tuple-element.45), channel_id=1, source_target_pairs={{0,4},{4,8},{8,12},{12,16},{16,20},{20,24},{24,28},{28,32},{32,36}... | collective-permute-start | bytes 786440 | tf_op jit(solution)/shard_map/ppermute | solution.py:23

commit v3 on v2

v3 whole, which is shorter than its diff:
```python
import functools
import math

import jax
import jax.numpy as jnp
from jax import lax
from jax.experimental import pallas as pl
from jax.experimental.pallas import tpu as pltpu
from jax.sharding import PartitionSpec as P

step_right = 0.25
step_left = 0.1
f32 = jnp.float32
bf16 = jnp.bfloat16
vmem_bytes = 12 << 20
chunk_rows = (256, 256)
in_vmem = pl.BlockSpec(memory_space=pltpu.VMEM)
in_hbm = pl.BlockSpec(memory_space=pltpu.HBM)
costs = (1, 1, 1, 1)


def price(s):
    return pl.CostEstimate(flops=int(costs[s] * 2e8), bytes_accessed=int(costs[s] * 1e6), transcendentals=0)


params = pltpu.CompilerParams(vmem_limit_bytes=vmem_bytes)


def passed_along(value):
    count = lax.axis_size("blk")
    return lax.ppermute(value, "blk", [(i, (i + 1) % count) for i in range(count)])


def both(value, bit):
    groups = [[i, i ^ bit] for i in range(lax.axis_size("lane")) if i < i ^ bit]
    return lax.all_gather(value, "lane", axis=0, axis_index_groups=groups, tiled=False)


def keep_hbm(*arrays):
    return [pltpu.with_memory_space_constraint(x, pltpu.HBM) for x in arrays]


def keep_vmem(*arrays):
    return [pltpu.with_memory_space_constraint(x, pltpu.VMEM) for x in arrays]


def times_transposed(a, left):
    return lax.dot_general(a, left, (((1,), (1,)), ((), ())), preferred_element_type=f32)


def errors(predicted, target, codes, shifts, scale):
    rows, columns = predicted.shape
    by_row = jnp.broadcast_to(shifts, (128, rows)).T
    by_row = jnp.concatenate([by_row] * (columns // 128), axis=1)
    bits = jnp.right_shift(jnp.broadcast_to(codes, (rows, columns)), by_row) & 1
    return jnp.where(bits == 1, predicted * scale - target.astype(f32), 0.0).astype(bf16)


def stepped(right, error, left, scale):
    grad = jnp.dot(error, left, preferred_element_type=f32)
    return (right.astype(f32) - step_right * scale * grad).astype(bf16)


def first_kernel(spans, scale, right_hbm, left_hbm, observed_hbm, codes_hbm, shifts_hbm, out, error, left, codes, shifts, *refs):
    count = len(spans)
    rights, others, target, sems = refs[:count], refs[count : 2 * count - 1], refs[-2], refs[-1]
    pairs = [
        (right_hbm.at[0, pl.ds(*spans[0])], rights[0]),
        (left_hbm, left),
        (observed_hbm.at[0, 0, pl.ds(*spans[0])], target),
        (codes_hbm, codes),
        (shifts_hbm, shifts),
    ]
    for i in range(1, count):
        pairs.append((right_hbm.at[0, pl.ds(*spans[i])], rights[i]))
        pairs.append((observed_hbm.at[0, 0, pl.ds(*spans[i])], others[i - 1]))
    copies = [pltpu.make_async_copy(a, b, sems.at[i]) for i, (a, b) in enumerate(pairs)]
    for c in copies:
        c.start()
    for c in copies[:2]:
        c.wait()
    right = rights[0][...]
    predicted = times_transposed(right, left[...])
    for c in copies[2:5]:
        c.wait()
    err = errors(predicted, target[...], codes[...], shifts[0:1, 0, 0 : spans[0][1]], scale)
    error[...] = err
    out[...] = stepped(right, err, left[...], scale)
    for c in copies[5:]:
        c.wait()


def visit_kernel(s, a, n, scale, right, left, target, codes, shifts, prior, out, error):
    predicted = times_transposed(right[...], left[...])
    err = errors(predicted, target[...], codes[...], shifts[0:1, s, a : a + n], scale)
    error[...] = err
    out[...] = stepped(right[...], err, left[...], scale)


def gradient_kernel(s, spans, observed_hbm, *refs):
    count = len(spans)
    errors_rights, rest = refs[: 2 * count], refs[2 * count :]
    before, out, following, sems = rest[: -count - 2], rest[-count - 2], rest[-count - 1 : -1], rest[-1]
    copies = [
        pltpu.make_async_copy(observed_hbm.at[0, s + 1, pl.ds(*spans[i])], ref, sems.at[i])
        for i, ref in enumerate(following)
    ]
    for c in copies:
        c.start()
    total = before[0][...] if before else None
    for i in range(count):
        error, right = errors_rights[2 * i : 2 * i + 2]
        term = lax.dot_general(error[...], right[...], (((0,), (0,)), ((), ())), preferred_element_type=f32)
        total = term if total is None else total + term
    out[...] = total
    for c in copies:
        c.wait()


def last_kernel(s, a, n, scale, right, left, target, codes, shifts, prior, grad_sum, out, theirs, mine, error):
    half = left.shape[0] // 2
    core = lax.rem(lax.axis_index("lane"), 2)
    predicted = times_transposed(right[...], left[...])
    err = errors(predicted, target[...], codes[...], shifts[0:1, s, a : a + n], scale)
    error[...] = err
    for ref, which in ((theirs, 1 - core), (mine, core)):
        own = pl.ds(pl.multiple_of(which * half, half), half)
        term = lax.dot_general(
            error[:, own], right[...], (((0,), (0,)), ((), ())), preferred_element_type=f32
        )
        ref[...] = (grad_sum[own, :] + term).astype(ref.dtype)
    out[...] = stepped(right[...], err, left[...], scale)


def settle_kernel(s, a, n, scale, right, left, target, codes, shifts, prior, right_out, error, fresh, sem):
    visit_kernel(s, a, n, scale, right, left, target, codes, shifts, prior, fresh, error)
    copy = pltpu.make_async_copy(fresh, right_out.at[0, pl.ds(a, n)], sem)
    copy.start()
    copy.wait()


def combine_kernel(mine, sent, out):
    core = lax.rem(lax.axis_index("lane"), 2)
    out[...] = (mine[...] + sent[1 - core].astype(f32)).astype(bf16)


def renew_kernel(scale, sums, left, out):
    half = out.shape[0]
    core = lax.rem(lax.axis_index("lane"), 2)
    own = left[pl.ds(pl.multiple_of(core * half, half), half), :].astype(f32)
    total = sums[0].astype(f32) + sums[1].astype(f32)
    out[...] = (own - step_left * scale * total).astype(bf16)


def store_kernel(first, left, part, right_hbm, left_hbm, right_out, sems):
    pairs = [(left, left_hbm), (part, right_out.at[0, pl.ds(first, part.shape[0])])]
    copies = [pltpu.make_async_copy(a, b, sems.at[i]) for i, (a, b) in enumerate(pairs)]
    for c in copies:
        c.start()
    for c in copies:
        c.wait()


def local(left_factor, right_factor, observed, row_codes, shift_codes):
    rows, w = left_factor.shape
    scale = 1.0 / math.sqrt(w)
    steps = observed.shape[1]
    spans = [(sum(chunk_rows[:i]), n) for i, n in enumerate(chunk_rows)]
    count = len(spans)
    parts_of = [pltpu.VMEM((n, w), bf16) for _, n in spans]
    tiles = [pltpu.VMEM((n, rows), bf16) for _, n in spans]
    right_hbm, left_hbm, observed_hbm, codes_hbm, shifts_hbm = keep_hbm(
        right_factor, left_factor, observed, row_codes[None, :], shift_codes
    )
    after, error, plain_left, codes, shifts, *loaded = pl.pallas_call(
        functools.partial(first_kernel, spans, scale),
        out_shape=[parts_of[0], tiles[0], pltpu.VMEM((rows, w), bf16), pltpu.VMEM((1, rows), jnp.int32),
                   pltpu.VMEM(shift_codes.shape, jnp.int32), *parts_of, *tiles[1:]],
        in_specs=[in_hbm] * 5,
        out_specs=[in_vmem] * (2 * count + 4),
        scratch_shapes=[tiles[0], pltpu.SemaphoreType.DMA((2 * count + 3,))],
        compiler_params=params,
        cost_estimate=price(0),
        name="first_visit",
    )(right_hbm, left_hbm, observed_hbm, codes_hbm, shifts_hbm)
    left, codes, shifts = keep_vmem(plain_left, codes, shifts)

    def visit(s, i, right, target, prior):
        right, target, prior = keep_vmem(right, target, prior)
        return pl.pallas_call(
            functools.partial(visit_kernel, s, *spans[i], scale),
            out_shape=[parts_of[i], tiles[i]],
            in_specs=[in_vmem] * 6,
            out_specs=[in_vmem] * 2,
            input_output_aliases={2: 1},
            compiler_params=params,
            cost_estimate=price(s),
            name="visit",
        )(right, left, target, codes, shifts, prior)

    moving, held = [passed_along(after)], [error, loaded[0]]
    for i in range(1, count):
        after, error = visit(0, i, loaded[i], loaded[count + i - 1], error)
        moving.append(passed_along(after))
        held += [error, loaded[i]]

    def gradient(s, *operands):
        added = len(operands) > 2 * count
        return pl.pallas_call(
            functools.partial(gradient_kernel, s, spans),
            out_shape=[pltpu.VMEM((rows, w), f32), *tiles],
            in_specs=[in_hbm] + [in_vmem] * len(operands),
            out_specs=[in_vmem] * (count + 1),
            scratch_shapes=[pltpu.SemaphoreType.DMA((count,))],
            input_output_aliases={2 * count + 1: 0} if added else {},
            compiler_params=params,
            cost_estimate=price(s),
            name="gradient",
        )(observed_hbm, *keep_vmem(*operands))

    grad_sum, *following = gradient(0, *held)
    parts = [None] * count
    for s in range(1, steps):
        held = []
        for i in range(count):
            right, = keep_vmem(moving[i])
            if s + 1 == steps and i + 1 == count:
                grad_in, = keep_vmem(grad_sum)
                parts[i], theirs, mine = pl.pallas_call(
                    functools.partial(last_kernel, s, *spans[i], scale),
                    out_shape=[parts_of[i], pltpu.VMEM((rows // 2, w), bf16), pltpu.VMEM((rows // 2, w), f32)],
                    in_specs=[in_vmem] * 7,
                    out_specs=[in_vmem] * 3,
                    scratch_shapes=[tiles[i]],
                    compiler_params=params,
                    cost_estimate=price(s),
                    name="last_visit",
                )(right, left, *keep_vmem(following[i]), codes, shifts, *keep_vmem(error), grad_in)
                continue
            if s + 1 < steps:
                parts[i], error = visit(s, i, moving[i], following[i], error)
            else:
                right_out, error = pl.pallas_call(
                    functools.partial(settle_kernel, s, *spans[i], scale),
                    out_shape=[pltpu.HBM(right_factor.shape, bf16), tiles[i]],
                    in_specs=[in_vmem] * 6,
                    out_specs=[in_hbm, in_vmem],
                    scratch_shapes=[parts_of[i], pltpu.SemaphoreType.DMA],
                    input_output_aliases={2: 1},
                    compiler_params=params,
                    cost_estimate=price(s),
                    name="settle",
                )(right, left, *keep_vmem(following[i]), codes, shifts, *keep_vmem(error))
            held += [error, moving[i]]
            if s + 1 < steps:
                moving[i] = passed_along(parts[i])
            else:
                grad_sum = grad_sum + lax.dot_general(
                    error, held[-1], (((0,), (0,)), ((), ())), preferred_element_type=f32
                )
        if s + 1 < steps:
            grad_sum, *following = gradient(s, *held, grad_sum)

    half = pltpu.VMEM((rows // 2, w), bf16)
    chip_sum = pl.pallas_call(
        combine_kernel, out_shape=half, in_specs=[in_vmem] * 2, out_specs=in_vmem, compiler_params=params, name="combine"
    )(*keep_vmem(mine, both(theirs, 1)))
    renewed = pl.pallas_call(
        functools.partial(renew_kernel, scale), out_shape=half, in_specs=[in_vmem] * 2, out_specs=in_vmem,
        compiler_params=params, name="renew"
    )(*keep_vmem(both(chip_sum, 2)), left)
    new_left = both(renewed, 1).reshape(rows, w)
    return tuple(
        pl.pallas_call(
            functools.partial(store_kernel, spans[-1][0]),
            out_shape=[jax.ShapeDtypeStruct((rows, w), bf16), jax.ShapeDtypeStruct(right_factor.shape, bf16)],
            in_specs=[in_vmem] * 2 + [in_hbm],
            out_specs=[in_hbm] * 2,
            scratch_shapes=[pltpu.SemaphoreType.DMA((2,))],
            input_output_aliases={2: 1},
            compiler_params=params,
            name="store",
        )(*keep_vmem(new_left, parts[-1]), *keep_hbm(right_out))
    )


def solution(mesh):
    in_specs = (
        P("blk", None),
        P("lane", "blk", None),
        P("lane", None, None, "blk"),
        P("blk"),
        P("lane", None, "blk"),
    )
    out_specs = (P("blk", None), P("lane", "blk", None))
    return jax.shard_map(local, mesh=mesh, in_specs=in_specs, out_specs=out_specs, check_vma=False)
```

time: 76.2 us -> 74.9 us (0.983)
  matrix products: 2.47 us -> 0.32 us
  Pallas kernels: 10.3 us -> 11.4 us
    dot_general x7 -> x1, matrix products: 2.47 us -> 0.32 us  [local(): lax.dot_general(error, held[-1], (((0,), (0,)), ((), ())), preferred_elem...]
    pallas_call x9 -> x14, Pallas kernels: 10.3 us -> 11.4 us  [the longest x3 3.21 us: gradient(): pl.pallas_call(functools.partial(gradient_kernel, s, spans), out_shape=[p...]
  transfers between devices with their start and end apart: 6 -> 6, of which waited for: 6 -> 6; matrix products, arithmetic and copies ran while one was open for 3% -> 1% of each run, Pallas kernels for 9% -> 10%
where the time goes in v3:
time: 74.9 us; the launch traced here: 74.5 us
  waiting for transfers between devices  29.1 us (39%)
  blocking collectives  17.6 us (23%)
  starting transfers between devices  15.1 us (20%)
  Pallas kernels  11.4 us (15%)
  between operations  0.78 us (1%)
    ppermute x6, waiting for transfers between devices, passed_along(): lax.ppermute(value, 'blk', [(i, (i + 1) % count) for i in range(count)])  29.1 us
    all_gather x3, blocking collectives, both(): lax.all_gather(value, 'lane', axis=0, axis_index_groups=groups, tiled=False)  17.6 us
    ppermute x6, starting transfers between devices, passed_along(): lax.ppermute(value, 'blk', [(i, (i + 1) % count) for i in range(count)])  15.1 us
    pallas_call x3, Pallas kernels, gradient(): pl.pallas_call(functools.partial(gradient_kernel, s, spans), out_shape=[p...  3.21 us
    pallas_call x5, Pallas kernels, visit(): pl.pallas_call(functools.partial(visit_kernel, s, *spans[i], scale), out_...  3 us
    pallas_call x1, Pallas kernels, local(): pl.pallas_call(functools.partial(first_kernel, spans, scale), out_shape=[...  1.9 us
  transfers between devices with their start and end apart: 6, of which 6 were waited for; matrix products, arithmetic and copies ran while one was open for 1% of the time, Pallas kernels for 10%

profile of v3, /device:TPU:1, one launch (start us, length us, event | category | flops | bytes accessed | tf_op | source)
XLA Modules:
  0.0 74.5 jit_solution(16619922504546634545)
XLA Ops:
  0.6 1.9 %first_visit.1 = (bf16[256,512]{1,0:T(8,128)(2,1)S(1)}, bf16[256,512]{1,0:T(8,128)(2,1)S(1)}, bf16[512,512]{1,0:T(8,128)(2,1)S(1)}, s32[1,512]{1,0:T(1,128)S(1)}...) custom-call(bf16[1,512,512]{2,1,0:T(8,128)(2,1)} %right_hbm.1, ...), custom_call_target="tpu_custom_call" | custom-call | flops 200000000 | bytes 1000000 | tf_op jit(solution)/shard_map/first_visit/pallas_call | solution.py:175
  2.5 4.0 %collective-permute-start.1 = (bf16[256,512]{1,0:T(8,128)(2,1)S(1)}, bf16[256,512]{1,0:T(8,128)(2,1)S(1)}, u32[]{:S(2)}, u32[]{:S(2)}) collective-permute-start(bf16[256,512]{1,0:T(8,128)(2,1)S(1)} %get-tuple-element.44), channel_id=1, source_target_pairs={{0,4},{4,8},{8,12},{12,16},{16,20},{20,24},{24,28},{28,32},{32,36}... | collective-permute-start | bytes 786440 | tf_op jit(solution)/shard_map/ppermute | solution.py:31
  6.6 0.6 visit.5
  7.2 3.4 %collective-permute-start = (bf16[256,512]{1,0:T(8,128)(2,1)S(1)}, bf16[256,512]{1,0:T(8,128)(2,1)S(1)}, u32[]{:S(2)}, u32[]{:S(2)}) collective-permute-start(bf16[256,512]{1,0:T(8,128)(2,1)S(1)} %get-tuple-element.40), channel_id=1, source_target_pairs={{0,4},{4,8},{8,12},{12,16},{16,20},{20,24},{24,28},{28,32},{32,36}... | collective-permute-start | bytes 786440 | tf_op jit(solution)/shard_map/ppermute | solution.py:31
  10.6 1.1 %gradient.3 = (f32[512,512]{1,0:T(8,128)S(1)}, bf16[256,512]{1,0:T(8,128)(2,1)S(1)}, bf16[256,512]{1,0:T(8,128)(2,1)S(1)}) custom-call(bf16[1,4,512,512]{3,2,1,0:T(8,128)(2,1)} %observed_hbm.7, bf16[256,512]{1,0:T(8,128)(2,1)S(1)} %get-tuple-element.39.prior.refs_0_, bf16[256,512]{1,0:T(8,128)(2,1)S(1)} %get-tuple-element.41.refs_1_, ...), custom_call_target="tpu_custom_call" | custom-call | flops 200000000 | bytes 1000000 | tf_op jit(solution)/shard_map/gradient/pallas_call | solution.py:209
  11.7 12.0 %collective-permute-done.1.right.refs_1_ = bf16[256,512]{1,0:T(8,128)(2,1)S(1)} collective-permute-done((bf16[256,512]{1,0:T(8,128)(2,1)S(1)}, bf16[256,512]{1,0:T(8,128)(2,1)S(1)}, u32[]{:S(2)}, u32[]{:S(2)}) %collective-permute-start.1) | collective-permute-done | bytes 262176 | tf_op jit(solution)/shard_map/ppermute | solution.py:31
  23.7 0.6 visit.6
  24.3 1.9 %collective-permute-start.3 = (bf16[256,512]{1,0:T(8,128)(2,1)S(1)}, bf16[256,512]{1,0:T(8,128)(2,1)S(1)}, u32[]{:S(2)}, u32[]{:S(2)}) collective-permute-start(bf16[256,512]{1,0:T(8,128)(2,1)S(1)} %get-tuple-element.51), channel_id=1, source_target_pairs={{0,4},{4,8},{8,12},{12,16},{16,20},{20,24},{24,28},{28,32},{32,36}... | collective-permute-start | bytes 786440 | tf_op jit(solution)/shard_map/ppermute | solution.py:31
  26.3 3.1 %collective-permute-done.right.refs_3_ = bf16[256,512]{1,0:T(8,128)(2,1)S(1)} collective-permute-done((bf16[256,512]{1,0:T(8,128)(2,1)S(1)}, bf16[256,512]{1,0:T(8,128)(2,1)S(1)}, u32[]{:S(2)}, u32[]{:S(2)}) %collective-permute-start) | collective-permute-done | bytes 262176 | tf_op jit(solution)/shard_map/ppermute | solution.py:31
  29.3 0.6 visit.7
  29.9 1.9 %collective-permute-start.2 = (bf16[256,512]{1,0:T(8,128)(2,1)S(1)}, bf16[256,512]{1,0:T(8,128)(2,1)S(1)}, u32[]{:S(2)}, u32[]{:S(2)}) collective-permute-start(bf16[256,512]{1,0:T(8,128)(2,1)S(1)} %get-tuple-element.47), channel_id=1, source_target_pairs={{0,4},{4,8},{8,12},{12,16},{16,20},{20,24},{24,28},{28,32},{32,36}... | collective-permute-start | bytes 786440 | tf_op jit(solution)/shard_map/ppermute | solution.py:31
  31.9 1.1 %gradient.4 = (f32[512,512]{1,0:T(8,128)S(1)}, bf16[256,512]{1,0:T(8,128)(2,1)S(1)}, bf16[256,512]{1,0:T(8,128)(2,1)S(1)}) custom-call(bf16[1,4,512,512]{3,2,1,0:T(8,128)(2,1)} %observed_hbm.7, bf16[256,512]{1,0:T(8,128)(2,1)S(1)} %get-tuple-element.46.prior.refs_0_, ...), custom_call_target="tpu_custom_call", output_to_operand_aliasing={{0}: (5, {})} | custom-call | flops 200000000 | bytes 1000000 | tf_op jit(solution)/shard_map/gradient/pallas_call | solution.py:209
  32.9 3.2 %collective-permute-done.3.right.refs_1_ = bf16[256,512]{1,0:T(8,128)(2,1)S(1)} collective-permute-done((bf16[256,512]{1,0:T(8,128)(2,1)S(1)}, bf16[256,512]{1,0:T(8,128)(2,1)S(1)}, u32[]{:S(2)}, u32[]{:S(2)}) %collective-permute-start.3) | collective-permute-done | bytes 262176 | tf_op jit(solution)/shard_map/ppermute | solution.py:31
  36.2 0.6 visit.8
  36.8 1.9 %collective-permute-start.5 = (bf16[256,512]{1,0:T(8,128)(2,1)S(1)}, bf16[256,512]{1,0:T(8,128)(2,1)S(1)}, u32[]{:S(2)}, u32[]{:S(2)}) collective-permute-start(bf16[256,512]{1,0:T(8,128)(2,1)S(1)} %get-tuple-element.58), channel_id=1, source_target_pairs={{0,4},{4,8},{8,12},{12,16},{16,20},{20,24},{24,28},{28,32},{32,36}... | collective-permute-start | bytes 786440 | tf_op jit(solution)/shard_map/ppermute | solution.py:31
  38.7 3.9 %collective-permute-done.2.right.refs_3_ = bf16[256,512]{1,0:T(8,128)(2,1)S(1)} collective-permute-done((bf16[256,512]{1,0:T(8,128)(2,1)S(1)}, bf16[256,512]{1,0:T(8,128)(2,1)S(1)}, u32[]{:S(2)}, u32[]{:S(2)}) %collective-permute-start.2) | collective-permute-done | bytes 262176 | tf_op jit(solution)/shard_map/ppermute | solution.py:31
  42.6 0.6 visit.9
  43.2 1.9 %collective-permute-start.4 = (bf16[256,512]{1,0:T(8,128)(2,1)S(1)}, bf16[256,512]{1,0:T(8,128)(2,1)S(1)}, u32[]{:S(2)}, u32[]{:S(2)}) collective-permute-start(bf16[256,512]{1,0:T(8,128)(2,1)S(1)} %get-tuple-element.54), channel_id=1, source_target_pairs={{0,4},{4,8},{8,12},{12,16},{16,20},{20,24},{24,28},{28,32},{32,36}... | collective-permute-start | bytes 786440 | tf_op jit(solution)/shard_map/ppermute | solution.py:31
  45.2 1.1 %gradient.5 = (f32[512,512]{1,0:T(8,128)S(1)}, bf16[256,512]{1,0:T(8,128)(2,1)S(1)}, bf16[256,512]{1,0:T(8,128)(2,1)S(1)}) custom-call(bf16[1,4,512,512]{3,2,1,0:T(8,128)(2,1)} %observed_hbm.7, bf16[256,512]{1,0:T(8,128)(2,1)S(1)} %get-tuple-element.53.prior.refs_0_, ...), custom_call_target="tpu_custom_call", output_to_operand_aliasing={{0}: (5, {})} | custom-call | flops 200000000 | bytes 1000000 | tf_op jit(solution)/shard_map/gradient/pallas_call | solution.py:209
  46.3 1.9 %collective-permute-done.5.right = bf16[256,512]{1,0:T(8,128)(2,1)S(1)} collective-permute-done((bf16[256,512]{1,0:T(8,128)(2,1)S(1)}, bf16[256,512]{1,0:T(8,128)(2,1)S(1)}, u32[]{:S(2)}, u32[]{:S(2)}) %collective-permute-start.5) | collective-permute-done | bytes 262176 | tf_op jit(solution)/shard_map/ppermute | solution.py:31
  48.1 1.3 %settle.1 = (bf16[1,512,512]{2,1,0:T(8,128)(2,1)}, bf16[256,512]{1,0:T(8,128)(2,1)S(1)}) custom-call(bf16[256,512]{1,0:T(8,128)(2,1)S(1)} %collective-permute-done.5.right, bf16[512,512]{1,0:T(8,128)(2,1)S(1)} %get-tuple-element.35.left, bf16[256,512]{1,0:T(8,128)(2,1)S(1)} %get-tuple-element.59.target, ...), custom_call_target="tpu_custom_call", output_to_operand_aliasing={{1}: (2, {})} | custom-call | flops 200000000 | bytes 1000000 | tf_op jit(solution)/shard_map/settle/pallas_call | solution.py:243
  49.4 0.3 fusion
  49.8 0.2 add.3.grad_sum
  50.0 5.0 %collective-permute-done.4.right = bf16[256,512]{1,0:T(8,128)(2,1)S(1)} collective-permute-done((bf16[256,512]{1,0:T(8,128)(2,1)S(1)}, bf16[256,512]{1,0:T(8,128)(2,1)S(1)}, u32[]{:S(2)}, u32[]{:S(2)}) %collective-permute-start.4) | collective-permute-done | bytes 262176 | tf_op jit(solution)/shard_map/ppermute | solution.py:31
  55.0 0.9 %last_visit.1 = (bf16[256,512]{1,0:T(8,128)(2,1)S(1)}, bf16[256,512]{1,0:T(8,128)(2,1)S(1)}, f32[256,512]{1,0:T(8,128)S(1)}) custom-call(bf16[256,512]{1,0:T(8,128)(2,1)S(1)} %collective-permute-done.4.right, bf16[512,512]{1,0:T(8,128)(2,1)S(1)} %get-tuple-element.35.left, bf16[256,512]{1,0:T(8,128)(2,1)S(1)} %get-tuple-element.57.target, ...), custom_call_target="tpu_custom_call" | custom-call | flops 200000000 | bytes 1000000 | tf_op jit(solution)/shard_map/last_visit/pallas_call | solution.py:229
  55.9 4.9 %all-gather = bf16[512,512]{1,0:T(8,128)(2,1)S(1)} all-gather(bf16[256,512]{1,0:T(8,128)(2,1)S(1)} %get-tuple-element.63), channel_id=2, replica_groups={{0,1},{2,3},{4,5},{6,7},{8,9},{10,11},{12,13},{14,15},{16,17},{18,19},{..., dimensions={0}, use_global_device_ids=true | all-gather | bytes 786432 | tf_op jit(solution)/shard_map/all_gather | solution.py:36
  60.8 9.7 %all-gather.1 = bf16[512,512]{1,0:T(8,128)(2,1)S(1)} all-gather(bf16[256,512]{1,0:T(8,128)(2,1)S(1)} %combine.1), channel_id=3, replica_groups={{0,2},{1,3},{4,6},{5,7},{8,10},{9,11},{12,14},{13,15},{16,18},{17,19},{..., dimensions={0}, use_global_device_ids=true | all-gather | bytes 786432 | tf_op jit(solution)/shard_map/all_gather | solution.py:36
  70.5 0.1 renew.1
  70.6 3.0 %all-gather.2.left = bf16[512,512]{1,0:T(8,128)(2,1)S(1)} all-gather(bf16[256,512]{1,0:T(8,128)(2,1)S(1)} %renew.1), channel_id=4, replica_groups={{0,1},{2,3},{4,5},{6,7},{8,9},{10,11},{12,13},{14,15},{16,17},{18,19},{..., dimensions={0}, use_global_device_ids=true | all-gather | bytes 786432 | tf_op jit(solution)/shard_map/all_gather | solution.py:36
  73.6 0.9 %store.1 = (bf16[512,512]{1,0:T(8,128)(2,1)}, bf16[1,512,512]{2,1,0:T(8,128)(2,1)}) custom-call(bf16[512,512]{1,0:T(8,128)(2,1)S(1)} %all-gather.2.left, bf16[256,512]{1,0:T(8,128)(2,1)S(1)} %get-tuple-element.64.part, bf16[1,512,512]{2,1,0:T(8,128)(2,1)} %get-tuple-element.65.right_hbm), custom_call_target="tpu_custom_call", output_to_operand_aliasing={{1}: (2, {})} | custom-call | tf_op jit(solution)/shard_map/store/pallas_call | solution.py:274
  (1 shorter events, 0.0 us)
Async XLA Ops:
  2.5 21.2 %collective-permute-start.1 = (bf16[256,512]{1,0:T(8,128)(2,1)S(1)}, bf16[256,512]{1,0:T(8,128)(2,1)S(1)}, u32[]{:S(2)}, u32[]{:S(2)}) collective-permute-start(bf16[256,512]{1,0:T(8,128)(2,1)S(1)} %get-tuple-element.44), channel_id=1, source_target_pairs={{0,4},{4,8},{8,12},{12,16},{16,20},{20,24},{24,28},{28,32},{32,36}... | collective-permute-start | bytes 786440 | tf_op jit(solution)/shard_map/ppermute | solution.py:31
  7.2 22.1 %collective-permute-start = (bf16[256,512]{1,0:T(8,128)(2,1)S(1)}, bf16[256,512]{1,0:T(8,128)(2,1)S(1)}, u32[]{:S(2)}, u32[]{:S(2)}) collective-permute-start(bf16[256,512]{1,0:T(8,128)(2,1)S(1)} %get-tuple-element.40), channel_id=1, source_target_pairs={{0,4},{4,8},{8,12},{12,16},{16,20},{20,24},{24,28},{28,32},{32,36}... | collective-permute-start | bytes 786440 | tf_op jit(solution)/shard_map/ppermute | solution.py:31
  24.3 11.8 %collective-permute-start.3 = (bf16[256,512]{1,0:T(8,128)(2,1)S(1)}, bf16[256,512]{1,0:T(8,128)(2,1)S(1)}, u32[]{:S(2)}, u32[]{:S(2)}) collective-permute-start(bf16[256,512]{1,0:T(8,128)(2,1)S(1)} %get-tuple-element.51), channel_id=1, source_target_pairs={{0,4},{4,8},{8,12},{12,16},{16,20},{20,24},{24,28},{28,32},{32,36}... | collective-permute-start | bytes 786440 | tf_op jit(solution)/shard_map/ppermute | solution.py:31
  29.9 12.7 %collective-permute-start.2 = (bf16[256,512]{1,0:T(8,128)(2,1)S(1)}, bf16[256,512]{1,0:T(8,128)(2,1)S(1)}, u32[]{:S(2)}, u32[]{:S(2)}) collective-permute-start(bf16[256,512]{1,0:T(8,128)(2,1)S(1)} %get-tuple-element.47), channel_id=1, source_target_pairs={{0,4},{4,8},{8,12},{12,16},{16,20},{20,24},{24,28},{28,32},{32,36}... | collective-permute-start | bytes 786440 | tf_op jit(solution)/shard_map/ppermute | solution.py:31
  36.8 11.3 %collective-permute-start.5 = (bf16[256,512]{1,0:T(8,128)(2,1)S(1)}, bf16[256,512]{1,0:T(8,128)(2,1)S(1)}, u32[]{:S(2)}, u32[]{:S(2)}) collective-permute-start(bf16[256,512]{1,0:T(8,128)(2,1)S(1)} %get-tuple-element.58), channel_id=1, source_target_pairs={{0,4},{4,8},{8,12},{12,16},{16,20},{20,24},{24,28},{28,32},{32,36}... | collective-permute-start | bytes 786440 | tf_op jit(solution)/shard_map/ppermute | solution.py:31
  43.2 11.8 %collective-permute-start.4 = (bf16[256,512]{1,0:T(8,128)(2,1)S(1)}, bf16[256,512]{1,0:T(8,128)(2,1)S(1)}, u32[]{:S(2)}, u32[]{:S(2)}) collective-permute-start(bf16[256,512]{1,0:T(8,128)(2,1)S(1)} %get-tuple-element.54), channel_id=1, source_target_pairs={{0,4},{4,8},{8,12},{12,16},{16,20},{20,24},{24,28},{28,32},{32,36}... | collective-permute-start | bytes 786440 | tf_op jit(solution)/shard_map/ppermute | solution.py:31

commit v4 on v3

--- a/solution.py
+++ b/solution.py
@@ -90,8 +90,10 @@
         c.wait()
 
 
-def visit_kernel(s, a, n, scale, right, left, target, codes, shifts, prior, out, error):
-    predicted = times_transposed(right[...], left[...])
+def visit_kernel(s, a, n, scale, right, left, turned, target, codes, shifts, prior, out, error):
+    predicted = times_transposed(right[...], left[...]) if s == 0 else jnp.dot(
+        right[...], turned[...], preferred_element_type=f32
+    )
     err = errors(predicted, target[...], codes[...], shifts[0:1, s, a : a + n], scale)
     error[...] = err
     out[...] = stepped(right[...], err, left[...], scale)
@@ -117,10 +119,14 @@
         c.wait()
 
 
-def last_kernel(s, a, n, scale, right, left, target, codes, shifts, prior, grad_sum, out, theirs, mine, error):
+def turn_kernel(left, prior, out):
+    out[...] = left[...].T
+
+
+def last_kernel(s, a, n, scale, right, left, turned, target, codes, shifts, prior, grad_sum, out, theirs, mine, error):
     half = left.shape[0] // 2
     core = lax.rem(lax.axis_index("lane"), 2)
-    predicted = times_transposed(right[...], left[...])
+    predicted = jnp.dot(right[...], turned[...], preferred_element_type=f32)
     err = errors(predicted, target[...], codes[...], shifts[0:1, s, a : a + n], scale)
     error[...] = err
     for ref, which in ((theirs, 1 - core), (mine, core)):
@@ -132,8 +138,8 @@
     out[...] = stepped(right[...], err, left[...], scale)
 
 
-def settle_kernel(s, a, n, scale, right, left, target, codes, shifts, prior, right_out, error, fresh, sem):
-    visit_kernel(s, a, n, scale, right, left, target, codes, shifts, prior, fresh, error)
+def settle_kernel(s, a, n, scale, right, left, turned, target, codes, shifts, prior, right_out, error, fresh, sem):
+    visit_kernel(s, a, n, scale, right, left, turned, target, codes, shifts, prior, fresh, error)
     copy = pltpu.make_async_copy(fresh, right_out.at[0, pl.ds(a, n)], sem)
     copy.start()
     copy.wait()
@@ -190,14 +196,15 @@
         return pl.pallas_call(
             functools.partial(visit_kernel, s, *spans[i], scale),
             out_shape=[parts_of[i], tiles[i]],
-            in_specs=[in_vmem] * 6,
+            in_specs=[in_vmem] * 7,
             out_specs=[in_vmem] * 2,
-            input_output_aliases={2: 1},
+            input_output_aliases={3: 1},
             compiler_params=params,
             cost_estimate=price(s),
             name="visit",
-        )(right, left, target, codes, shifts, prior)
-
+        )(right, left, turned[0], target, codes, shifts, prior)
+
+    turned = [left]
     moving, held = [passed_along(after)], [error, loaded[0]]
     for i in range(1, count):
         after, error = visit(0, i, loaded[i], loaded[count + i - 1], error)
@@ -218,6 +225,12 @@
             name="gradient",
         )(observed_hbm, *keep_vmem(*operands))
 
+    turned = keep_vmem(
+        pl.pallas_call(
+            turn_kernel, out_shape=pltpu.VMEM((w, rows), bf16), in_specs=[in_vmem] * 2, out_specs=in_vmem,
+            compiler_params=params, cost_estimate=price(0), name="turn"
+        )(left, *keep_vmem(error))
+    )
     grad_sum, *following = gradient(0, *held)
     parts = [None] * count
     for s in range(1, steps):
@@ -229,13 +242,13 @@
                 parts[i], theirs, mine = pl.pallas_call(
                     functools.partial(last_kernel, s, *spans[i], scale),
                     out_shape=[parts_of[i], pltpu.VMEM((rows // 2, w), bf16), pltpu.VMEM((rows // 2, w), f32)],
-                    in_specs=[in_vmem] * 7,
+                    in_specs=[in_vmem] * 8,
                     out_specs=[in_vmem] * 3,
                     scratch_shapes=[tiles[i]],
                     compiler_params=params,
                     cost_estimate=price(s),
                     name="last_visit",
-                )(right, left, *keep_vmem(following[i]), codes, shifts, *keep_vmem(error), grad_in)
+                )(right, left, turned[0], *keep_vmem(following[i]), codes, shifts, *keep_vmem(error), grad_in)
                 continue
             if s + 1 < steps:
                 parts[i], error = visit(s, i, moving[i], following[i], error)
@@ -243,14 +256,14 @@
                 right_out, error = pl.pallas_call(
                     functools.partial(settle_kernel, s, *spans[i], scale),
                     out_shape=[pltpu.HBM(right_factor.shape, bf16), tiles[i]],
-                    in_specs=[in_vmem] * 6,
+                    in_specs=[in_vmem] * 7,
                     out_specs=[in_hbm, in_vmem],
                     scratch_shapes=[parts_of[i], pltpu.SemaphoreType.DMA],
-                    input_output_aliases={2: 1},
+                    input_output_aliases={3: 1},
                     compiler_params=params,
                     cost_estimate=price(s),
                     name="settle",
-                )(right, left, *keep_vmem(following[i]), codes, shifts, *keep_vmem(error))
+                )(right, left, turned[0], *keep_vmem(following[i]), codes, shifts, *keep_vmem(error))
             held += [error, moving[i]]
             if s + 1 < steps:
                 moving[i] = passed_along(parts[i])

time: 74.9 us -> 74.8 us (level)
  no operation moved by 1% of the time
where the time goes in v4:
time: 74.8 us; the launch traced here: 74.4 us
  waiting for transfers between devices  29 us (39%)
  blocking collectives  17.6 us (24%)
  starting transfers between devices  15.2 us (20%)
  Pallas kernels  11.3 us (15%)
  between operations  0.79 us (1%)
    ppermute x6, waiting for transfers between devices, passed_along(): lax.ppermute(value, 'blk', [(i, (i + 1) % count) for i in range(count)])  29 us
    all_gather x3, blocking collectives, both(): lax.all_gather(value, 'lane', axis=0, axis_index_groups=groups, tiled=False)  17.6 us
    ppermute x6, starting transfers between devices, passed_along(): lax.ppermute(value, 'blk', [(i, (i + 1) % count) for i in range(count)])  15.2 us
    pallas_call x3, Pallas kernels, gradient(): pl.pallas_call(functools.partial(gradient_kernel, s, spans), out_shape=[p...  3.23 us
    pallas_call x5, Pallas kernels, visit(): pl.pallas_call(functools.partial(visit_kernel, s, *spans[i], scale), out_...  2.84 us
    pallas_call x1, Pallas kernels, local(): pl.pallas_call(functools.partial(first_kernel, spans, scale), out_shape=[...  1.9 us
  transfers between devices with their start and end apart: 6, of which 6 were waited for; matrix products, arithmetic and copies ran while one was open for 1% of the time, Pallas kernels for 10%

profile of v4, /device:TPU:1, one launch (start us, length us, event | category | flops | bytes accessed | tf_op | source)
XLA Modules:
  0.0 74.4 jit_solution(5568641822902419188)
XLA Ops:
  0.6 1.9 %first_visit.1 = (bf16[256,512]{1,0:T(8,128)(2,1)S(1)}, bf16[256,512]{1,0:T(8,128)(2,1)S(1)}, bf16[512,512]{1,0:T(8,128)(2,1)S(1)}, s32[1,512]{1,0:T(1,128)S(1)}...) custom-call(bf16[1,512,512]{2,1,0:T(8,128)(2,1)} %right_hbm.1, ...), custom_call_target="tpu_custom_call" | custom-call | flops 200000000 | bytes 1000000 | tf_op jit(solution)/shard_map/first_visit/pallas_call | solution.py:181
  2.5 4.0 %collective-permute-start.1 = (bf16[256,512]{1,0:T(8,128)(2,1)S(1)}, bf16[256,512]{1,0:T(8,128)(2,1)S(1)}, u32[]{:S(2)}, u32[]{:S(2)}) collective-permute-start(bf16[256,512]{1,0:T(8,128)(2,1)S(1)} %get-tuple-element.44), channel_id=1, source_target_pairs={{0,4},{4,8},{8,12},{12,16},{16,20},{20,24},{24,28},{28,32},{32,36}... | collective-permute-start | bytes 786440 | tf_op jit(solution)/shard_map/ppermute | solution.py:31
  6.6 0.6 visit.5
  7.2 3.4 %collective-permute-start = (bf16[256,512]{1,0:T(8,128)(2,1)S(1)}, bf16[256,512]{1,0:T(8,128)(2,1)S(1)}, u32[]{:S(2)}, u32[]{:S(2)}) collective-permute-start(bf16[256,512]{1,0:T(8,128)(2,1)S(1)} %get-tuple-element.40), channel_id=1, source_target_pairs={{0,4},{4,8},{8,12},{12,16},{16,20},{20,24},{24,28},{28,32},{32,36}... | collective-permute-start | bytes 786440 | tf_op jit(solution)/shard_map/ppermute | solution.py:31
  10.6 0.2 turn.1.turned
  10.8 1.1 %gradient.3 = (f32[512,512]{1,0:T(8,128)S(1)}, bf16[256,512]{1,0:T(8,128)(2,1)S(1)}, bf16[256,512]{1,0:T(8,128)(2,1)S(1)}) custom-call(bf16[1,4,512,512]{3,2,1,0:T(8,128)(2,1)} %observed_hbm.7, bf16[256,512]{1,0:T(8,128)(2,1)S(1)} %get-tuple-element.39.prior.refs_0_, bf16[256,512]{1,0:T(8,128)(2,1)S(1)} %get-tuple-element.42.refs_1_, ...), custom_call_target="tpu_custom_call" | custom-call | flops 200000000 | bytes 1000000 | tf_op jit(solution)/shard_map/gradient/pallas_call | solution.py:216
  11.9 11.8 %collective-permute-done.1.right.refs_1_ = bf16[256,512]{1,0:T(8,128)(2,1)S(1)} collective-permute-done((bf16[256,512]{1,0:T(8,128)(2,1)S(1)}, bf16[256,512]{1,0:T(8,128)(2,1)S(1)}, u32[]{:S(2)}, u32[]{:S(2)}) %collective-permute-start.1) | collective-permute-done | bytes 262176 | tf_op jit(solution)/shard_map/ppermute | solution.py:31
  23.7 0.6 visit.6
  24.3 1.9 %collective-permute-start.3 = (bf16[256,512]{1,0:T(8,128)(2,1)S(1)}, bf16[256,512]{1,0:T(8,128)(2,1)S(1)}, u32[]{:S(2)}, u32[]{:S(2)}) collective-permute-start(bf16[256,512]{1,0:T(8,128)(2,1)S(1)} %get-tuple-element.51), channel_id=1, source_target_pairs={{0,4},{4,8},{8,12},{12,16},{16,20},{20,24},{24,28},{28,32},{32,36}... | collective-permute-start | bytes 786440 | tf_op jit(solution)/shard_map/ppermute | solution.py:31
  26.2 3.1 %collective-permute-done.right.refs_3_ = bf16[256,512]{1,0:T(8,128)(2,1)S(1)} collective-permute-done((bf16[256,512]{1,0:T(8,128)(2,1)S(1)}, bf16[256,512]{1,0:T(8,128)(2,1)S(1)}, u32[]{:S(2)}, u32[]{:S(2)}) %collective-permute-start) | collective-permute-done | bytes 262176 | tf_op jit(solution)/shard_map/ppermute | solution.py:31
  29.3 0.6 visit.7
  29.9 1.9 %collective-permute-start.2 = (bf16[256,512]{1,0:T(8,128)(2,1)S(1)}, bf16[256,512]{1,0:T(8,128)(2,1)S(1)}, u32[]{:S(2)}, u32[]{:S(2)}) collective-permute-start(bf16[256,512]{1,0:T(8,128)(2,1)S(1)} %get-tuple-element.47), channel_id=1, source_target_pairs={{0,4},{4,8},{8,12},{12,16},{16,20},{20,24},{24,28},{28,32},{32,36}... | collective-permute-start | bytes 786440 | tf_op jit(solution)/shard_map/ppermute | solution.py:31
  31.8 1.1 %gradient.4 = (f32[512,512]{1,0:T(8,128)S(1)}, bf16[256,512]{1,0:T(8,128)(2,1)S(1)}, bf16[256,512]{1,0:T(8,128)(2,1)S(1)}) custom-call(bf16[1,4,512,512]{3,2,1,0:T(8,128)(2,1)} %observed_hbm.7, bf16[256,512]{1,0:T(8,128)(2,1)S(1)} %get-tuple-element.46.prior.refs_0_, ...), custom_call_target="tpu_custom_call", output_to_operand_aliasing={{0}: (5, {})} | custom-call | flops 200000000 | bytes 1000000 | tf_op jit(solution)/shard_map/gradient/pallas_call | solution.py:216
  32.9 3.2 %collective-permute-done.3.right.refs_1_ = bf16[256,512]{1,0:T(8,128)(2,1)S(1)} collective-permute-done((bf16[256,512]{1,0:T(8,128)(2,1)S(1)}, bf16[256,512]{1,0:T(8,128)(2,1)S(1)}, u32[]{:S(2)}, u32[]{:S(2)}) %collective-permute-start.3) | collective-permute-done | bytes 262176 | tf_op jit(solution)/shard_map/ppermute | solution.py:31
  36.2 0.6 visit.8
  36.7 1.9 %collective-permute-start.5 = (bf16[256,512]{1,0:T(8,128)(2,1)S(1)}, bf16[256,512]{1,0:T(8,128)(2,1)S(1)}, u32[]{:S(2)}, u32[]{:S(2)}) collective-permute-start(bf16[256,512]{1,0:T(8,128)(2,1)S(1)} %get-tuple-element.58), channel_id=1, source_target_pairs={{0,4},{4,8},{8,12},{12,16},{16,20},{20,24},{24,28},{28,32},{32,36}... | collective-permute-start | bytes 786440 | tf_op jit(solution)/shard_map/ppermute | solution.py:31
  38.6 4.0 %collective-permute-done.2.right.refs_3_ = bf16[256,512]{1,0:T(8,128)(2,1)S(1)} collective-permute-done((bf16[256,512]{1,0:T(8,128)(2,1)S(1)}, bf16[256,512]{1,0:T(8,128)(2,1)S(1)}, u32[]{:S(2)}, u32[]{:S(2)}) %collective-permute-start.2) | collective-permute-done | bytes 262176 | tf_op jit(solution)/shard_map/ppermute | solution.py:31
  42.6 0.6 visit.9
  43.2 1.9 %collective-permute-start.4 = (bf16[256,512]{1,0:T(8,128)(2,1)S(1)}, bf16[256,512]{1,0:T(8,128)(2,1)S(1)}, u32[]{:S(2)}, u32[]{:S(2)}) collective-permute-start(bf16[256,512]{1,0:T(8,128)(2,1)S(1)} %get-tuple-element.54), channel_id=1, source_target_pairs={{0,4},{4,8},{8,12},{12,16},{16,20},{20,24},{24,28},{28,32},{32,36}... | collective-permute-start | bytes 786440 | tf_op jit(solution)/shard_map/ppermute | solution.py:31
  45.1 1.1 %gradient.5 = (f32[512,512]{1,0:T(8,128)S(1)}, bf16[256,512]{1,0:T(8,128)(2,1)S(1)}, bf16[256,512]{1,0:T(8,128)(2,1)S(1)}) custom-call(bf16[1,4,512,512]{3,2,1,0:T(8,128)(2,1)} %observed_hbm.7, bf16[256,512]{1,0:T(8,128)(2,1)S(1)} %get-tuple-element.53.prior.refs_0_, ...), custom_call_target="tpu_custom_call", output_to_operand_aliasing={{0}: (5, {})} | custom-call | flops 200000000 | bytes 1000000 | tf_op jit(solution)/shard_map/gradient/pallas_call | solution.py:216
  46.2 1.9 %collective-permute-done.5.right = bf16[256,512]{1,0:T(8,128)(2,1)S(1)} collective-permute-done((bf16[256,512]{1,0:T(8,128)(2,1)S(1)}, bf16[256,512]{1,0:T(8,128)(2,1)S(1)}, u32[]{:S(2)}, u32[]{:S(2)}) %collective-permute-start.5) | collective-permute-done | bytes 262176 | tf_op jit(solution)/shard_map/ppermute | solution.py:31
  48.0 1.3 %settle.1 = (bf16[1,512,512]{2,1,0:T(8,128)(2,1)}, bf16[256,512]{1,0:T(8,128)(2,1)S(1)}) custom-call(bf16[256,512]{1,0:T(8,128)(2,1)S(1)} %collective-permute-done.5.right, bf16[512,512]{1,0:T(8,128)(2,1)S(1)} %get-tuple-element.35.left.turned, bf16[512,512]{1,0:T(8,128)(2,1)S(1)} %turn.1.turned, ...), custom_call_target="tpu_custom_call", output_to_operand_aliasing={{1}: (3, {})} | custom-call | flops 200000000 | bytes 1000000 | tf_op jit(solution)/shard_map/settle/pallas_call | solution.py:256
  49.3 0.3 fusion
  49.7 0.2 add.3.grad_sum
  49.9 5.1 %collective-permute-done.4.right = bf16[256,512]{1,0:T(8,128)(2,1)S(1)} collective-permute-done((bf16[256,512]{1,0:T(8,128)(2,1)S(1)}, bf16[256,512]{1,0:T(8,128)(2,1)S(1)}, u32[]{:S(2)}, u32[]{:S(2)}) %collective-permute-start.4) | collective-permute-done | bytes 262176 | tf_op jit(solution)/shard_map/ppermute | solution.py:31
  54.9 0.8 %last_visit.1 = (bf16[256,512]{1,0:T(8,128)(2,1)S(1)}, bf16[256,512]{1,0:T(8,128)(2,1)S(1)}, f32[256,512]{1,0:T(8,128)S(1)}) custom-call(bf16[256,512]{1,0:T(8,128)(2,1)S(1)} %collective-permute-done.4.right, bf16[512,512]{1,0:T(8,128)(2,1)S(1)} %get-tuple-element.35.left.turned, bf16[512,512]{1,0:T(8,128)(2,1)S(1)} %turn.1.turned, ...), custom_call_target="tpu_custom_call" | custom-call | flops 200000000 | bytes 1000000 | tf_op jit(solution)/shard_map/last_visit/pallas_call | solution.py:242
  55.8 4.9 %all-gather = bf16[512,512]{1,0:T(8,128)(2,1)S(1)} all-gather(bf16[256,512]{1,0:T(8,128)(2,1)S(1)} %get-tuple-element.63), channel_id=2, replica_groups={{0,1},{2,3},{4,5},{6,7},{8,9},{10,11},{12,13},{14,15},{16,17},{18,19},{..., dimensions={0}, use_global_device_ids=true | all-gather | bytes 786432 | tf_op jit(solution)/shard_map/all_gather | solution.py:36
  60.7 9.7 %all-gather.1 = bf16[512,512]{1,0:T(8,128)(2,1)S(1)} all-gather(bf16[256,512]{1,0:T(8,128)(2,1)S(1)} %combine.1), channel_id=3, replica_groups={{0,2},{1,3},{4,6},{5,7},{8,10},{9,11},{12,14},{13,15},{16,18},{17,19},{..., dimensions={0}, use_global_device_ids=true | all-gather | bytes 786432 | tf_op jit(solution)/shard_map/all_gather | solution.py:36
  70.4 0.1 renew.1
  70.5 3.0 %all-gather.2.left = bf16[512,512]{1,0:T(8,128)(2,1)S(1)} all-gather(bf16[256,512]{1,0:T(8,128)(2,1)S(1)} %renew.1), channel_id=4, replica_groups={{0,1},{2,3},{4,5},{6,7},{8,9},{10,11},{12,13},{14,15},{16,17},{18,19},{..., dimensions={0}, use_global_device_ids=true | all-gather | bytes 786432 | tf_op jit(solution)/shard_map/all_gather | solution.py:36
  73.5 0.9 %store.1 = (bf16[512,512]{1,0:T(8,128)(2,1)}, bf16[1,512,512]{2,1,0:T(8,128)(2,1)}) custom-call(bf16[512,512]{1,0:T(8,128)(2,1)S(1)} %all-gather.2.left, bf16[256,512]{1,0:T(8,128)(2,1)S(1)} %get-tuple-element.64.part, bf16[1,512,512]{2,1,0:T(8,128)(2,1)} %get-tuple-element.65.right_hbm), custom_call_target="tpu_custom_call", output_to_operand_aliasing={{1}: (2, {})} | custom-call | tf_op jit(solution)/shard_map/store/pallas_call | solution.py:287
  (1 shorter events, 0.0 us)
Async XLA Ops:
  2.5 21.2 %collective-permute-start.1 = (bf16[256,512]{1,0:T(8,128)(2,1)S(1)}, bf16[256,512]{1,0:T(8,128)(2,1)S(1)}, u32[]{:S(2)}, u32[]{:S(2)}) collective-permute-start(bf16[256,512]{1,0:T(8,128)(2,1)S(1)} %get-tuple-element.44), channel_id=1, source_target_pairs={{0,4},{4,8},{8,12},{12,16},{16,20},{20,24},{24,28},{28,32},{32,36}... | collective-permute-start | bytes 786440 | tf_op jit(solution)/shard_map/ppermute | solution.py:31
  7.2 22.1 %collective-permute-start = (bf16[256,512]{1,0:T(8,128)(2,1)S(1)}, bf16[256,512]{1,0:T(8,128)(2,1)S(1)}, u32[]{:S(2)}, u32[]{:S(2)}) collective-permute-start(bf16[256,512]{1,0:T(8,128)(2,1)S(1)} %get-tuple-element.40), channel_id=1, source_target_pairs={{0,4},{4,8},{8,12},{12,16},{16,20},{20,24},{24,28},{28,32},{32,36}... | collective-permute-start | bytes 786440 | tf_op jit(solution)/shard_map/ppermute | solution.py:31
  24.3 11.9 %collective-permute-start.3 = (bf16[256,512]{1,0:T(8,128)(2,1)S(1)}, bf16[256,512]{1,0:T(8,128)(2,1)S(1)}, u32[]{:S(2)}, u32[]{:S(2)}) collective-permute-start(bf16[256,512]{1,0:T(8,128)(2,1)S(1)} %get-tuple-element.51), channel_id=1, source_target_pairs={{0,4},{4,8},{8,12},{12,16},{16,20},{20,24},{24,28},{28,32},{32,36}... | collective-permute-start | bytes 786440 | tf_op jit(solution)/shard_map/ppermute | solution.py:31
  29.9 12.7 %collective-permute-start.2 = (bf16[256,512]{1,0:T(8,128)(2,1)S(1)}, bf16[256,512]{1,0:T(8,128)(2,1)S(1)}, u32[]{:S(2)}, u32[]{:S(2)}) collective-permute-start(bf16[256,512]{1,0:T(8,128)(2,1)S(1)} %get-tuple-element.47), channel_id=1, source_target_pairs={{0,4},{4,8},{8,12},{12,16},{16,20},{20,24},{24,28},{28,32},{32,36}... | collective-permute-start | bytes 786440 | tf_op jit(solution)/shard_map/ppermute | solution.py:31
  36.7 11.3 %collective-permute-start.5 = (bf16[256,512]{1,0:T(8,128)(2,1)S(1)}, bf16[256,512]{1,0:T(8,128)(2,1)S(1)}, u32[]{:S(2)}, u32[]{:S(2)}) collective-permute-start(bf16[256,512]{1,0:T(8,128)(2,1)S(1)} %get-tuple-element.58), channel_id=1, source_target_pairs={{0,4},{4,8},{8,12},{12,16},{16,20},{20,24},{24,28},{28,32},{32,36}... | collective-permute-start | bytes 786440 | tf_op jit(solution)/shard_map/ppermute | solution.py:31
  43.2 11.8 %collective-permute-start.4 = (bf16[256,512]{1,0:T(8,128)(2,1)S(1)}, bf16[256,512]{1,0:T(8,128)(2,1)S(1)}, u32[]{:S(2)}, u32[]{:S(2)}) collective-permute-start(bf16[256,512]{1,0:T(8,128)(2,1)S(1)} %get-tuple-element.54), channel_id=1, source_target_pairs={{0,4},{4,8},{8,12},{12,16},{16,20},{20,24},{24,28},{28,32},{32,36}... | collective-permute-start | bytes 786440 | tf_op jit(solution)/shard_map/ppermute | solution.py:31

commit v5 on v4

--- a/solution.py
+++ b/solution.py
@@ -123,7 +123,7 @@
     out[...] = left[...].T
 
 
-def last_kernel(s, a, n, scale, right, left, turned, target, codes, shifts, prior, grad_sum, out, theirs, mine, error):
+def last_kernel(s, a, n, scale, right, left, turned, target, codes, shifts, prior, grad_sum, error, theirs, mine):
     half = left.shape[0] // 2
     core = lax.rem(lax.axis_index("lane"), 2)
     predicted = jnp.dot(right[...], turned[...], preferred_element_type=f32)
@@ -135,7 +135,6 @@
             error[:, own], right[...], (((0,), (0,)), ((), ())), preferred_element_type=f32
         )
         ref[...] = (grad_sum[own, :] + term).astype(ref.dtype)
-    out[...] = stepped(right[...], err, left[...], scale)
 
 
 def settle_kernel(s, a, n, scale, right, left, turned, target, codes, shifts, prior, right_out, error, fresh, sem):
@@ -158,11 +157,14 @@
     out[...] = (own - step_left * scale * total).astype(bf16)
 
 
-def store_kernel(first, left, part, right_hbm, left_hbm, right_out, sems):
-    pairs = [(left, left_hbm), (part, right_out.at[0, pl.ds(first, part.shape[0])])]
-    copies = [pltpu.make_async_copy(a, b, sems.at[i]) for i, (a, b) in enumerate(pairs)]
-    for c in copies:
-        c.start()
+def store_kernel(first, scale, new_left, right, error, left, right_hbm, left_hbm, right_out, fresh, sems):
+    copies = [
+        pltpu.make_async_copy(new_left, left_hbm, sems.at[0]),
+        pltpu.make_async_copy(fresh, right_out.at[0, pl.ds(first, fresh.shape[0])], sems.at[1]),
+    ]
+    copies[0].start()
+    fresh[...] = stepped(right[...], error[...], left[...], scale)
+    copies[1].start()
     for c in copies:
         c.wait()
 
@@ -239,12 +241,12 @@
             right, = keep_vmem(moving[i])
             if s + 1 == steps and i + 1 == count:
                 grad_in, = keep_vmem(grad_sum)
-                parts[i], theirs, mine = pl.pallas_call(
+                error, theirs, mine = pl.pallas_call(
                     functools.partial(last_kernel, s, *spans[i], scale),
-                    out_shape=[parts_of[i], pltpu.VMEM((rows // 2, w), bf16), pltpu.VMEM((rows // 2, w), f32)],
+                    out_shape=[tiles[i], pltpu.VMEM((rows // 2, w), bf16), pltpu.VMEM((rows // 2, w), f32)],
                     in_specs=[in_vmem] * 8,
                     out_specs=[in_vmem] * 3,
-                    scratch_shapes=[tiles[i]],
+                    input_output_aliases={3: 0},
                     compiler_params=params,
                     cost_estimate=price(s),
                     name="last_visit",
@@ -285,15 +287,15 @@
     new_left = both(renewed, 1).reshape(rows, w)
     return tuple(
         pl.pallas_call(
-            functools.partial(store_kernel, spans[-1][0]),
+            functools.partial(store_kernel, spans[-1][0], scale),
             out_shape=[jax.ShapeDtypeStruct((rows, w), bf16), jax.ShapeDtypeStruct(right_factor.shape, bf16)],
-            in_specs=[in_vmem] * 2 + [in_hbm],
+            in_specs=[in_vmem] * 4 + [in_hbm],
             out_specs=[in_hbm] * 2,
-            scratch_shapes=[pltpu.SemaphoreType.DMA((2,))],
-            input_output_aliases={2: 1},
+            scratch_shapes=[parts_of[-1], pltpu.SemaphoreType.DMA((2,))],
+            input_output_aliases={4: 1},
             compiler_params=params,
             name="store",
-        )(*keep_vmem(new_left, parts[-1]), *keep_hbm(right_out))
+        )(*keep_vmem(new_left, moving[-1], error), left, *keep_hbm(right_out))
     )
 
 

time: 74.8 us -> 74.7 us (level)
  no operation moved by 1% of the time
where the time goes in v5:
time: 74.7 us; the launch traced here: 74.4 us
  waiting for transfers between devices  29.1 us (39%)
  blocking collectives  17.6 us (24%)
  starting transfers between devices  15.1 us (20%)
  Pallas kernels  11.2 us (15%)
  between operations  0.79 us (1%)
    ppermute x6, waiting for transfers between devices, passed_along(): lax.ppermute(value, 'blk', [(i, (i + 1) % count) for i in range(count)])  29.1 us
    all_gather x3, blocking collectives, both(): lax.all_gather(value, 'lane', axis=0, axis_index_groups=groups, tiled=False)  17.6 us
    ppermute x6, starting transfers between devices, passed_along(): lax.ppermute(value, 'blk', [(i, (i + 1) % count) for i in range(count)])  15.1 us
    pallas_call x3, Pallas kernels, gradient(): pl.pallas_call(functools.partial(gradient_kernel, s, spans), out_shape=[p...  3.22 us
    pallas_call x5, Pallas kernels, visit(): pl.pallas_call(functools.partial(visit_kernel, s, *spans[i], scale), out_...  2.82 us
    pallas_call x1, Pallas kernels, local(): pl.pallas_call(functools.partial(first_kernel, spans, scale), out_shape=[...  1.9 us
  transfers between devices with their start and end apart: 6, of which 6 were waited for; matrix products, arithmetic and copies ran while one was open for 1% of the time, Pallas kernels for 10%

profile of v5, /device:TPU:1, one launch (start us, length us, event | category | flops | bytes accessed | tf_op | source)
XLA Modules:
  0.0 74.4 jit_solution(6411440571022765796)
XLA Ops:
  0.6 1.9 %first_visit.1 = (bf16[256,512]{1,0:T(8,128)(2,1)S(1)}, bf16[256,512]{1,0:T(8,128)(2,1)S(1)}, bf16[512,512]{1,0:T(8,128)(2,1)S(1)}, s32[1,512]{1,0:T(1,128)S(1)}...) custom-call(bf16[1,512,512]{2,1,0:T(8,128)(2,1)} %right_hbm.1, ...), custom_call_target="tpu_custom_call" | custom-call | flops 200000000 | bytes 1000000 | tf_op jit(solution)/shard_map/first_visit/pallas_call | solution.py:183
  2.5 4.0 %collective-permute-start.1 = (bf16[256,512]{1,0:T(8,128)(2,1)S(1)}, bf16[256,512]{1,0:T(8,128)(2,1)S(1)}, u32[]{:S(2)}, u32[]{:S(2)}) collective-permute-start(bf16[256,512]{1,0:T(8,128)(2,1)S(1)} %get-tuple-element.44), channel_id=1, source_target_pairs={{0,4},{4,8},{8,12},{12,16},{16,20},{20,24},{24,28},{28,32},{32,36}... | collective-permute-start | bytes 786440 | tf_op jit(solution)/shard_map/ppermute | solution.py:31
  6.6 0.6 visit.5
  7.2 3.4 %collective-permute-start = (bf16[256,512]{1,0:T(8,128)(2,1)S(1)}, bf16[256,512]{1,0:T(8,128)(2,1)S(1)}, u32[]{:S(2)}, u32[]{:S(2)}) collective-permute-start(bf16[256,512]{1,0:T(8,128)(2,1)S(1)} %get-tuple-element.40), channel_id=1, source_target_pairs={{0,4},{4,8},{8,12},{12,16},{16,20},{20,24},{24,28},{28,32},{32,36}... | collective-permute-start | bytes 786440 | tf_op jit(solution)/shard_map/ppermute | solution.py:31
  10.6 0.2 turn.1.turned
  10.8 1.1 %gradient.3 = (f32[512,512]{1,0:T(8,128)S(1)}, bf16[256,512]{1,0:T(8,128)(2,1)S(1)}, bf16[256,512]{1,0:T(8,128)(2,1)S(1)}) custom-call(bf16[1,4,512,512]{3,2,1,0:T(8,128)(2,1)} %observed_hbm.7, bf16[256,512]{1,0:T(8,128)(2,1)S(1)} %get-tuple-element.39.prior.refs_0_, bf16[256,512]{1,0:T(8,128)(2,1)S(1)} %get-tuple-element.42.refs_1_, ...), custom_call_target="tpu_custom_call" | custom-call | flops 200000000 | bytes 1000000 | tf_op jit(solution)/shard_map/gradient/pallas_call | solution.py:218
  11.9 11.8 %collective-permute-done.1.right.refs_1_ = bf16[256,512]{1,0:T(8,128)(2,1)S(1)} collective-permute-done((bf16[256,512]{1,0:T(8,128)(2,1)S(1)}, bf16[256,512]{1,0:T(8,128)(2,1)S(1)}, u32[]{:S(2)}, u32[]{:S(2)}) %collective-permute-start.1) | collective-permute-done | bytes 262176 | tf_op jit(solution)/shard_map/ppermute | solution.py:31
  23.7 0.6 visit.6
  24.3 1.9 %collective-permute-start.3 = (bf16[256,512]{1,0:T(8,128)(2,1)S(1)}, bf16[256,512]{1,0:T(8,128)(2,1)S(1)}, u32[]{:S(2)}, u32[]{:S(2)}) collective-permute-start(bf16[256,512]{1,0:T(8,128)(2,1)S(1)} %get-tuple-element.51), channel_id=1, source_target_pairs={{0,4},{4,8},{8,12},{12,16},{16,20},{20,24},{24,28},{28,32},{32,36}... | collective-permute-start | bytes 786440 | tf_op jit(solution)/shard_map/ppermute | solution.py:31
  26.2 3.1 %collective-permute-done.right.refs_3_ = bf16[256,512]{1,0:T(8,128)(2,1)S(1)} collective-permute-done((bf16[256,512]{1,0:T(8,128)(2,1)S(1)}, bf16[256,512]{1,0:T(8,128)(2,1)S(1)}, u32[]{:S(2)}, u32[]{:S(2)}) %collective-permute-start) | collective-permute-done | bytes 262176 | tf_op jit(solution)/shard_map/ppermute | solution.py:31
  29.3 0.6 visit.7
  29.9 1.9 %collective-permute-start.2 = (bf16[256,512]{1,0:T(8,128)(2,1)S(1)}, bf16[256,512]{1,0:T(8,128)(2,1)S(1)}, u32[]{:S(2)}, u32[]{:S(2)}) collective-permute-start(bf16[256,512]{1,0:T(8,128)(2,1)S(1)} %get-tuple-element.47), channel_id=1, source_target_pairs={{0,4},{4,8},{8,12},{12,16},{16,20},{20,24},{24,28},{28,32},{32,36}... | collective-permute-start | bytes 786440 | tf_op jit(solution)/shard_map/ppermute | solution.py:31
  31.8 1.1 %gradient.4 = (f32[512,512]{1,0:T(8,128)S(1)}, bf16[256,512]{1,0:T(8,128)(2,1)S(1)}, bf16[256,512]{1,0:T(8,128)(2,1)S(1)}) custom-call(bf16[1,4,512,512]{3,2,1,0:T(8,128)(2,1)} %observed_hbm.7, bf16[256,512]{1,0:T(8,128)(2,1)S(1)} %get-tuple-element.46.prior.refs_0_, ...), custom_call_target="tpu_custom_call", output_to_operand_aliasing={{0}: (5, {})} | custom-call | flops 200000000 | bytes 1000000 | tf_op jit(solution)/shard_map/gradient/pallas_call | solution.py:218
  32.9 3.2 %collective-permute-done.3.right.refs_1_ = bf16[256,512]{1,0:T(8,128)(2,1)S(1)} collective-permute-done((bf16[256,512]{1,0:T(8,128)(2,1)S(1)}, bf16[256,512]{1,0:T(8,128)(2,1)S(1)}, u32[]{:S(2)}, u32[]{:S(2)}) %collective-permute-start.3) | collective-permute-done | bytes 262176 | tf_op jit(solution)/shard_map/ppermute | solution.py:31
  36.1 0.6 visit.8
  36.7 1.9 %collective-permute-start.5 = (bf16[256,512]{1,0:T(8,128)(2,1)S(1)}, bf16[256,512]{1,0:T(8,128)(2,1)S(1)}, u32[]{:S(2)}, u32[]{:S(2)}) collective-permute-start(bf16[256,512]{1,0:T(8,128)(2,1)S(1)} %get-tuple-element.58), channel_id=1, source_target_pairs={{0,4},{4,8},{8,12},{12,16},{16,20},{20,24},{24,28},{28,32},{32,36}... | collective-permute-start | bytes 786440 | tf_op jit(solution)/shard_map/ppermute | solution.py:31
  38.6 4.0 %collective-permute-done.2.right.refs_3_ = bf16[256,512]{1,0:T(8,128)(2,1)S(1)} collective-permute-done((bf16[256,512]{1,0:T(8,128)(2,1)S(1)}, bf16[256,512]{1,0:T(8,128)(2,1)S(1)}, u32[]{:S(2)}, u32[]{:S(2)}) %collective-permute-start.2) | collective-permute-done | bytes 262176 | tf_op jit(solution)/shard_map/ppermute | solution.py:31
  42.6 0.6 visit.9
  43.1 1.9 %collective-permute-start.4 = (bf16[256,512]{1,0:T(8,128)(2,1)S(1)}, bf16[256,512]{1,0:T(8,128)(2,1)S(1)}, u32[]{:S(2)}, u32[]{:S(2)}) collective-permute-start(bf16[256,512]{1,0:T(8,128)(2,1)S(1)} %get-tuple-element.54), channel_id=1, source_target_pairs={{0,4},{4,8},{8,12},{12,16},{16,20},{20,24},{24,28},{28,32},{32,36}... | collective-permute-start | bytes 786440 | tf_op jit(solution)/shard_map/ppermute | solution.py:31
  45.1 1.1 %gradient.5 = (f32[512,512]{1,0:T(8,128)S(1)}, bf16[256,512]{1,0:T(8,128)(2,1)S(1)}, bf16[256,512]{1,0:T(8,128)(2,1)S(1)}) custom-call(bf16[1,4,512,512]{3,2,1,0:T(8,128)(2,1)} %observed_hbm.7, bf16[256,512]{1,0:T(8,128)(2,1)S(1)} %get-tuple-element.53.prior.refs_0_, ...), custom_call_target="tpu_custom_call", output_to_operand_aliasing={{0}: (5, {})} | custom-call | flops 200000000 | bytes 1000000 | tf_op jit(solution)/shard_map/gradient/pallas_call | solution.py:218
  46.2 1.9 %collective-permute-done.5.right = bf16[256,512]{1,0:T(8,128)(2,1)S(1)} collective-permute-done((bf16[256,512]{1,0:T(8,128)(2,1)S(1)}, bf16[256,512]{1,0:T(8,128)(2,1)S(1)}, u32[]{:S(2)}, u32[]{:S(2)}) %collective-permute-start.5) | collective-permute-done | bytes 262176 | tf_op jit(solution)/shard_map/ppermute | solution.py:31
  48.0 1.3 %settle.1 = (bf16[1,512,512]{2,1,0:T(8,128)(2,1)}, bf16[256,512]{1,0:T(8,128)(2,1)S(1)}) custom-call(bf16[256,512]{1,0:T(8,128)(2,1)S(1)} %collective-permute-done.5.right, bf16[512,512]{1,0:T(8,128)(2,1)S(1)} %get-tuple-element.35.left.turned, bf16[512,512]{1,0:T(8,128)(2,1)S(1)} %turn.1.turned, ...), custom_call_target="tpu_custom_call", output_to_operand_aliasing={{1}: (3, {})} | custom-call | flops 200000000 | bytes 1000000 | tf_op jit(solution)/shard_map/settle/pallas_call | solution.py:258
  49.3 0.3 fusion
  49.6 0.2 add.3.grad_sum
  49.8 5.1 %collective-permute-done.4.right = bf16[256,512]{1,0:T(8,128)(2,1)S(1)} collective-permute-done((bf16[256,512]{1,0:T(8,128)(2,1)S(1)}, bf16[256,512]{1,0:T(8,128)(2,1)S(1)}, u32[]{:S(2)}, u32[]{:S(2)}) %collective-permute-start.4) | collective-permute-done | bytes 262176 | tf_op jit(solution)/shard_map/ppermute | solution.py:31
  54.9 0.7 last_visit.1
  55.6 4.9 %all-gather = bf16[512,512]{1,0:T(8,128)(2,1)S(1)} all-gather(bf16[256,512]{1,0:T(8,128)(2,1)S(1)} %get-tuple-element.63), channel_id=2, replica_groups={{0,1},{2,3},{4,5},{6,7},{8,9},{10,11},{12,13},{14,15},{16,17},{18,19},{..., dimensions={0}, use_global_device_ids=true | all-gather | bytes 786432 | tf_op jit(solution)/shard_map/all_gather | solution.py:36
  60.5 9.7 %all-gather.1 = bf16[512,512]{1,0:T(8,128)(2,1)S(1)} all-gather(bf16[256,512]{1,0:T(8,128)(2,1)S(1)} %combine.1), channel_id=3, replica_groups={{0,2},{1,3},{4,6},{5,7},{8,10},{9,11},{12,14},{13,15},{16,18},{17,19},{..., dimensions={0}, use_global_device_ids=true | all-gather | bytes 786432 | tf_op jit(solution)/shard_map/all_gather | solution.py:36
  70.2 0.1 renew.1
  70.3 3.0 %all-gather.2.new_left = bf16[512,512]{1,0:T(8,128)(2,1)S(1)} all-gather(bf16[256,512]{1,0:T(8,128)(2,1)S(1)} %renew.1), channel_id=4, replica_groups={{0,1},{2,3},{4,5},{6,7},{8,9},{10,11},{12,13},{14,15},{16,17},{18,19},{..., dimensions={0}, use_global_device_ids=true | all-gather | bytes 786432 | tf_op jit(solution)/shard_map/all_gather | solution.py:36
  73.3 1.0 %store.1 = (bf16[512,512]{1,0:T(8,128)(2,1)}, bf16[1,512,512]{2,1,0:T(8,128)(2,1)}) custom-call(bf16[512,512]{1,0:T(8,128)(2,1)S(1)} %all-gather.2.new_left, bf16[256,512]{1,0:T(8,128)(2,1)S(1)} %collective-permute-done.4.right, bf16[256,512]{1,0:T(8,128)(2,1)S(1)} %get-tuple-element.64.error, ...), custom_call_target="tpu_custom_call", output_to_operand_aliasing={{1}: (4, {})} | custom-call | tf_op jit(solution)/shard_map/store/pallas_call | solution.py:289
  (1 shorter events, 0.0 us)
Async XLA Ops:
  2.5 21.2 %collective-permute-start.1 = (bf16[256,512]{1,0:T(8,128)(2,1)S(1)}, bf16[256,512]{1,0:T(8,128)(2,1)S(1)}, u32[]{:S(2)}, u32[]{:S(2)}) collective-permute-start(bf16[256,512]{1,0:T(8,128)(2,1)S(1)} %get-tuple-element.44), channel_id=1, source_target_pairs={{0,4},{4,8},{8,12},{12,16},{16,20},{20,24},{24,28},{28,32},{32,36}... | collective-permute-start | bytes 786440 | tf_op jit(solution)/shard_map/ppermute | solution.py:31
  7.2 22.1 %collective-permute-start = (bf16[256,512]{1,0:T(8,128)(2,1)S(1)}, bf16[256,512]{1,0:T(8,128)(2,1)S(1)}, u32[]{:S(2)}, u32[]{:S(2)}) collective-permute-start(bf16[256,512]{1,0:T(8,128)(2,1)S(1)} %get-tuple-element.40), channel_id=1, source_target_pairs={{0,4},{4,8},{8,12},{12,16},{16,20},{20,24},{24,28},{28,32},{32,36}... | collective-permute-start | bytes 786440 | tf_op jit(solution)/shard_map/ppermute | solution.py:31
  24.3 11.9 %collective-permute-start.3 = (bf16[256,512]{1,0:T(8,128)(2,1)S(1)}, bf16[256,512]{1,0:T(8,128)(2,1)S(1)}, u32[]{:S(2)}, u32[]{:S(2)}) collective-permute-start(bf16[256,512]{1,0:T(8,128)(2,1)S(1)} %get-tuple-element.51), channel_id=1, source_target_pairs={{0,4},{4,8},{8,12},{12,16},{16,20},{20,24},{24,28},{28,32},{32,36}... | collective-permute-start | bytes 786440 | tf_op jit(solution)/shard_map/ppermute | solution.py:31
  29.9 12.7 %collective-permute-start.2 = (bf16[256,512]{1,0:T(8,128)(2,1)S(1)}, bf16[256,512]{1,0:T(8,128)(2,1)S(1)}, u32[]{:S(2)}, u32[]{:S(2)}) collective-permute-start(bf16[256,512]{1,0:T(8,128)(2,1)S(1)} %get-tuple-element.47), channel_id=1, source_target_pairs={{0,4},{4,8},{8,12},{12,16},{16,20},{20,24},{24,28},{28,32},{32,36}... | collective-permute-start | bytes 786440 | tf_op jit(solution)/shard_map/ppermute | solution.py:31
  36.7 11.3 %collective-permute-start.5 = (bf16[256,512]{1,0:T(8,128)(2,1)S(1)}, bf16[256,512]{1,0:T(8,128)(2,1)S(1)}, u32[]{:S(2)}, u32[]{:S(2)}) collective-permute-start(bf16[256,512]{1,0:T(8,128)(2,1)S(1)} %get-tuple-element.58), channel_id=1, source_target_pairs={{0,4},{4,8},{8,12},{12,16},{16,20},{20,24},{24,28},{28,32},{32,36}... | collective-permute-start | bytes 786440 | tf_op jit(solution)/shard_map/ppermute | solution.py:31
  43.1 11.8 %collective-permute-start.4 = (bf16[256,512]{1,0:T(8,128)(2,1)S(1)}, bf16[256,512]{1,0:T(8,128)(2,1)S(1)}, u32[]{:S(2)}, u32[]{:S(2)}) collective-permute-start(bf16[256,512]{1,0:T(8,128)(2,1)S(1)} %get-tuple-element.54), channel_id=1, source_target_pairs={{0,4},{4,8},{8,12},{12,16},{16,20},{20,24},{24,28},{28,32},{32,36}... | collective-permute-start | bytes 786440 | tf_op jit(solution)/shard_map/ppermute | solution.py:31

commit v6 on v4

--- a/solution.py
+++ b/solution.py
@@ -206,8 +206,14 @@
 
     turned = [left]
     moving, held = [passed_along(after)], [error, loaded[0]]
+    turned = keep_vmem(
+        pl.pallas_call(
+            turn_kernel, out_shape=pltpu.VMEM((w, rows), bf16), in_specs=[in_vmem] * 2, out_specs=in_vmem,
+            compiler_params=params, cost_estimate=price(0), name="turn"
+        )(left, *keep_vmem(error))
+    )
     for i in range(1, count):
-        after, error = visit(0, i, loaded[i], loaded[count + i - 1], error)
+        after, error = visit(0, i, loaded[i], loaded[count + i - 1], turned[0])
         moving.append(passed_along(after))
         held += [error, loaded[i]]
 
@@ -225,12 +231,6 @@
             name="gradient",
         )(observed_hbm, *keep_vmem(*operands))
 
-    turned = keep_vmem(
-        pl.pallas_call(
-            turn_kernel, out_shape=pltpu.VMEM((w, rows), bf16), in_specs=[in_vmem] * 2, out_specs=in_vmem,
-            compiler_params=params, cost_estimate=price(0), name="turn"
-        )(left, *keep_vmem(error))
-    )
     grad_sum, *following = gradient(0, *held)
     parts = [None] * count
     for s in range(1, steps):

time: 74.8 us -> 74.8 us (level)
  no operation moved by 1% of the time
where the time goes in v6:
time: 74.8 us; the launch traced here: 74.4 us
  waiting for transfers between devices  29.1 us (39%)
  blocking collectives  17.6 us (24%)
  starting transfers between devices  15.2 us (20%)
  Pallas kernels  11.3 us (15%)
  between operations  0.79 us (1%)
    ppermute x6, waiting for transfers between devices, passed_along(): lax.ppermute(value, 'blk', [(i, (i + 1) % count) for i in range(count)])  29.1 us
    all_gather x3, blocking collectives, both(): lax.all_gather(value, 'lane', axis=0, axis_index_groups=groups, tiled=False)  17.6 us
    ppermute x6, starting transfers between devices, passed_along(): lax.ppermute(value, 'blk', [(i, (i + 1) % count) for i in range(count)])  15.2 us
    pallas_call x3, Pallas kernels, gradient(): pl.pallas_call(functools.partial(gradient_kernel, s, spans), out_shape=[p...  3.2 us
    pallas_call x5, Pallas kernels, visit(): pl.pallas_call(functools.partial(visit_kernel, s, *spans[i], scale), out_...  2.83 us
    pallas_call x1, Pallas kernels, local(): pl.pallas_call(functools.partial(first_kernel, spans, scale), out_shape=[...  1.9 us
  transfers between devices with their start and end apart: 6, of which 6 were waited for; matrix products, arithmetic and copies ran while one was open for 1% of the time, Pallas kernels for 10%

profile of v6, /device:TPU:1, one launch (start us, length us, event | category | flops | bytes accessed | tf_op | source)
XLA Modules:
  0.0 74.4 jit_solution(5349777552580368326)
XLA Ops:
  0.6 1.9 %first_visit.1 = (bf16[256,512]{1,0:T(8,128)(2,1)S(1)}, bf16[256,512]{1,0:T(8,128)(2,1)S(1)}, bf16[512,512]{1,0:T(8,128)(2,1)S(1)}, s32[1,512]{1,0:T(1,128)S(1)}...) custom-call(bf16[1,512,512]{2,1,0:T(8,128)(2,1)} %right_hbm.1, ...), custom_call_target="tpu_custom_call" | custom-call | flops 200000000 | bytes 1000000 | tf_op jit(solution)/shard_map/first_visit/pallas_call | solution.py:181
  2.5 4.0 %collective-permute-start.1 = (bf16[256,512]{1,0:T(8,128)(2,1)S(1)}, bf16[256,512]{1,0:T(8,128)(2,1)S(1)}, u32[]{:S(2)}, u32[]{:S(2)}) collective-permute-start(bf16[256,512]{1,0:T(8,128)(2,1)S(1)} %get-tuple-element.44), channel_id=1, source_target_pairs={{0,4},{4,8},{8,12},{12,16},{16,20},{20,24},{24,28},{28,32},{32,36}... | collective-permute-start | bytes 786440 | tf_op jit(solution)/shard_map/ppermute | solution.py:31
  6.6 0.2 turn.1.turned.prior
  6.8 0.6 visit.5
  7.4 3.4 %collective-permute-start = (bf16[256,512]{1,0:T(8,128)(2,1)S(1)}, bf16[256,512]{1,0:T(8,128)(2,1)S(1)}, u32[]{:S(2)}, u32[]{:S(2)}) collective-permute-start(bf16[256,512]{1,0:T(8,128)(2,1)S(1)} %get-tuple-element.40), channel_id=1, source_target_pairs={{0,4},{4,8},{8,12},{12,16},{16,20},{20,24},{24,28},{28,32},{32,36}... | collective-permute-start | bytes 786440 | tf_op jit(solution)/shard_map/ppermute | solution.py:31
  10.8 1.1 %gradient.3 = (f32[512,512]{1,0:T(8,128)S(1)}, bf16[256,512]{1,0:T(8,128)(2,1)S(1)}, bf16[256,512]{1,0:T(8,128)(2,1)S(1)}) custom-call(bf16[1,4,512,512]{3,2,1,0:T(8,128)(2,1)} %observed_hbm.7, bf16[256,512]{1,0:T(8,128)(2,1)S(1)} %get-tuple-element.36.prior.refs_0_, bf16[256,512]{1,0:T(8,128)(2,1)S(1)} %get-tuple-element.41.refs_1_, ...), custom_call_target="tpu_custom_call" | custom-call | flops 200000000 | bytes 1000000 | tf_op jit(solution)/shard_map/gradient/pallas_call | solution.py:222
  11.9 11.8 %collective-permute-done.1.right.refs_1_ = bf16[256,512]{1,0:T(8,128)(2,1)S(1)} collective-permute-done((bf16[256,512]{1,0:T(8,128)(2,1)S(1)}, bf16[256,512]{1,0:T(8,128)(2,1)S(1)}, u32[]{:S(2)}, u32[]{:S(2)}) %collective-permute-start.1) | collective-permute-done | bytes 262176 | tf_op jit(solution)/shard_map/ppermute | solution.py:31
  23.7 0.6 visit.6
  24.3 1.9 %collective-permute-start.3 = (bf16[256,512]{1,0:T(8,128)(2,1)S(1)}, bf16[256,512]{1,0:T(8,128)(2,1)S(1)}, u32[]{:S(2)}, u32[]{:S(2)}) collective-permute-start(bf16[256,512]{1,0:T(8,128)(2,1)S(1)} %get-tuple-element.51), channel_id=1, source_target_pairs={{0,4},{4,8},{8,12},{12,16},{16,20},{20,24},{24,28},{28,32},{32,36}... | collective-permute-start | bytes 786440 | tf_op jit(solution)/shard_map/ppermute | solution.py:31
  26.2 3.1 %collective-permute-done.right.refs_3_ = bf16[256,512]{1,0:T(8,128)(2,1)S(1)} collective-permute-done((bf16[256,512]{1,0:T(8,128)(2,1)S(1)}, bf16[256,512]{1,0:T(8,128)(2,1)S(1)}, u32[]{:S(2)}, u32[]{:S(2)}) %collective-permute-start) | collective-permute-done | bytes 262176 | tf_op jit(solution)/shard_map/ppermute | solution.py:31
  29.3 0.6 visit.7
  29.9 1.9 %collective-permute-start.2 = (bf16[256,512]{1,0:T(8,128)(2,1)S(1)}, bf16[256,512]{1,0:T(8,128)(2,1)S(1)}, u32[]{:S(2)}, u32[]{:S(2)}) collective-permute-start(bf16[256,512]{1,0:T(8,128)(2,1)S(1)} %get-tuple-element.47), channel_id=1, source_target_pairs={{0,4},{4,8},{8,12},{12,16},{16,20},{20,24},{24,28},{28,32},{32,36}... | collective-permute-start | bytes 786440 | tf_op jit(solution)/shard_map/ppermute | solution.py:31
  31.8 1.1 %gradient.4 = (f32[512,512]{1,0:T(8,128)S(1)}, bf16[256,512]{1,0:T(8,128)(2,1)S(1)}, bf16[256,512]{1,0:T(8,128)(2,1)S(1)}) custom-call(bf16[1,4,512,512]{3,2,1,0:T(8,128)(2,1)} %observed_hbm.7, bf16[256,512]{1,0:T(8,128)(2,1)S(1)} %get-tuple-element.46.prior.refs_0_, ...), custom_call_target="tpu_custom_call", output_to_operand_aliasing={{0}: (5, {})} | custom-call | flops 200000000 | bytes 1000000 | tf_op jit(solution)/shard_map/gradient/pallas_call | solution.py:222
  32.9 3.2 %collective-permute-done.3.right.refs_1_ = bf16[256,512]{1,0:T(8,128)(2,1)S(1)} collective-permute-done((bf16[256,512]{1,0:T(8,128)(2,1)S(1)}, bf16[256,512]{1,0:T(8,128)(2,1)S(1)}, u32[]{:S(2)}, u32[]{:S(2)}) %collective-permute-start.3) | collective-permute-done | bytes 262176 | tf_op jit(solution)/shard_map/ppermute | solution.py:31
  36.1 0.6 visit.8
  36.7 1.9 %collective-permute-start.5 = (bf16[256,512]{1,0:T(8,128)(2,1)S(1)}, bf16[256,512]{1,0:T(8,128)(2,1)S(1)}, u32[]{:S(2)}, u32[]{:S(2)}) collective-permute-start(bf16[256,512]{1,0:T(8,128)(2,1)S(1)} %get-tuple-element.58), channel_id=1, source_target_pairs={{0,4},{4,8},{8,12},{12,16},{16,20},{20,24},{24,28},{28,32},{32,36}... | collective-permute-start | bytes 786440 | tf_op jit(solution)/shard_map/ppermute | solution.py:31
  38.6 4.0 %collective-permute-done.2.right.refs_3_ = bf16[256,512]{1,0:T(8,128)(2,1)S(1)} collective-permute-done((bf16[256,512]{1,0:T(8,128)(2,1)S(1)}, bf16[256,512]{1,0:T(8,128)(2,1)S(1)}, u32[]{:S(2)}, u32[]{:S(2)}) %collective-permute-start.2) | collective-permute-done | bytes 262176 | tf_op jit(solution)/shard_map/ppermute | solution.py:31
  42.6 0.6 visit.9
  43.2 1.9 %collective-permute-start.4 = (bf16[256,512]{1,0:T(8,128)(2,1)S(1)}, bf16[256,512]{1,0:T(8,128)(2,1)S(1)}, u32[]{:S(2)}, u32[]{:S(2)}) collective-permute-start(bf16[256,512]{1,0:T(8,128)(2,1)S(1)} %get-tuple-element.54), channel_id=1, source_target_pairs={{0,4},{4,8},{8,12},{12,16},{16,20},{20,24},{24,28},{28,32},{32,36}... | collective-permute-start | bytes 786440 | tf_op jit(solution)/shard_map/ppermute | solution.py:31
  45.1 1.1 %gradient.5 = (f32[512,512]{1,0:T(8,128)S(1)}, bf16[256,512]{1,0:T(8,128)(2,1)S(1)}, bf16[256,512]{1,0:T(8,128)(2,1)S(1)}) custom-call(bf16[1,4,512,512]{3,2,1,0:T(8,128)(2,1)} %observed_hbm.7, bf16[256,512]{1,0:T(8,128)(2,1)S(1)} %get-tuple-element.53.prior.refs_0_, ...), custom_call_target="tpu_custom_call", output_to_operand_aliasing={{0}: (5, {})} | custom-call | flops 200000000 | bytes 1000000 | tf_op jit(solution)/shard_map/gradient/pallas_call | solution.py:222
  46.2 1.9 %collective-permute-done.5.right = bf16[256,512]{1,0:T(8,128)(2,1)S(1)} collective-permute-done((bf16[256,512]{1,0:T(8,128)(2,1)S(1)}, bf16[256,512]{1,0:T(8,128)(2,1)S(1)}, u32[]{:S(2)}, u32[]{:S(2)}) %collective-permute-start.5) | collective-permute-done | bytes 262176 | tf_op jit(solution)/shard_map/ppermute | solution.py:31
  48.0 1.3 %settle.1 = (bf16[1,512,512]{2,1,0:T(8,128)(2,1)}, bf16[256,512]{1,0:T(8,128)(2,1)S(1)}) custom-call(bf16[256,512]{1,0:T(8,128)(2,1)S(1)} %collective-permute-done.5.right, bf16[512,512]{1,0:T(8,128)(2,1)S(1)} %get-tuple-element.35.left, bf16[512,512]{1,0:T(8,128)(2,1)S(1)} %turn.1.turned.prior, ...), custom_call_target="tpu_custom_call", output_to_operand_aliasing={{1}: (3, {})} | custom-call | flops 200000000 | bytes 1000000 | tf_op jit(solution)/shard_map/settle/pallas_call | solution.py:256
  49.3 0.3 fusion
  49.6 0.2 add.3.grad_sum
  49.9 5.1 %collective-permute-done.4.right = bf16[256,512]{1,0:T(8,128)(2,1)S(1)} collective-permute-done((bf16[256,512]{1,0:T(8,128)(2,1)S(1)}, bf16[256,512]{1,0:T(8,128)(2,1)S(1)}, u32[]{:S(2)}, u32[]{:S(2)}) %collective-permute-start.4) | collective-permute-done | bytes 262176 | tf_op jit(solution)/shard_map/ppermute | solution.py:31
  54.9 0.8 %last_visit.1 = (bf16[256,512]{1,0:T(8,128)(2,1)S(1)}, bf16[256,512]{1,0:T(8,128)(2,1)S(1)}, f32[256,512]{1,0:T(8,128)S(1)}) custom-call(bf16[256,512]{1,0:T(8,128)(2,1)S(1)} %collective-permute-done.4.right, bf16[512,512]{1,0:T(8,128)(2,1)S(1)} %get-tuple-element.35.left, bf16[512,512]{1,0:T(8,128)(2,1)S(1)} %turn.1.turned.prior, ...), custom_call_target="tpu_custom_call" | custom-call | flops 200000000 | bytes 1000000 | tf_op jit(solution)/shard_map/last_visit/pallas_call | solution.py:242
  55.8 4.9 %all-gather = bf16[512,512]{1,0:T(8,128)(2,1)S(1)} all-gather(bf16[256,512]{1,0:T(8,128)(2,1)S(1)} %get-tuple-element.63), channel_id=2, replica_groups={{0,1},{2,3},{4,5},{6,7},{8,9},{10,11},{12,13},{14,15},{16,17},{18,19},{..., dimensions={0}, use_global_device_ids=true | all-gather | bytes 786432 | tf_op jit(solution)/shard_map/all_gather | solution.py:36
  60.7 9.7 %all-gather.1 = bf16[512,512]{1,0:T(8,128)(2,1)S(1)} all-gather(bf16[256,512]{1,0:T(8,128)(2,1)S(1)} %combine.1), channel_id=3, replica_groups={{0,2},{1,3},{4,6},{5,7},{8,10},{9,11},{12,14},{13,15},{16,18},{17,19},{..., dimensions={0}, use_global_device_ids=true | all-gather | bytes 786432 | tf_op jit(solution)/shard_map/all_gather | solution.py:36
  70.4 0.1 renew.1
  70.5 3.0 %all-gather.2.left = bf16[512,512]{1,0:T(8,128)(2,1)S(1)} all-gather(bf16[256,512]{1,0:T(8,128)(2,1)S(1)} %renew.1), channel_id=4, replica_groups={{0,1},{2,3},{4,5},{6,7},{8,9},{10,11},{12,13},{14,15},{16,17},{18,19},{..., dimensions={0}, use_global_device_ids=true | all-gather | bytes 786432 | tf_op jit(solution)/shard_map/all_gather | solution.py:36
  73.5 0.9 %store.1 = (bf16[512,512]{1,0:T(8,128)(2,1)}, bf16[1,512,512]{2,1,0:T(8,128)(2,1)}) custom-call(bf16[512,512]{1,0:T(8,128)(2,1)S(1)} %all-gather.2.left, bf16[256,512]{1,0:T(8,128)(2,1)S(1)} %get-tuple-element.64.part, bf16[1,512,512]{2,1,0:T(8,128)(2,1)} %get-tuple-element.65.right_hbm), custom_call_target="tpu_custom_call", output_to_operand_aliasing={{1}: (2, {})} | custom-call | tf_op jit(solution)/shard_map/store/pallas_call | solution.py:287
  (1 shorter events, 0.0 us)
Async XLA Ops:
  2.5 21.2 %collective-permute-start.1 = (bf16[256,512]{1,0:T(8,128)(2,1)S(1)}, bf16[256,512]{1,0:T(8,128)(2,1)S(1)}, u32[]{:S(2)}, u32[]{:S(2)}) collective-permute-start(bf16[256,512]{1,0:T(8,128)(2,1)S(1)} %get-tuple-element.44), channel_id=1, source_target_pairs={{0,4},{4,8},{8,12},{12,16},{16,20},{20,24},{24,28},{28,32},{32,36}... | collective-permute-start | bytes 786440 | tf_op jit(solution)/shard_map/ppermute | solution.py:31
  7.4 22.0 %collective-permute-start = (bf16[256,512]{1,0:T(8,128)(2,1)S(1)}, bf16[256,512]{1,0:T(8,128)(2,1)S(1)}, u32[]{:S(2)}, u32[]{:S(2)}) collective-permute-start(bf16[256,512]{1,0:T(8,128)(2,1)S(1)} %get-tuple-element.40), channel_id=1, source_target_pairs={{0,4},{4,8},{8,12},{12,16},{16,20},{20,24},{24,28},{28,32},{32,36}... | collective-permute-start | bytes 786440 | tf_op jit(solution)/shard_map/ppermute | solution.py:31
  24.3 11.9 %collective-permute-start.3 = (bf16[256,512]{1,0:T(8,128)(2,1)S(1)}, bf16[256,512]{1,0:T(8,128)(2,1)S(1)}, u32[]{:S(2)}, u32[]{:S(2)}) collective-permute-start(bf16[256,512]{1,0:T(8,128)(2,1)S(1)} %get-tuple-element.51), channel_id=1, source_target_pairs={{0,4},{4,8},{8,12},{12,16},{16,20},{20,24},{24,28},{28,32},{32,36}... | collective-permute-start | bytes 786440 | tf_op jit(solution)/shard_map/ppermute | solution.py:31
  29.9 12.7 %collective-permute-start.2 = (bf16[256,512]{1,0:T(8,128)(2,1)S(1)}, bf16[256,512]{1,0:T(8,128)(2,1)S(1)}, u32[]{:S(2)}, u32[]{:S(2)}) collective-permute-start(bf16[256,512]{1,0:T(8,128)(2,1)S(1)} %get-tuple-element.47), channel_id=1, source_target_pairs={{0,4},{4,8},{8,12},{12,16},{16,20},{20,24},{24,28},{28,32},{32,36}... | collective-permute-start | bytes 786440 | tf_op jit(solution)/shard_map/ppermute | solution.py:31
  36.7 11.3 %collective-permute-start.5 = (bf16[256,512]{1,0:T(8,128)(2,1)S(1)}, bf16[256,512]{1,0:T(8,128)(2,1)S(1)}, u32[]{:S(2)}, u32[]{:S(2)}) collective-permute-start(bf16[256,512]{1,0:T(8,128)(2,1)S(1)} %get-tuple-element.58), channel_id=1, source_target_pairs={{0,4},{4,8},{8,12},{12,16},{16,20},{20,24},{24,28},{28,32},{32,36}... | collective-permute-start | bytes 786440 | tf_op jit(solution)/shard_map/ppermute | solution.py:31
  43.2 11.8 %collective-permute-start.4 = (bf16[256,512]{1,0:T(8,128)(2,1)S(1)}, bf16[256,512]{1,0:T(8,128)(2,1)S(1)}, u32[]{:S(2)}, u32[]{:S(2)}) collective-permute-start(bf16[256,512]{1,0:T(8,128)(2,1)S(1)} %get-tuple-element.54), channel_id=1, source_target_pairs={{0,4},{4,8},{8,12},{12,16},{16,20},{20,24},{24,28},{28,32},{32,36}... | collective-permute-start | bytes 786440 | tf_op jit(solution)/shard_map/ppermute | solution.py:31

commit v7 on v3

--- a/solution.py
+++ b/solution.py
@@ -64,12 +64,14 @@
 def first_kernel(spans, scale, right_hbm, left_hbm, observed_hbm, codes_hbm, shifts_hbm, out, error, left, codes, shifts, *refs):
     count = len(spans)
     rights, others, target, sems = refs[:count], refs[count : 2 * count - 1], refs[-2], refs[-1]
+    half = left.shape[0] // 2
     pairs = [
         (right_hbm.at[0, pl.ds(*spans[0])], rights[0]),
-        (left_hbm, left),
+        (left_hbm.at[pl.ds(0, half)], left.at[pl.ds(0, half)]),
         (observed_hbm.at[0, 0, pl.ds(*spans[0])], target),
         (codes_hbm, codes),
         (shifts_hbm, shifts),
+        (left_hbm.at[pl.ds(half, half)], left.at[pl.ds(half, half)]),
     ]
     for i in range(1, count):
         pairs.append((right_hbm.at[0, pl.ds(*spans[i])], rights[i]))
@@ -77,16 +79,21 @@
     copies = [pltpu.make_async_copy(a, b, sems.at[i]) for i, (a, b) in enumerate(pairs)]
     for c in copies:
         c.start()
-    for c in copies[:2]:
-        c.wait()
-    right = rights[0][...]
-    predicted = times_transposed(right, left[...])
-    for c in copies[2:5]:
-        c.wait()
-    err = errors(predicted, target[...], codes[...], shifts[0:1, 0, 0 : spans[0][1]], scale)
-    error[...] = err
-    out[...] = stepped(right, err, left[...], scale)
-    for c in copies[5:]:
+    grad = None
+    copies[0].wait()
+    for i in range(2):
+        own = slice(i * half, (i + 1) * half)
+        copies[1 + 4 * i].wait()
+        predicted = times_transposed(rights[0][...], left[own, :])
+        if i == 0:
+            for c in copies[2:5]:
+                c.wait()
+        err = errors(predicted, target[:, own], codes[:, own], shifts[0:1, 0, 0 : spans[0][1]], scale)
+        error[:, own] = err
+        term = jnp.dot(err, left[own, :], preferred_element_type=f32)
+        grad = term if grad is None else grad + term
+    out[...] = (rights[0][...].astype(f32) - step_right * scale * grad).astype(bf16)
+    for c in copies[6:]:
         c.wait()
 
 
@@ -178,7 +185,7 @@
                    pltpu.VMEM(shift_codes.shape, jnp.int32), *parts_of, *tiles[1:]],
         in_specs=[in_hbm] * 5,
         out_specs=[in_vmem] * (2 * count + 4),
-        scratch_shapes=[tiles[0], pltpu.SemaphoreType.DMA((2 * count + 3,))],
+        scratch_shapes=[tiles[0], pltpu.SemaphoreType.DMA((2 * count + 4,))],
         compiler_params=params,
         cost_estimate=price(0),
         name="first_visit",

time: 74.9 us -> 75.1 us (level)
  no operation moved by 1% of the time
where the time goes in v7:
time: 75.1 us; the launch traced here: 74.7 us
  waiting for transfers between devices  29.1 us (39%)
  blocking collectives  17.6 us (23%)
  starting transfers between devices  15.1 us (20%)
  Pallas kernels  11.5 us (15%)
  between operations  0.78 us (1%)
    ppermute x6, waiting for transfers between devices, passed_along(): lax.ppermute(value, 'blk', [(i, (i + 1) % count) for i in range(count)])  29.1 us
    all_gather x3, blocking collectives, both(): lax.all_gather(value, 'lane', axis=0, axis_index_groups=groups, tiled=False)  17.6 us
    ppermute x6, starting transfers between devices, passed_along(): lax.ppermute(value, 'blk', [(i, (i + 1) % count) for i in range(count)])  15.1 us
    pallas_call x3, Pallas kernels, gradient(): pl.pallas_call(functools.partial(gradient_kernel, s, spans), out_shape=[p...  3.21 us
    pallas_call x5, Pallas kernels, visit(): pl.pallas_call(functools.partial(visit_kernel, s, *spans[i], scale), out_...  3 us
    pallas_call x1, Pallas kernels, local(): pl.pallas_call(functools.partial(first_kernel, spans, scale), out_shape=[...  2.09 us
  transfers between devices with their start and end apart: 6, of which 6 were waited for; matrix products, arithmetic and copies ran while one was open for 1% of the time, Pallas kernels for 10%

profile of v7, /device:TPU:1, one launch (start us, length us, event | category | flops | bytes accessed | tf_op | source)
XLA Modules:
  0.0 74.7 jit_solution(14125106360070144961)
XLA Ops:
  0.6 2.1 %first_visit.1 = (bf16[256,512]{1,0:T(8,128)(2,1)S(1)}, bf16[256,512]{1,0:T(8,128)(2,1)S(1)}, bf16[512,512]{1,0:T(8,128)(2,1)S(1)}, s32[1,512]{1,0:T(1,128)S(1)}...) custom-call(bf16[1,512,512]{2,1,0:T(8,128)(2,1)} %right_hbm.1, ...), custom_call_target="tpu_custom_call" | custom-call | flops 200000000 | bytes 1000000 | tf_op jit(solution)/shard_map/first_visit/pallas_call | solution.py:182
  2.7 4.0 %collective-permute-start.1 = (bf16[256,512]{1,0:T(8,128)(2,1)S(1)}, bf16[256,512]{1,0:T(8,128)(2,1)S(1)}, u32[]{:S(2)}, u32[]{:S(2)}) collective-permute-start(bf16[256,512]{1,0:T(8,128)(2,1)S(1)} %get-tuple-element.44), channel_id=1, source_target_pairs={{0,4},{4,8},{8,12},{12,16},{16,20},{20,24},{24,28},{28,32},{32,36}... | collective-permute-start | bytes 786440 | tf_op jit(solution)/shard_map/ppermute | solution.py:31
  6.8 0.6 visit.5
  7.4 3.4 %collective-permute-start = (bf16[256,512]{1,0:T(8,128)(2,1)S(1)}, bf16[256,512]{1,0:T(8,128)(2,1)S(1)}, u32[]{:S(2)}, u32[]{:S(2)}) collective-permute-start(bf16[256,512]{1,0:T(8,128)(2,1)S(1)} %get-tuple-element.40), channel_id=1, source_target_pairs={{0,4},{4,8},{8,12},{12,16},{16,20},{20,24},{24,28},{28,32},{32,36}... | collective-permute-start | bytes 786440 | tf_op jit(solution)/shard_map/ppermute | solution.py:31
  10.8 1.1 %gradient.3 = (f32[512,512]{1,0:T(8,128)S(1)}, bf16[256,512]{1,0:T(8,128)(2,1)S(1)}, bf16[256,512]{1,0:T(8,128)(2,1)S(1)}) custom-call(bf16[1,4,512,512]{3,2,1,0:T(8,128)(2,1)} %observed_hbm.7, bf16[256,512]{1,0:T(8,128)(2,1)S(1)} %get-tuple-element.39.prior.refs_0_, bf16[256,512]{1,0:T(8,128)(2,1)S(1)} %get-tuple-element.41.refs_1_, ...), custom_call_target="tpu_custom_call" | custom-call | flops 200000000 | bytes 1000000 | tf_op jit(solution)/shard_map/gradient/pallas_call | solution.py:216
  11.9 12.0 %collective-permute-done.1.right.refs_1_ = bf16[256,512]{1,0:T(8,128)(2,1)S(1)} collective-permute-done((bf16[256,512]{1,0:T(8,128)(2,1)S(1)}, bf16[256,512]{1,0:T(8,128)(2,1)S(1)}, u32[]{:S(2)}, u32[]{:S(2)}) %collective-permute-start.1) | collective-permute-done | bytes 262176 | tf_op jit(solution)/shard_map/ppermute | solution.py:31
  23.9 0.6 visit.6
  24.5 1.9 %collective-permute-start.3 = (bf16[256,512]{1,0:T(8,128)(2,1)S(1)}, bf16[256,512]{1,0:T(8,128)(2,1)S(1)}, u32[]{:S(2)}, u32[]{:S(2)}) collective-permute-start(bf16[256,512]{1,0:T(8,128)(2,1)S(1)} %get-tuple-element.51), channel_id=1, source_target_pairs={{0,4},{4,8},{8,12},{12,16},{16,20},{20,24},{24,28},{28,32},{32,36}... | collective-permute-start | bytes 786440 | tf_op jit(solution)/shard_map/ppermute | solution.py:31
  26.4 3.1 %collective-permute-done.right.refs_3_ = bf16[256,512]{1,0:T(8,128)(2,1)S(1)} collective-permute-done((bf16[256,512]{1,0:T(8,128)(2,1)S(1)}, bf16[256,512]{1,0:T(8,128)(2,1)S(1)}, u32[]{:S(2)}, u32[]{:S(2)}) %collective-permute-start) | collective-permute-done | bytes 262176 | tf_op jit(solution)/shard_map/ppermute | solution.py:31
  29.5 0.6 visit.7
  30.1 1.9 %collective-permute-start.2 = (bf16[256,512]{1,0:T(8,128)(2,1)S(1)}, bf16[256,512]{1,0:T(8,128)(2,1)S(1)}, u32[]{:S(2)}, u32[]{:S(2)}) collective-permute-start(bf16[256,512]{1,0:T(8,128)(2,1)S(1)} %get-tuple-element.47), channel_id=1, source_target_pairs={{0,4},{4,8},{8,12},{12,16},{16,20},{20,24},{24,28},{28,32},{32,36}... | collective-permute-start | bytes 786440 | tf_op jit(solution)/shard_map/ppermute | solution.py:31
  32.1 1.1 %gradient.4 = (f32[512,512]{1,0:T(8,128)S(1)}, bf16[256,512]{1,0:T(8,128)(2,1)S(1)}, bf16[256,512]{1,0:T(8,128)(2,1)S(1)}) custom-call(bf16[1,4,512,512]{3,2,1,0:T(8,128)(2,1)} %observed_hbm.7, bf16[256,512]{1,0:T(8,128)(2,1)S(1)} %get-tuple-element.46.prior.refs_0_, ...), custom_call_target="tpu_custom_call", output_to_operand_aliasing={{0}: (5, {})} | custom-call | flops 200000000 | bytes 1000000 | tf_op jit(solution)/shard_map/gradient/pallas_call | solution.py:216
  33.1 3.3 %collective-permute-done.3.right.refs_1_ = bf16[256,512]{1,0:T(8,128)(2,1)S(1)} collective-permute-done((bf16[256,512]{1,0:T(8,128)(2,1)S(1)}, bf16[256,512]{1,0:T(8,128)(2,1)S(1)}, u32[]{:S(2)}, u32[]{:S(2)}) %collective-permute-start.3) | collective-permute-done | bytes 262176 | tf_op jit(solution)/shard_map/ppermute | solution.py:31
  36.4 0.6 visit.8
  37.0 1.9 %collective-permute-start.5 = (bf16[256,512]{1,0:T(8,128)(2,1)S(1)}, bf16[256,512]{1,0:T(8,128)(2,1)S(1)}, u32[]{:S(2)}, u32[]{:S(2)}) collective-permute-start(bf16[256,512]{1,0:T(8,128)(2,1)S(1)} %get-tuple-element.58), channel_id=1, source_target_pairs={{0,4},{4,8},{8,12},{12,16},{16,20},{20,24},{24,28},{28,32},{32,36}... | collective-permute-start | bytes 786440 | tf_op jit(solution)/shard_map/ppermute | solution.py:31
  38.9 3.9 %collective-permute-done.2.right.refs_3_ = bf16[256,512]{1,0:T(8,128)(2,1)S(1)} collective-permute-done((bf16[256,512]{1,0:T(8,128)(2,1)S(1)}, bf16[256,512]{1,0:T(8,128)(2,1)S(1)}, u32[]{:S(2)}, u32[]{:S(2)}) %collective-permute-start.2) | collective-permute-done | bytes 262176 | tf_op jit(solution)/shard_map/ppermute | solution.py:31
  42.8 0.6 visit.9
  43.4 1.9 %collective-permute-start.4 = (bf16[256,512]{1,0:T(8,128)(2,1)S(1)}, bf16[256,512]{1,0:T(8,128)(2,1)S(1)}, u32[]{:S(2)}, u32[]{:S(2)}) collective-permute-start(bf16[256,512]{1,0:T(8,128)(2,1)S(1)} %get-tuple-element.54), channel_id=1, source_target_pairs={{0,4},{4,8},{8,12},{12,16},{16,20},{20,24},{24,28},{28,32},{32,36}... | collective-permute-start | bytes 786440 | tf_op jit(solution)/shard_map/ppermute | solution.py:31
  45.4 1.1 %gradient.5 = (f32[512,512]{1,0:T(8,128)S(1)}, bf16[256,512]{1,0:T(8,128)(2,1)S(1)}, bf16[256,512]{1,0:T(8,128)(2,1)S(1)}) custom-call(bf16[1,4,512,512]{3,2,1,0:T(8,128)(2,1)} %observed_hbm.7, bf16[256,512]{1,0:T(8,128)(2,1)S(1)} %get-tuple-element.53.prior.refs_0_, ...), custom_call_target="tpu_custom_call", output_to_operand_aliasing={{0}: (5, {})} | custom-call | flops 200000000 | bytes 1000000 | tf_op jit(solution)/shard_map/gradient/pallas_call | solution.py:216
  46.5 1.9 %collective-permute-done.5.right = bf16[256,512]{1,0:T(8,128)(2,1)S(1)} collective-permute-done((bf16[256,512]{1,0:T(8,128)(2,1)S(1)}, bf16[256,512]{1,0:T(8,128)(2,1)S(1)}, u32[]{:S(2)}, u32[]{:S(2)}) %collective-permute-start.5) | collective-permute-done | bytes 262176 | tf_op jit(solution)/shard_map/ppermute | solution.py:31
  48.3 1.3 %settle.1 = (bf16[1,512,512]{2,1,0:T(8,128)(2,1)}, bf16[256,512]{1,0:T(8,128)(2,1)S(1)}) custom-call(bf16[256,512]{1,0:T(8,128)(2,1)S(1)} %collective-permute-done.5.right, bf16[512,512]{1,0:T(8,128)(2,1)S(1)} %get-tuple-element.35.left, bf16[256,512]{1,0:T(8,128)(2,1)S(1)} %get-tuple-element.59.target, ...), custom_call_target="tpu_custom_call", output_to_operand_aliasing={{1}: (2, {})} | custom-call | flops 200000000 | bytes 1000000 | tf_op jit(solution)/shard_map/settle/pallas_call | solution.py:250
  49.7 0.3 fusion
  50.0 0.2 add.3.grad_sum
  50.2 5.0 %collective-permute-done.4.right = bf16[256,512]{1,0:T(8,128)(2,1)S(1)} collective-permute-done((bf16[256,512]{1,0:T(8,128)(2,1)S(1)}, bf16[256,512]{1,0:T(8,128)(2,1)S(1)}, u32[]{:S(2)}, u32[]{:S(2)}) %collective-permute-start.4) | collective-permute-done | bytes 262176 | tf_op jit(solution)/shard_map/ppermute | solution.py:31
  55.2 0.9 %last_visit.1 = (bf16[256,512]{1,0:T(8,128)(2,1)S(1)}, bf16[256,512]{1,0:T(8,128)(2,1)S(1)}, f32[256,512]{1,0:T(8,128)S(1)}) custom-call(bf16[256,512]{1,0:T(8,128)(2,1)S(1)} %collective-permute-done.4.right, bf16[512,512]{1,0:T(8,128)(2,1)S(1)} %get-tuple-element.35.left, bf16[256,512]{1,0:T(8,128)(2,1)S(1)} %get-tuple-element.57.target, ...), custom_call_target="tpu_custom_call" | custom-call | flops 200000000 | bytes 1000000 | tf_op jit(solution)/shard_map/last_visit/pallas_call | solution.py:236
  56.1 4.9 %all-gather = bf16[512,512]{1,0:T(8,128)(2,1)S(1)} all-gather(bf16[256,512]{1,0:T(8,128)(2,1)S(1)} %get-tuple-element.63), channel_id=2, replica_groups={{0,1},{2,3},{4,5},{6,7},{8,9},{10,11},{12,13},{14,15},{16,17},{18,19},{..., dimensions={0}, use_global_device_ids=true | all-gather | bytes 786432 | tf_op jit(solution)/shard_map/all_gather | solution.py:36
  61.0 9.7 %all-gather.1 = bf16[512,512]{1,0:T(8,128)(2,1)S(1)} all-gather(bf16[256,512]{1,0:T(8,128)(2,1)S(1)} %combine.1), channel_id=3, replica_groups={{0,2},{1,3},{4,6},{5,7},{8,10},{9,11},{12,14},{13,15},{16,18},{17,19},{..., dimensions={0}, use_global_device_ids=true | all-gather | bytes 786432 | tf_op jit(solution)/shard_map/all_gather | solution.py:36
  70.7 0.1 renew.1
  70.8 3.0 %all-gather.2.left = bf16[512,512]{1,0:T(8,128)(2,1)S(1)} all-gather(bf16[256,512]{1,0:T(8,128)(2,1)S(1)} %renew.1), channel_id=4, replica_groups={{0,1},{2,3},{4,5},{6,7},{8,9},{10,11},{12,13},{14,15},{16,17},{18,19},{..., dimensions={0}, use_global_device_ids=true | all-gather | bytes 786432 | tf_op jit(solution)/shard_map/all_gather | solution.py:36
  73.8 0.9 %store.1 = (bf16[512,512]{1,0:T(8,128)(2,1)}, bf16[1,512,512]{2,1,0:T(8,128)(2,1)}) custom-call(bf16[512,512]{1,0:T(8,128)(2,1)S(1)} %all-gather.2.left, bf16[256,512]{1,0:T(8,128)(2,1)S(1)} %get-tuple-element.64.part, bf16[1,512,512]{2,1,0:T(8,128)(2,1)} %get-tuple-element.65.right_hbm), custom_call_target="tpu_custom_call", output_to_operand_aliasing={{1}: (2, {})} | custom-call | tf_op jit(solution)/shard_map/store/pallas_call | solution.py:281
  (1 shorter events, 0.0 us)
Async XLA Ops:
  2.7 21.2 %collective-permute-start.1 = (bf16[256,512]{1,0:T(8,128)(2,1)S(1)}, bf16[256,512]{1,0:T(8,128)(2,1)S(1)}, u32[]{:S(2)}, u32[]{:S(2)}) collective-permute-start(bf16[256,512]{1,0:T(8,128)(2,1)S(1)} %get-tuple-element.44), channel_id=1, source_target_pairs={{0,4},{4,8},{8,12},{12,16},{16,20},{20,24},{24,28},{28,32},{32,36}... | collective-permute-start | bytes 786440 | tf_op jit(solution)/shard_map/ppermute | solution.py:31
  7.4 22.1 %collective-permute-start = (bf16[256,512]{1,0:T(8,128)(2,1)S(1)}, bf16[256,512]{1,0:T(8,128)(2,1)S(1)}, u32[]{:S(2)}, u32[]{:S(2)}) collective-permute-start(bf16[256,512]{1,0:T(8,128)(2,1)S(1)} %get-tuple-element.40), channel_id=1, source_target_pairs={{0,4},{4,8},{8,12},{12,16},{16,20},{20,24},{24,28},{28,32},{32,36}... | collective-permute-start | bytes 786440 | tf_op jit(solution)/shard_map/ppermute | solution.py:31
  24.5 11.9 %collective-permute-start.3 = (bf16[256,512]{1,0:T(8,128)(2,1)S(1)}, bf16[256,512]{1,0:T(8,128)(2,1)S(1)}, u32[]{:S(2)}, u32[]{:S(2)}) collective-permute-start(bf16[256,512]{1,0:T(8,128)(2,1)S(1)} %get-tuple-element.51), channel_id=1, source_target_pairs={{0,4},{4,8},{8,12},{12,16},{16,20},{20,24},{24,28},{28,32},{32,36}... | collective-permute-start | bytes 786440 | tf_op jit(solution)/shard_map/ppermute | solution.py:31
  30.1 12.7 %collective-permute-start.2 = (bf16[256,512]{1,0:T(8,128)(2,1)S(1)}, bf16[256,512]{1,0:T(8,128)(2,1)S(1)}, u32[]{:S(2)}, u32[]{:S(2)}) collective-permute-start(bf16[256,512]{1,0:T(8,128)(2,1)S(1)} %get-tuple-element.47), channel_id=1, source_target_pairs={{0,4},{4,8},{8,12},{12,16},{16,20},{20,24},{24,28},{28,32},{32,36}... | collective-permute-start | bytes 786440 | tf_op jit(solution)/shard_map/ppermute | solution.py:31
  37.0 11.3 %collective-permute-start.5 = (bf16[256,512]{1,0:T(8,128)(2,1)S(1)}, bf16[256,512]{1,0:T(8,128)(2,1)S(1)}, u32[]{:S(2)}, u32[]{:S(2)}) collective-permute-start(bf16[256,512]{1,0:T(8,128)(2,1)S(1)} %get-tuple-element.58), channel_id=1, source_target_pairs={{0,4},{4,8},{8,12},{12,16},{16,20},{20,24},{24,28},{28,32},{32,36}... | collective-permute-start | bytes 786440 | tf_op jit(solution)/shard_map/ppermute | solution.py:31
  43.4 11.8 %collective-permute-start.4 = (bf16[256,512]{1,0:T(8,128)(2,1)S(1)}, bf16[256,512]{1,0:T(8,128)(2,1)S(1)}, u32[]{:S(2)}, u32[]{:S(2)}) collective-permute-start(bf16[256,512]{1,0:T(8,128)(2,1)S(1)} %get-tuple-element.54), channel_id=1, source_target_pairs={{0,4},{4,8},{8,12},{12,16},{16,20},{20,24},{24,28},{28,32},{32,36}... | collective-permute-start | bytes 786440 | tf_op jit(solution)/shard_map/ppermute | solution.py:31
